TPU v7x, 32 devices: a whole 2x2x4 slice. The times are simulated.
32 devices in a mesh: dp: 8 (over z, core), tensor: 4 (over y, x).
Axes of the slice: x: 2, y: 2, z: 4, core: 2. Of those that a mesh axis runs over, the one named last changes fastest.
Arguments:
- hidden_in: float32 [8192, 2048], P('dp'), may hold values from -16 to 16
- cotangent: bfloat16 [8192, 2048], P('dp'), may hold values from -6 to 6
- doc_lengths: int32 [8], replicated, may hold values from 1 to 7680, 8192 in all
- valid_mask: int32 [8192], P('dp'), may hold values from 0 to 1, as said below
- w_qkv: float32 [2048, 4096], P('dp', 'tensor'), may hold values from -0.125 to 0.125
- w_out: float32 [2048, 2048], P('tensor', 'dp'), may hold values from -1 to 1
- w_gate_up: float32 [2, 2048, 6144], P(None, 'dp', 'tensor'), may hold values from -0.125 to 0.125
- w_down: float32 [6144, 2048], P('tensor', 'dp'), may hold values from -0.078125 to 0.078125
- norm_gains: float32 [4352], replicated, may hold values from 0.3 to 2.8
- m_qkv: float32 [2048, 4096], P('dp', 'tensor'), may hold values from -256 to 256
- m_out: float32 [2048, 2048], P('tensor', 'dp'), may hold values from -256 to 256
- m_gate_up: float32 [2, 2048, 6144], P(None, 'dp', 'tensor'), may hold values from -256 to 256
- m_down: float32 [6144, 2048], P('tensor', 'dp'), may hold values from -256 to 256
- m_gains: float32 [4352], replicated, may hold values from -128 to 128
- a_qkv: float32 [2048, 4096], P('dp', 'tensor'), may hold values from -0.125 to 0.125
- a_out: float32 [2048, 2048], P('tensor', 'dp'), may hold values from -1 to 1
- a_gate_up: float32 [2, 2048, 6144], P(None, 'dp', 'tensor'), may hold values from -0.125 to 0.125
- a_down: float32 [6144, 2048], P('tensor', 'dp'), may hold values from -0.078125 to 0.078125
- a_gains: float32 [4352], replicated, may hold values from 0.3 to 2.8
Outputs:
- mixed_out: float32 [8192, 2048], P('dp', 'tensor')
- grad_input: float32 [8192, 2048], P('dp', 'tensor')
- branch_rms: float32 [3], replicated
- qkv_new: float32 [2048, 4096], P('dp', 'tensor')
- qkv_moment: float32 [2048, 4096], P('dp', 'tensor')
- qkv_average: float32 [2048, 4096], P('dp', 'tensor')
- qkv_average_b: bfloat16 [2048, 4096], P('dp', 'tensor')
- out_new: float32 [2048, 2048], P('tensor', 'dp')
- out_moment: float32 [2048, 2048], P('tensor', 'dp')
- out_average: float32 [2048, 2048], P('tensor', 'dp')
- out_average_b: bfloat16 [2048, 2048], P('tensor', 'dp')
- gate_up_new: float32 [2, 2048, 6144], P(None, 'dp', 'tensor')
- gate_up_moment: float32 [2, 2048, 6144], P(None, 'dp', 'tensor')
- gate_up_average: float32 [2, 2048, 6144], P(None, 'dp', 'tensor')
- gate_up_average_b: bfloat16 [2, 2048, 6144], P(None, 'dp', 'tensor')
- down_new: float32 [6144, 2048], P('tensor', 'dp')
- down_moment: float32 [6144, 2048], P('tensor', 'dp')
- down_average: float32 [6144, 2048], P('tensor', 'dp')
- down_average_b: bfloat16 [6144, 2048], P('tensor', 'dp')
- gains_new: float32 [4352], replicated
- gains_moment: float32 [4352], replicated
- gains_average: float32 [4352], replicated
- gains_average_b: bfloat16 [4352], replicated
Inputs may be any that keep to these rules, and one draw needn't show every extreme that they name: `doc_lengths`: the documents tile the stream of 8192 tokens in order; the longest has exactly 7680 tokens. `valid_mask`: the valid tokens form a prefix of the stream of at least 2048 tokens.
All inputs are finite; a program needn't handle non-finite values.
Results may differ from a plain program's by a relative error of at most 0.04.
Values may be sent and summed in bfloat16 or wider, within the bound.
A program may use at most 256 MiB of HBM per device.

v0:
```python
import functools, math
import jax, jax.numpy as jnp
from jax import lax
from jax.experimental import pallas as pl
from jax.experimental.pallas import tpu as pltpu
NT = (((1,), (1,)), ((), ()))
NN = (((1,), (0,)), ((), ()))
TN = (((0,), (0,)), ((), ()))
NEG_FILL = -1e30
LOG2E = math.log2(math.e)
MIB = 1024 * 1024

def matmul(a, b, dims):
    return lax.dot_general(a, b, dims, preferred_element_type=jnp.float32)

def row_of(column):
    return jnp.transpose(jnp.broadcast_to(column, (column.shape[0], 128)))[:1]

def attend_kernel(head_dim, key_rows, bound_ref, query_ref, begin_ref, kv_ref, out_ref, total_ref, q_two, accum):
    rows = query_ref.shape[0]
    block = pl.program_id(0)
    first = bound_ref[0, block]
    begin_first = bound_ref[1, block]
    begin_last = bound_ref[2, block]
    scale = LOG2E * head_dim**-0.5
    q_two[:rows] = query_ref[:, :head_dim]
    q_two[rows:] = query_ref[:, head_dim:]
    places = first + lax.broadcasted_iota(jnp.int32, (1, rows), 1)
    places = jnp.concatenate([places, places], axis=1)
    begins = jnp.concatenate([begin_ref[0], begin_ref[0]], axis=1)

    def step(masked, index, carry):
        top, total = carry
        key_begin = pl.multiple_of(index * key_rows, key_rows)
        keys = kv_ref[pl.ds(key_begin, key_rows), :head_dim]
        values = kv_ref[pl.ds(key_begin, key_rows), head_dim:]
        raw = matmul(keys, q_two[...], NT) * scale
        if masked:
            key_places = key_begin + lax.broadcasted_iota(jnp.int32, (key_rows, 1), 0)
            allowed = (key_places >= begins) & (key_places <= places)
            raw = jnp.where(allowed, raw, NEG_FILL)
        new_top = jnp.maximum(top, jnp.max(raw, axis=0, keepdims=True))
        probs = jnp.exp2(raw - new_top)
        fade = jnp.exp2(top - new_top)
        total = total * fade + jnp.sum(probs, axis=0, keepdims=True)
        accum[...] = accum[...] * fade + matmul(values, probs.astype(jnp.bfloat16), TN)
        return (new_top, total)

    def either(index, carry):
        key_begin = index * key_rows
        plain = (key_begin >= begin_last) & (key_begin + key_rows - 1 <= first)
        return lax.cond(
            plain, functools.partial(step, False, index), functools.partial(step, True, index), carry
        )

    accum[...] = jnp.zeros_like(accum)
    start = (
        jnp.full((1, 2 * rows), NEG_FILL, jnp.float32),
        jnp.zeros((1, 2 * rows), jnp.float32),
    )
    low = begin_first // key_rows
    high = (first + rows - 1) // key_rows + 1
    top, total = lax.fori_loop(low, high, either, start)
    out = jnp.transpose(accum[...] / total)
    out_ref[:, :head_dim] = out[:rows].astype(out_ref.dtype)
    out_ref[:, head_dim:] = out[rows:].astype(out_ref.dtype)
    total_ref[0] = top + jnp.log2(total)

def attend(bounds, queries, begins, kv_all, head_dim, query_rows, key_rows):
    rows = queries.shape[0]
    blocks = rows // query_rows
    return pl.pallas_call(
        functools.partial(attend_kernel, head_dim, key_rows),
        out_shape=(jax.ShapeDtypeStruct(queries.shape, jnp.bfloat16), jax.ShapeDtypeStruct((blocks, 1, 2 * query_rows), jnp.float32)),
        grid_spec=pltpu.PrefetchScalarGridSpec(
            num_scalar_prefetch=1,
            grid=(blocks,),
            in_specs=[
                pl.BlockSpec((query_rows, 2 * head_dim), lambda i, *_: (i, 0)),
                pl.BlockSpec((1, 1, query_rows), lambda i, *_: (i, 0, 0)),
                pl.BlockSpec(kv_all.shape, lambda i, *_: (0, 0)),
            ],
            out_specs=[
                pl.BlockSpec((query_rows, 2 * head_dim), lambda i, *_: (i, 0)),
                pl.BlockSpec((1, 1, 2 * query_rows), lambda i, *_: (i, 0, 0)),
            ],
            scratch_shapes=[pltpu.VMEM((2 * query_rows, head_dim), jnp.bfloat16), pltpu.VMEM((head_dim, 2 * query_rows), jnp.float32)],
        ),
        compiler_params=pltpu.CompilerParams(vmem_limit_bytes=48 * MIB),
    )(bounds, queries, begins, kv_all)

def attend_back_kernel(head_dim, key_rows, bound_ref, query_ref, grad_ref, out_ref, total_ref, begin_ref, kv_ref, grad_q_ref, grad_kv_ref, q_two, g_two, dq_two, kv_sum):
    rows = query_ref.shape[0]
    block = pl.program_id(0)
    first = bound_ref[0, block]
    begin_first = bound_ref[1, block]
    begin_last = bound_ref[2, block]
    unit = head_dim**-0.5
    scale = LOG2E * unit

    @pl.when(block == 0)
    def _():
        kv_sum[...] = jnp.zeros_like(kv_sum)

    for half in range(2):
        part = slice(half * rows, (half + 1) * rows)
        cols = slice(half * head_dim, (half + 1) * head_dim)
        q_two[part] = query_ref[:, cols]
        g_two[part] = grad_ref[:, cols]
    dq_two[...] = jnp.zeros_like(dq_two)
    product = grad_ref[...].astype(jnp.float32) * out_ref[...].astype(jnp.float32)
    delta = jnp.concatenate(
        [
            row_of(jnp.sum(product[:, :head_dim], axis=1, keepdims=True)),
            row_of(jnp.sum(product[:, head_dim:], axis=1, keepdims=True)),
        ],
        axis=1,
    )
    totals = total_ref[0]
    places = first + lax.broadcasted_iota(jnp.int32, (1, rows), 1)
    places = jnp.concatenate([places, places], axis=1)
    begins = jnp.concatenate([begin_ref[0], begin_ref[0]], axis=1)

    def step(masked, index):
        key_begin = pl.multiple_of(index * key_rows, key_rows)
        place = pl.ds(key_begin, key_rows)
        keys = kv_ref[place, :head_dim]
        values = kv_ref[place, head_dim:]
        raw = matmul(keys, q_two[...], NT)
        probs = jnp.exp2(raw * scale - totals)
        if masked:
            key_places = key_begin + lax.broadcasted_iota(jnp.int32, (key_rows, 1), 0)
            allowed = (key_places >= begins) & (key_places <= places)
            probs = jnp.where(allowed, probs, 0.0)
        kv_sum[place, head_dim:] += matmul(probs.astype(jnp.bfloat16), g_two[...], NN)
        grad_probs = matmul(values, g_two[...], NT)
        grad_scores = (probs * ((grad_probs - delta) * unit)).astype(jnp.bfloat16)
        kv_sum[place, :head_dim] += matmul(grad_scores, q_two[...], NN)
        dq_two[...] += matmul(grad_scores, keys, TN)

    def either(index, carry):
        key_begin = index * key_rows
        plain = (key_begin >= begin_last) & (key_begin + key_rows - 1 <= first)

        @pl.when(plain)
        def _():
            step(False, index)

        @pl.when(jnp.logical_not(plain))
        def _():
            step(True, index)

        return carry

    low = begin_first // key_rows
    high = (first + rows - 1) // key_rows + 1
    lax.fori_loop(low, high, either, 0)
    grad_q_ref[:, :head_dim] = dq_two[:rows].astype(grad_q_ref.dtype)
    grad_q_ref[:, head_dim:] = dq_two[rows:].astype(grad_q_ref.dtype)

    @pl.when(block == pl.num_programs(0) - 1)
    def _():
        grad_kv_ref[...] = kv_sum[...].astype(grad_kv_ref.dtype)

def attend_back(bounds, queries, grads, outs, totals, begin_rows, kv_all, head_dim, query_rows, key_rows):
    rows = queries.shape[0]
    blocks = rows // query_rows
    wide = pl.BlockSpec((query_rows, 2 * head_dim), lambda i, *_: (i, 0))
    whole = pl.BlockSpec(kv_all.shape, lambda i, *_: (0, 0))
    return pl.pallas_call(
        functools.partial(attend_back_kernel, head_dim, key_rows),
        out_shape=(jax.ShapeDtypeStruct(queries.shape, jnp.float32), jax.ShapeDtypeStruct(kv_all.shape, jnp.bfloat16)),
        grid_spec=pltpu.PrefetchScalarGridSpec(
            num_scalar_prefetch=1,
            grid=(blocks,),
            in_specs=[wide, wide, wide,
                pl.BlockSpec((1, 1, 2 * query_rows), lambda i, *_: (i, 0, 0)),
                pl.BlockSpec((1, 1, query_rows), lambda i, *_: (i, 0, 0)),
                whole],
            out_specs=[wide, whole],
            scratch_shapes=[pltpu.VMEM((2 * query_rows, head_dim), jnp.bfloat16)] * 2
            + [pltpu.VMEM((2 * query_rows, head_dim), jnp.float32), pltpu.VMEM(kv_all.shape, jnp.float32)],
        ),
        compiler_params=pltpu.CompilerParams(vmem_limit_bytes=56 * MIB),
    )(bounds, queries, grads, outs, totals, begin_rows, kv_all)


from jax.sharding import PartitionSpec as P

EPSILON = 1e-06
ROPE_BASE = 1000000.0
MOMENTUM = 0.5
EMA_DECAY = 0.5
LR_MATRIX = 0.08
LR_GAIN = 0.5
FF_BLOCK = 256
CHUNKS = 3


def mlp_kernel(normed_ref, cot_ref, normed_t_ref, cot_t_ref, weight_ref, hidden_ref, gate_grad_ref, up_grad_ref, weight_grad_ref):
    ways, _, shard, width = weight_ref.shape
    rows = normed_ref.shape[0]
    depth = ways * shard
    row_tile = min(512, rows)

    @pl.loop(0, rows // row_tile)
    def _(tile):
        place = pl.ds(pl.multiple_of(tile * row_tile, row_tile), row_tile)
        x = normed_ref[place, :]
        gate = matmul(x, weight_ref[:, 0].reshape(depth, width), NN)
        up = matmul(x, weight_ref[:, 1].reshape(depth, width), NN)
        grad_hidden = matmul(cot_ref[place, :], weight_ref[:, 2].reshape(depth, width), NN)
        sigmoid = 1.0 / (1.0 + jnp.exp(-gate))
        silu = gate * sigmoid
        hidden_ref[place, :] = (silu * up).astype(hidden_ref.dtype)
        gate_grad_ref[place, :] = (
            grad_hidden * up * (sigmoid * (1.0 + gate * (1.0 - sigmoid)))
        ).astype(gate_grad_ref.dtype)
        up_grad_ref[place, :] = (grad_hidden * silu).astype(up_grad_ref.dtype)

    @pl.loop(0, ways)
    def _(way):
        place = pl.ds(pl.multiple_of(way * shard, shard), shard)
        left = normed_t_ref[place, :]
        weight_grad_ref[way, 0] = matmul(left, gate_grad_ref[...], NN).astype(weight_grad_ref.dtype)
        weight_grad_ref[way, 1] = matmul(left, up_grad_ref[...], NN).astype(weight_grad_ref.dtype)
        weight_grad_ref[way, 2] = matmul(cot_t_ref[place, :], hidden_ref[...], NN).astype(weight_grad_ref.dtype)


def mlp_chunk(normed, cotangent, normed_t, cotangent_t, weights):
    ways, kinds, shard, width = weights.shape
    rows, depth = normed.shape
    block = min(FF_BLOCK, width)

    def held(array):
        return pl.BlockSpec(array.shape, lambda i: (0, 0), pipeline_mode=pl.Buffered(1))

    weight_spec = pl.BlockSpec((ways, kinds, shard, block), lambda i: (0, 0, 0, i))
    row_spec = pl.BlockSpec((rows, block), lambda i: (0, i))
    row_shape = jax.ShapeDtypeStruct((rows, width), jnp.bfloat16)
    return pl.pallas_call(
        mlp_kernel,
        grid=(width // block,),
        in_specs=[held(normed), held(cotangent), held(normed_t), held(cotangent_t), weight_spec],
        out_specs=[row_spec, row_spec, row_spec, weight_spec],
        out_shape=(row_shape, row_shape, row_shape, jax.ShapeDtypeStruct(weights.shape, jnp.bfloat16)),
        compiler_params=pltpu.CompilerParams(vmem_limit_bytes=56 * MIB),
        cost_estimate=pl.CostEstimate(flops=12 * rows * depth * width, bytes_accessed=12 * depth * width, transcendentals=rows * width),
    )(normed, cotangent, normed_t, cotangent_t, weights)


def back_product_kernel(kinds, *refs):
    out_ref = refs[-1]
    total = None
    chunks = (len(refs) - 1) // (kinds + 1)
    for chunk in range(chunks):
        weight_ref = refs[chunk * (kinds + 1) + kinds]
        for kind in range(kinds):
            part = matmul(refs[chunk * (kinds + 1) + kind][...], weight_ref[0, kind], NT)
            total = part if total is None else total + part
    out_ref[...] = total.astype(out_ref.dtype)


def back_product(groups_of, weights, kind_begin):
    kinds = len(groups_of[0])
    ways, _, shard, width = weights[0].shape
    rows = groups_of[0][0].shape[0]
    args, specs = [], []
    for lefts, weight in zip(groups_of, weights):
        for left in lefts:
            args.append(left)
            specs.append(pl.BlockSpec(left.shape, lambda i: (0, 0), pipeline_mode=pl.Buffered(1)))
        args.append(weight)
        specs.append(pl.BlockSpec((1, kinds, shard, width), lambda i: (i, kind_begin // kinds, 0, 0)))
    return pl.pallas_call(
        functools.partial(back_product_kernel, kinds),
        grid=(ways,),
        in_specs=specs,
        out_specs=pl.BlockSpec((rows, shard), lambda i: (0, i)),
        out_shape=jax.ShapeDtypeStruct((rows, ways * shard), jnp.bfloat16),
        compiler_params=pltpu.CompilerParams(vmem_limit_bytes=56 * MIB),
        cost_estimate=pl.CostEstimate(flops=2 * len(weights) * kinds * rows * width * ways * shard, bytes_accessed=2 * len(weights) * kinds * width * ways * shard, transcendentals=0),
    )(*args)


def rms_scale(values_in):
    return lax.rsqrt(jnp.mean(values_in * values_in, axis=-1, keepdims=True) + EPSILON)


def rotate_half(values_in, cosine, sine):
    half_dim = values_in.shape[-1] // 2
    turned = jnp.concatenate([-values_in[..., half_dim:], values_in[..., :half_dim]], axis=-1)
    return values_in * cosine + turned * sine


def rotate_back(grads, cosine, sine):
    half_dim = grads.shape[-1] // 2
    scaled = grads * sine
    turned = jnp.concatenate([scaled[..., half_dim:], -scaled[..., :half_dim]], axis=-1)
    return grads * cosine + turned


def norm_back(grads, normal, scale_rows, gain):
    grad_hat = grads * gain
    return scale_rows * (grad_hat - normal * jnp.mean(grad_hat * normal, axis=-1, keepdims=True))


def rope_tables(offsets, head_dim):
    half_dim = head_dim // 2
    frequency = 1.0 / ROPE_BASE ** (jnp.arange(half_dim, dtype=jnp.float32) * 2.0 / head_dim)
    angles = offsets.astype(jnp.float32)[:, None] * frequency[None, :]
    cosine = jnp.cos(angles)
    sine = jnp.sin(angles)
    return (jnp.concatenate([cosine, cosine], axis=-1), jnp.concatenate([sine, sine], axis=-1))


def nesterov(weight, moment, average, gradient, rate):
    new_moment = MOMENTUM * moment + gradient
    new_weight = weight - rate * (gradient + MOMENTUM * new_moment)
    new_average = EMA_DECAY * average + (1.0 - EMA_DECAY) * new_weight
    return (new_weight, new_moment, new_average, new_average.astype(jnp.bfloat16))


def dot(a, b, dims):
    return lax.dot_general(a, b, dims, preferred_element_type=jnp.float32)


def after(value, *others):
    return lax.optimization_barrier((value, *others))[0]


def local(
    hidden_in,
    cotangent,
    doc_lengths,
    valid_mask,
    w_qkv,
    w_out,
    w_gate_up,
    w_down,
    norm_gains,
    m_qkv,
    m_out,
    m_gate_up,
    m_down,
    m_gains,
    a_qkv,
    a_out,
    a_gate_up,
    a_down,
    a_gains,
):
    row_count, model_dim = hidden_in.shape
    head_dim = (norm_gains.shape[0] - 2 * model_dim) // 2
    data_ways = lax.axis_size("dp")
    tensor_ways = lax.axis_size("tensor")
    tensor_at = lax.axis_index("tensor")
    tokens_all = row_count * data_ways
    width_cols = model_dim // tensor_ways
    col_begin = tensor_at * width_cols
    groups = w_qkv.shape[1] // (4 * head_dim)
    ff_local = w_down.shape[0]
    ff_chunk = ff_local // CHUNKS
    bf16 = jnp.bfloat16
    f32 = jnp.float32

    def columns_of(values_in):
        return lax.dynamic_slice_in_dim(values_in, col_begin, width_cols, values_in.ndim - 1)

    qkv_full = lax.all_gather(w_qkv.astype(bf16), "dp", axis=0, tiled=True)
    out_shard_t = after(w_out.astype(bf16).T, qkv_full)
    out_full_t = lax.all_gather(out_shard_t, "dp", axis=0, tiled=True)

    ends_at = jnp.cumsum(doc_lengths)
    starts_at = ends_at - doc_lengths
    place_begin = lax.axis_index("dp") * row_count
    places = place_begin + jnp.arange(row_count, dtype=jnp.int32)
    doc_ids = jnp.sum((places[:, None] >= ends_at[None, :]).astype(jnp.int32), axis=1)
    owned = doc_ids[:, None] == jnp.arange(doc_lengths.shape[0], dtype=jnp.int32)[None, :]
    doc_begin = jnp.sum(jnp.where(owned, starts_at[None, :], 0), axis=1)
    cosine, sine = rope_tables(places - doc_begin, head_dim)
    query_rows = min(512, row_count)
    blocks = row_count // query_rows
    bounds = jnp.stack(
        [
            place_begin + jnp.arange(blocks, dtype=jnp.int32) * query_rows,
            doc_begin[::query_rows],
            doc_begin[query_rows - 1 :: query_rows],
        ]
    ).astype(jnp.int32)
    begin_rows = doc_begin.astype(jnp.int32).reshape(blocks, 1, query_rows)

    gain_attn = norm_gains[:model_dim]
    gain_mlp = norm_gains[model_dim : 2 * model_dim]
    gain_query = norm_gains[2 * model_dim : 2 * model_dim + head_dim]
    gain_key = norm_gains[2 * model_dim + head_dim :]
    scale_one = rms_scale(hidden_in)
    normal_one = hidden_in * scale_one
    normed_one_b = (normal_one * gain_attn).astype(bf16)
    projected = dot(normed_one_b, qkv_full, NN)

    raw_queries, raw_keys, queries, kv_every = [], [], [], []
    for group in range(groups):
        base = group * 4 * head_dim
        query_raw = projected[:, base : base + 2 * head_dim].reshape(row_count, 2, head_dim)
        key_raw = projected[:, base + 2 * head_dim : base + 3 * head_dim]
        value = projected[:, base + 3 * head_dim : base + 4 * head_dim]
        query = rotate_half(
            query_raw * rms_scale(query_raw) * gain_query, cosine[:, None], sine[:, None]
        )
        key = rotate_half(key_raw * rms_scale(key_raw) * gain_key, cosine, sine)
        raw_queries.append(query_raw)
        raw_keys.append(key_raw)
        queries.append(query.reshape(row_count, 2 * head_dim).astype(bf16))
        kv_local = jnp.concatenate([key, value], axis=1).astype(bf16)
        kv_every.append(lax.all_gather(kv_local, "dp", axis=0, tiled=True))

    down_t = w_down.T
    chunk_weights = []
    previous = kv_every[-1]
    for chunk in range(CHUNKS):
        units = slice(chunk * ff_chunk, (chunk + 1) * ff_chunk)
        shard = jnp.stack(
            [w_gate_up[0, :, units], w_gate_up[1, :, units], down_t[:, units]]
        ).astype(bf16)
        previous = lax.all_gather(after(shard, previous), "dp", axis=0)
        chunk_weights.append(previous)

    mixed, totals = [], []
    for group in range(groups):
        mixed_rows, total_rows = attend(
            bounds, queries[group], begin_rows, kv_every[group], head_dim, query_rows, min(1024, tokens_all)
        )
        mixed.append(mixed_rows)
        totals.append(total_rows)
    mixed_b = jnp.concatenate(mixed, axis=1)
    attn_part = dot(mixed_b, out_full_t, NT).astype(bf16)
    attn = lax.psum(attn_part, "tensor").astype(f32)
    resid_one = hidden_in + attn
    scale_two = rms_scale(resid_one)
    normal_two = resid_one * scale_two
    normed_two_b = (normal_two * gain_mlp).astype(bf16)

    normed_two_t = normed_two_b.T
    cotangent_t = cotangent.T
    weight_grads, hiddens, back_pairs = [], [], []
    for chunk in range(CHUNKS):
        hidden_b, gate_grad, up_grad, weight_grad = mlp_chunk(
            normed_two_b, cotangent, normed_two_t, cotangent_t, chunk_weights[chunk]
        )
        hiddens.append((hidden_b,))
        back_pairs.append((gate_grad, up_grad))
        weight_grads.append(lax.psum_scatter(weight_grad, "dp", scatter_dimension=0))

    part_two = back_product(back_pairs, chunk_weights, 0)
    grad_normed_two = lax.psum(part_two, "tensor").astype(f32)
    mlp_part = back_product(hiddens, chunk_weights, 2)
    mlp_cols = lax.psum_scatter(mlp_part, "tensor", scatter_dimension=1, tiled=True).astype(f32)
    gain_mlp_part = jnp.sum(columns_of(grad_normed_two * normal_two), axis=0)
    grad_resid = cotangent.astype(f32) + norm_back(grad_normed_two, normal_two, scale_two, gain_mlp)
    grad_attn_b = grad_resid.astype(bf16)
    grad_mixed_b = dot(grad_attn_b, out_full_t, NN).astype(bf16)

    grad_queries, kv_grads = [], []
    for group in range(groups):
        cols = slice(group * 2 * head_dim, (group + 1) * 2 * head_dim)
        grad_query, kv_grad = attend_back(
            bounds,
            queries[group],
            grad_mixed_b[:, cols],
            mixed[group],
            totals[group],
            begin_rows,
            kv_every[group],
            head_dim,
            query_rows,
            min(512, tokens_all),
        )
        grad_queries.append(grad_query)
        kv_grads.append(lax.psum_scatter(kv_grad, "dp", scatter_dimension=0, tiled=True).astype(f32))
    grad_out_t = dot(grad_attn_b, mixed_b, TN).astype(bf16)
    out_shard = lax.psum_scatter(grad_out_t, "dp", scatter_dimension=0, tiled=True).astype(f32).T

    grad_parts = []
    gain_query_part = jnp.zeros((head_dim,), f32)
    gain_key_part = jnp.zeros((head_dim,), f32)
    for group in range(groups):
        query_raw = raw_queries[group]
        key_raw = raw_keys[group]
        query_scale = rms_scale(query_raw)
        query_normal = query_raw * query_scale
        key_scale = rms_scale(key_raw)
        key_normal = key_raw * key_scale
        grad_query_norm = rotate_back(
            grad_queries[group].reshape(row_count, 2, head_dim), cosine[:, None], sine[:, None]
        )
        gain_query_part += jnp.sum(grad_query_norm * query_normal, axis=(0, 1))
        grad_query_raw = norm_back(grad_query_norm, query_normal, query_scale, gain_query)
        grad_key_norm = rotate_back(kv_grads[group][:, :head_dim], cosine, sine)
        gain_key_part += jnp.sum(grad_key_norm * key_normal, axis=0)
        grad_key_raw = norm_back(grad_key_norm, key_normal, key_scale, gain_key)
        grad_parts += [
            grad_query_raw.reshape(row_count, 2 * head_dim),
            grad_key_raw,
            kv_grads[group][:, head_dim:],
        ]
    grad_projected_b = jnp.concatenate([part.astype(bf16) for part in grad_parts], axis=1)
    grad_qkv = dot(normed_one_b, grad_projected_b, TN).astype(bf16)
    qkv_shard = lax.psum_scatter(grad_qkv, "dp", scatter_dimension=0, tiled=True).astype(f32)
    part_one = dot(grad_projected_b, qkv_full, NT)
    grad_one_cols = lax.psum_scatter(
        part_one.astype(bf16), "tensor", scatter_dimension=1, tiled=True
    ).astype(f32)
    row_dots = lax.psum(
        jnp.sum(part_one * (normal_one * gain_attn), axis=1, keepdims=True), "tensor"
    )
    gain_attn_part = jnp.sum(part_one * normal_one, axis=0)

    grad_cols = columns_of(grad_resid) + scale_one * (
        grad_one_cols * columns_of(gain_attn)
        - columns_of(normal_one) * (row_dots / model_dim)
    )
    attn_cols = columns_of(attn)
    mixed_cols = columns_of(resid_one) + mlp_cols
    mask_rows = valid_mask.astype(f32)[:, None]

    def column_squares(columns):
        return jnp.sum(mask_rows * columns * columns)

    count_part = jnp.where(tensor_at == 0, jnp.sum(valid_mask.astype(f32)), 0.0)
    stats_part = jnp.stack(
        [
            column_squares(columns_of(hidden_in)),
            column_squares(attn_cols),
            column_squares(mlp_cols),
            count_part,
        ]
    )
    gain_mlp_wide = lax.dynamic_update_slice_in_dim(
        jnp.zeros((model_dim,), f32), gain_mlp_part, col_begin, 0
    )
    gains_part = jnp.concatenate(
        [gain_attn_part, gain_mlp_wide, gain_query_part, gain_key_part, stats_part]
    )
    gains_sum = lax.psum(gains_part, ("dp", "tensor"))
    grad_gains = gains_sum[: norm_gains.shape[0]]
    stats_sum = gains_sum[norm_gains.shape[0] :]
    branch_rms = jnp.sqrt(stats_sum[:3] / (stats_sum[3] * model_dim))

    rate_matrix = LR_MATRIX / math.sqrt(tokens_all)
    rate_gain = LR_GAIN / math.sqrt(tokens_all)
    gate_up_shard = jnp.concatenate([grad[:2] for grad in weight_grads], axis=2).astype(f32)
    down_shard = jnp.concatenate([grad[2] for grad in weight_grads], axis=1).astype(f32).T
    return (
        mixed_cols,
        grad_cols,
        branch_rms,
        *nesterov(w_qkv, m_qkv, a_qkv, qkv_shard, rate_matrix),
        *nesterov(w_out, m_out, a_out, out_shard, rate_matrix),
        *nesterov(w_gate_up, m_gate_up, a_gate_up, gate_up_shard, rate_matrix),
        *nesterov(w_down, m_down, a_down, down_shard, rate_matrix),
        *nesterov(norm_gains, m_gains, a_gains, grad_gains, rate_gain),
    )


def solution(mesh):
    rows = P("dp", None)
    spread = P("dp", "tensor")
    turned = P("tensor", "dp")
    stacked = P(None, "dp", "tensor")
    matrices = (spread, turned, stacked, turned, P())
    in_specs = (rows, rows, P(), P("dp"), *matrices, *matrices, *matrices)
    out_specs = (spread, spread, P(), *(spec for spec in matrices for _ in range(4)))
    return jax.shard_map(local, mesh=mesh, in_specs=in_specs, out_specs=out_specs, check_vma=False)
```

profile of v0, /device:TPU:0, one launch (start us, length us, event | category | flops | bytes accessed | tf_op | source)
XLA Modules:
  0.0 1267.6 jit_solution(6859682503192790335)
XLA Ops:
  11.9 4.1 multiply_reduce_fusion.4
  18.0 4.0 broadcast_multiply_fusion.1
  22.1 38.0 %all-gather.11.cloned.1.call-done = bf16[2048,1024]{1,0:T(8,128)(2,1)} async-done(((bf16[256,1024]{1,0:T(8,128)(2,1)}), bf16[2048,1024]{1,0:T(8,128)(2,1)}) %all-gather.11.cloned.1.call-update) | async-done | bytes 4194320 | tf_op jit(solution)/shard_map/all_gather | solution.py:370
  60.1 8.2 fusion.61
  79.7 39.4 %all-gather.15.cloned.1.call-done.kv_ref = bf16[8192,256]{1,0:T(8,128)(2,1)} async-done(((bf16[1024,256]{1,0:T(8,128)(2,1)}), bf16[8192,256]{1,0:T(8,128)(2,1)}) %all-gather.15.cloned.1.call-update) | async-done | bytes 4194320 | tf_op jit(solution)/shard_map/all_gather | solution.py:416
  121.8 63.0 %all-gather.19.cloned.1.call-done = bf16[24,256,512]{2,1,0:T(8,128)(2,1)} async-done(((bf16[3,256,512]{2,1,0:T(8,128)(2,1)}), bf16[24,256,512]{2,1,0:T(8,128)(2,1)}) %all-gather.19.cloned.1.call-update) | async-done | bytes 6291472 | tf_op jit(solution)/shard_map/all_gather | solution.py:426
  207.1 4.9 shard_map.363
  212.6 20.0 %all-gather.13.cloned.1.call-done.kv_ref = bf16[8192,256]{1,0:T(8,128)(2,1)} async-done(((bf16[1024,256]{1,0:T(8,128)(2,1)}), bf16[8192,256]{1,0:T(8,128)(2,1)}) %all-gather.13.cloned.1.call-update) | async-done | bytes 4194320 | tf_op jit(solution)/shard_map/all_gather | solution.py:416
  234.8 16.6 %shard_map.362 = (bf16[1024,256]{1,0:T(8,128)(2,1)S(1)}, f32[2,1,1024]{2,1,0:T(1,128)S(1)}) custom-call(s32[3,2]{1,0:T(4,128)S(1)} %pad_add_fusion.bound_ref, bf16[1024,256]{1,0:T(8,128)(2,1)S(1)} %get-tuple-element.208.query_ref, s32[2,1,512]{2,1,0:T(1,128)S(1)} %bitcast.167, bf16[8192,256]{1,0:T(8,128)(2,1)S(1)} %copy-done.1), custom_call_target="tpu_custom_call" | custom-call | tf_op jit(solution)/shard_map/pallas_call | solution.py:72
  252.2 12.1 all-gather.17.cloned.1.call-done
  264.3 5.9 convolution_convert_fusion
  272.2 58.0 %all-gather.21.cloned.1.call-done = bf16[24,256,512]{2,1,0:T(8,128)(2,1)} async-done(((bf16[3,256,512]{2,1,0:T(8,128)(2,1)}), bf16[24,256,512]{2,1,0:T(8,128)(2,1)}) %all-gather.21.cloned.1.call-update) | async-done | bytes 6291472 | tf_op jit(solution)/shard_map/all_gather | solution.py:426
  330.2 6.4 copy.123
  336.6 99.3 %all-reduce.3.cloned.1.call-done = bf16[1024,2048]{1,0:T(8,128)(2,1)} async-done(((bf16[1024,2048]{1,0:T(8,128)(2,1)}), bf16[1024,2048]{1,0:T(8,128)(2,1)}) %all-reduce.3.cloned.1.call-update) | async-done | bytes 4194320 | tf_op jit(solution)/shard_map/psum | solution.py:438
  435.9 5.7 multiply_reduce_fusion.3
  441.7 5.9 multiply_convert_fusion
  449.3 6.4 copy.125.normed_t_ref
  455.8 25.8 %shard_map.364 = (bf16[1024,512]{1,0:T(8,128)(2,1)}, bf16[1024,512]{1,0:T(8,128)(2,1)}, bf16[1024,512]{1,0:T(8,128)(2,1)}, bf16[8,3,256,512]{3,2,1,0:T(8,128)(2,1)}) custom-call(bf16[1024,2048]{1,0:T(8,128)(2,1)} %get-tuple-element.202.normed_ref, bf16[1024,2048]{1,0:T(8,128)(2,1)} %cot_ref.5, bf16[2048,1024]{1,0:T(8,128)(2,1)} %copy.125.normed_t_ref, ...), custom_call_target="tpu_custom_call" | custom-call | flops 12884901888 | bytes 12582912 | tf_op jit(solution)/shard_map/pallas_call | solution.py:241
  481.6 25.8 %shard_map.365 = (bf16[1024,512]{1,0:T(8,128)(2,1)}, bf16[1024,512]{1,0:T(8,128)(2,1)}, bf16[1024,512]{1,0:T(8,128)(2,1)}, bf16[8,3,256,512]{3,2,1,0:T(8,128)(2,1)}) custom-call(bf16[1024,2048]{1,0:T(8,128)(2,1)} %get-tuple-element.202.normed_ref, bf16[1024,2048]{1,0:T(8,128)(2,1)} %cot_ref.5, bf16[2048,1024]{1,0:T(8,128)(2,1)} %copy.125.normed_t_ref, ...), custom_call_target="tpu_custom_call" | custom-call | flops 12884901888 | bytes 12582912 | tf_op jit(solution)/shard_map/pallas_call | solution.py:241
  507.3 25.6 %shard_map.366 = (bf16[1024,512]{1,0:T(8,128)(2,1)}, bf16[1024,512]{1,0:T(8,128)(2,1)}, bf16[1024,512]{1,0:T(8,128)(2,1)}, bf16[8,3,256,512]{3,2,1,0:T(8,128)(2,1)}) custom-call(bf16[1024,2048]{1,0:T(8,128)(2,1)} %get-tuple-element.202.normed_ref, bf16[1024,2048]{1,0:T(8,128)(2,1)} %cot_ref.5, bf16[2048,1024]{1,0:T(8,128)(2,1)} %copy.125.normed_t_ref, ...), custom_call_target="tpu_custom_call" | custom-call | flops 12884901888 | bytes 12582912 | tf_op jit(solution)/shard_map/pallas_call | solution.py:241
  532.9 19.1 %shard_map.368 = bf16[1024,2048]{1,0:T(8,128)(2,1)} custom-call(bf16[1024,512]{1,0:T(8,128)(2,1)} %get-tuple-element.56.refs_0_, bf16[1024,512]{1,0:T(8,128)(2,1)} %get-tuple-element.57.refs_1_, bf16[8,3,256,512]{3,2,1,0:T(8,128)(2,1)} %bitcast.188, bf16[1024,512]{1,0:T(8,128)(2,1)} %get-tuple-element.58.refs_3_, ...), custom_call_target="tpu_custom_call" | custom-call | flops 12884901888 | bytes 12582912 | tf_op jit(solution)/shard_map/pallas_call | solution.py:275
  552.1 104.0 %all-reduce.5.cloned.1.call-done = bf16[1024,2048]{1,0:T(8,128)(2,1)} async-done(((bf16[1024,2048]{1,0:T(8,128)(2,1)}), bf16[1024,2048]{1,0:T(8,128)(2,1)}) %all-reduce.5.cloned.1.call-update) | async-done | bytes 4194320 | tf_op jit(solution)/shard_map/psum | solution.py:456
  656.0 5.9 multiply_reduce_fusion.2
  663.1 5.6 multiply_add_fusion
  673.1 13.0 %shard_map.369 = (f32[1024,256]{1,0:T(8,128)}, bf16[8192,256]{1,0:T(8,128)(2,1)}) custom-call(s32[3,2]{1,0:T(4,128)} %copy-done.7, bf16[1024,256]{1,0:T(8,128)(2,1)} %copy-done.3, bf16[1024,256]{1,0:T(8,128)(2,1)} %get-tuple-element.224.grad_ref, bf16[1024,256]{1,0:T(8,128)(2,1)} %copy-done.5, f32[2,1,1024]{2,1,0:T(1,128)} %copy-done.9, ...), custom_call_target="tpu_custom_call" | custom-call | tf_op jit(solution)/shard_map/pallas_call | solution.py:170
  686.1 13.5 %shard_map.370 = (f32[1024,256]{1,0:T(8,128)}, bf16[8192,256]{1,0:T(8,128)(2,1)}) custom-call(s32[3,2]{1,0:T(4,128)} %copy-done.7, bf16[1024,256]{1,0:T(8,128)(2,1)} %copy-done.2, bf16[1024,256]{1,0:T(8,128)(2,1)} %get-tuple-element.225.grad_ref, bf16[1024,256]{1,0:T(8,128)(2,1)} %copy-done.4, f32[2,1,1024]{2,1,0:T(1,128)} %copy-done.8, ...), custom_call_target="tpu_custom_call" | custom-call | tf_op jit(solution)/shard_map/pallas_call | solution.py:170
  701.0 12.3 shard_map.367
  713.4 7.1 convolution_convert_fusion.2
  729.8 19.2 %multiply_reduce_fusion.7 = (f32[1024,2]{1,0:T(8,128)S(1)}, f32[1024,2]{1,0:T(8,128)S(1)}, f32[1024,2,128]{2,1,0:T(2,128)S(1)}, f32[1024,2,128]{2,1,0:T(2,128)}) fusion(f32[1024,2,128]{2,1,0:T(2,128)S(1)} %reshape.241, f32[1024,2,128]{2,1,0:T(2,128)S(1)} %copy-done.22, f32[1024,2]{1,0:T(8,128)S(1)} %copy-done.38, f32[128]{0:T(128)S(1)} %get-tuple-element.253, ...), kind=kLoop, calls=%fused_computation.75 | loop fusion | flops 3665920 | bytes 8946176 | tf_op jit(solution)/shard_map/reduce_sum | solution.py:305
  753.8 30.3 %reduce-scatter.12.cloned.1.call-done = bf16[1024,256]{1,0:T(8,128)(2,1)} async-done(((bf16[8192,256]{1,0:T(8,128)(2,1)}), bf16[1024,256]{1,0:T(8,128)(2,1)}) %reduce-scatter.12.cloned.1.call-update) | async-done | bytes 524304 | tf_op jit(solution)/shard_map/reduce_scatter | solution.py:480
  784.1 61.9 %reduce-scatter.14.cloned.1.call-done = bf16[1024,256]{1,0:T(8,128)(2,1)} async-done(((bf16[8192,256]{1,0:T(8,128)(2,1)}), bf16[1024,256]{1,0:T(8,128)(2,1)}) %reduce-scatter.14.cloned.1.call-update) | async-done | bytes 524304 | tf_op jit(solution)/shard_map/reduce_scatter | solution.py:480
  856.4 7.9 convolution_convert_fusion.1
  864.6 12.4 multiply_reduce_fusion
  890.6 6.5 convert_element_type.117
  897.1 19.0 %reduce-scatter.22.cloned.1.call-done = bf16[1,3,256,512]{3,2,1,0:T(8,128)(2,1)} async-done(((bf16[8,3,256,512]{3,2,1,0:T(8,128)(2,1)}), bf16[1,3,256,512]{3,2,1,0:T(8,128)(2,1)}) %reduce-scatter.22.cloned.1.call-update) | async-done | bytes 786448 | tf_op jit(solution)/shard_map/reduce_scatter | solution.py:453
  919.7 66.9 %reduce-scatter.24.cloned.1.call-done = bf16[1,3,256,512]{3,2,1,0:T(8,128)(2,1)} async-done(((bf16[8,3,256,512]{3,2,1,0:T(8,128)(2,1)}), bf16[1,3,256,512]{3,2,1,0:T(8,128)(2,1)}) %reduce-scatter.24.cloned.1.call-update) | async-done | bytes 786448 | tf_op jit(solution)/shard_map/reduce_scatter | solution.py:453
  990.2 3.7 multiply_reduce_fusion.5
  997.8 42.7 %reduce-scatter.10.cloned.1.call-done = bf16[1024,512]{1,0:T(8,128)(2,1)} async-done(((bf16[1024,2048]{1,0:T(8,128)(2,1)}), bf16[1024,512]{1,0:T(8,128)(2,1)}) %reduce-scatter.10.cloned.1.call-update) | async-done | bytes 1048592 | tf_op jit(solution)/shard_map/reduce_scatter | solution.py:458
  1040.5 5.6 fusion.4
  1046.1 33.0 %reduce-scatter.20.cloned.1.call-done = bf16[256,512]{1,0:T(8,128)(2,1)} async-done(((bf16[2048,512]{1,0:T(8,128)(2,1)}), bf16[256,512]{1,0:T(8,128)(2,1)}) %reduce-scatter.20.cloned.1.call-update) | async-done | bytes 262160 | tf_op jit(solution)/shard_map/reduce_scatter | solution.py:482
  1088.9 61.0 %reduce-scatter.26.cloned.1.call-done = bf16[1,3,256,512]{3,2,1,0:T(8,128)(2,1)} async-done(((bf16[8,3,256,512]{3,2,1,0:T(8,128)(2,1)}), bf16[1,3,256,512]{3,2,1,0:T(8,128)(2,1)}) %reduce-scatter.26.cloned.1.call-update) | async-done | bytes 786448 | tf_op jit(solution)/shard_map/reduce_scatter | solution.py:453
  1150.8 4.5 fusion.41
  1167.9 39.5 %psum.31 = f32[4356]{0:T(1024)S(1)} all-reduce(f32[4356]{0:T(1024)S(1)} %concatenate.73), channel_id=1, replica_groups=mesh['dp'=8,'tensor'=4] {'dp','tensor'}, use_global_device_ids=true, to_apply=%region_34.35 | all-reduce | flops 4356 | bytes 34848 | tf_op jit(solution)/shard_map/psum | solution.py:545
  1208.7 10.0 psum.30
  1220.9 7.0 fusion.43
  1228.0 4.3 fusion.47
  1232.3 23.5 %reduce-scatter.16.cloned.1.call-done = bf16[1024,512]{1,0:T(8,128)(2,1)} async-done(((bf16[1024,2048]{1,0:T(8,128)(2,1)}), bf16[1024,512]{1,0:T(8,128)(2,1)}) %reduce-scatter.16.cloned.1.call-update) | async-done | bytes 1048592 | tf_op jit(solution)/shard_map/reduce_scatter | solution.py:511
  1255.8 4.4 multiply_add_fusion.1
  (295 shorter events, 131.4 us)
Async XLA Ops:
  7.2 52.9 %all-gather.11.cloned.1.call-start = ((), (), s32[]{:S(2)}) async-start(), calls=%async_computation.9 | async-start | bytes 4718592 | tf_op jit(solution)/shard_map/all_gather | solution.py:370
  9.4 109.7 %all-gather.15.cloned.1.call-start = ((), (), s32[]{:S(2)}) async-start(), calls=%async_computation.11 | async-start | bytes 4718592 | tf_op jit(solution)/shard_map/all_gather | solution.py:416
  11.1 221.5 %copy-start.6 = (s32[1024]{0:T(1024)}, s32[1024]{0:T(1024)S(1)}, u32[]{:S(2)}) copy-start(s32[1024]{0:T(1024)S(1)} %select_reduce_fusion) | copy-start | bytes 12292
  11.9 56.8 %copy-start.65 = (f32[128]{0:T(128)}, f32[128]{0:T(128)S(1)}, u32[]{:S(2)}) copy-start(f32[128]{0:T(128)S(1)} %get-tuple-element.252) | copy-start | bytes 1540
  11.9 6.1 copy-start.10
  16.1 6.0 copy-start.60
  16.1 44.0 %copy-start.67 = (f32[2048]{0:T(1024)}, f32[2048]{0:T(1024)S(1)}, u32[]{:S(2)}) copy-start(f32[2048]{0:T(1024)S(1)} %get-tuple-element.254) | copy-start | bytes 24580
  18.0 52.7 %copy-start.45 = (f32[1024,64]{1,0:T(8,128)}, f32[1024,64]{1,0:T(8,128)S(1)}, u32[]{:S(2)}) copy-start(f32[1024,64]{1,0:T(8,128)S(1)} %get-tuple-element.256) | copy-start | bytes 786436
  18.0 52.7 %copy-start.47 = (f32[1024,64]{1,0:T(8,128)}, f32[1024,64]{1,0:T(8,128)S(1)}, u32[]{:S(2)}) copy-start(f32[1024,64]{1,0:T(8,128)S(1)} %get-tuple-element.257) | copy-start | bytes 786436
  72.1 126.7 %copy-start.48 = (f32[1024,128]{1,0:T(8,128)}, f32[1024,128]{1,0:T(8,128)S(1)}, u32[]{:S(2)}) copy-start(f32[1024,128]{1,0:T(8,128)S(1)} %get-tuple-element.245) | copy-start | bytes 1572868
  73.1 111.7 %all-gather.19.cloned.1.call-start = ((), (), s32[]{:S(2)}) async-start(), calls=%async_computation.24 | async-start | bytes 7077888 | tf_op jit(solution)/shard_map/all_gather | solution.py:426
  77.8 42.2 %copy-start.50 = (f32[512,256]{1,0:T(8,128)S(1)}, f32[512,256]{1,0:T(8,128)}, u32[]{:S(2)}) copy-start(f32[512,256]{1,0:T(8,128)} %param.24) | copy-start | bytes 1572868
  119.1 113.6 %all-gather.13.cloned.1.call-start = ((), (), s32[]{:S(2)}) async-start(), calls=%async_computation.10 | async-start | bytes 4718592 | tf_op jit(solution)/shard_map/all_gather | solution.py:416
  120.0 144.3 %all-gather.17.cloned.1.call-start = ((), (), s32[]{:S(2)}) async-start(), calls=%async_computation.12 | async-start | bytes 2359296 | tf_op jit(solution)/shard_map/all_gather | solution.py:372
  120.8 209.3 %all-gather.21.cloned.1.call-start = ((), (), s32[]{:S(2)}) async-start(), calls=%async_computation.25 | async-start | bytes 7077888 | tf_op jit(solution)/shard_map/all_gather | solution.py:426
  184.8 251.2 %all-reduce.3.cloned.1.call-start = ((), (), s32[]{:S(2)}) async-start(), calls=%async_computation.13 | async-start | bytes 8388608 | tf_op jit(solution)/shard_map/psum | solution.py:438
  185.3 47.3 %copy-start.7 = (s32[3,2]{1,0:T(4,128)}, s32[3,2]{1,0:T(4,128)S(1)}, u32[]{:S(2)}) copy-start(s32[3,2]{1,0:T(4,128)S(1)} %pad_add_fusion.bound_ref) | copy-start | bytes 76
  193.1 9.8 copy-start.37
  193.2 8.4 copy-start.39
  205.0 46.4 %copy-start.2 = (bf16[1024,256]{1,0:T(8,128)(2,1)}, bf16[1024,256]{1,0:T(8,128)(2,1)S(1)}, u32[]{:S(2)}) copy-start(bf16[1024,256]{1,0:T(8,128)(2,1)S(1)} %get-tuple-element.207.query_ref) | copy-start | bytes 1572868
  205.0 46.4 %copy-start.3 = (bf16[1024,256]{1,0:T(8,128)(2,1)}, bf16[1024,256]{1,0:T(8,128)(2,1)S(1)}, u32[]{:S(2)}) copy-start(bf16[1024,256]{1,0:T(8,128)(2,1)S(1)} %get-tuple-element.208.query_ref) | copy-start | bytes 1572868
  212.6 39.5 %copy-start.4 = (bf16[1024,256]{1,0:T(8,128)(2,1)}, bf16[1024,256]{1,0:T(8,128)(2,1)S(1)}, u32[]{:S(2)}) copy-start(bf16[1024,256]{1,0:T(8,128)(2,1)S(1)} %get-tuple-element.48.out_ref) | copy-start | bytes 1572868
  252.1 18.1 %copy-start.5 = (bf16[1024,256]{1,0:T(8,128)(2,1)}, bf16[1024,256]{1,0:T(8,128)(2,1)S(1)}, u32[]{:S(2)}) copy-start(bf16[1024,256]{1,0:T(8,128)(2,1)S(1)} %get-tuple-element.47.out_ref) | copy-start | bytes 1572868
  270.2 237.1 %all-gather.23.cloned.1.call-start = ((), (), s32[]{:S(2)}) async-start(), calls=%async_computation.26 | async-start | bytes 7077888 | tf_op jit(solution)/shard_map/all_gather | solution.py:426
  330.2 325.9 %all-reduce.5.cloned.1.call-start = ((), (), s32[]{:S(2)}) async-start(), calls=%async_computation.15 | async-start | bytes 8388608 | tf_op jit(solution)/shard_map/psum | solution.py:456
  441.7 7.6 copy-start.11
  552.0 232.0 %reduce-scatter.12.cloned.1.call-start = ((), (), s32[]{:S(2)}) async-start(), calls=%async_computation.16 | async-start | bytes 4718592 | tf_op jit(solution)/shard_map/reduce_scatter | solution.py:480
  656.0 7.0 copy-start.25
  686.1 159.9 %reduce-scatter.14.cloned.1.call-start = ((), (), s32[]{:S(2)}) async-start(), calls=%async_computation.17 | async-start | bytes 4718592 | tf_op jit(solution)/shard_map/reduce_scatter | solution.py:480
  699.6 216.5 %reduce-scatter.22.cloned.1.call-start = ((), (), s32[]{:S(2)}) async-start(), calls=%async_computation.21 | async-start | bytes 7077888 | tf_op jit(solution)/shard_map/reduce_scatter | solution.py:453
  700.2 286.4 %reduce-scatter.24.cloned.1.call-start = ((), (), s32[]{:S(2)}) async-start(), calls=%async_computation.22 | async-start | bytes 7077888 | tf_op jit(solution)/shard_map/reduce_scatter | solution.py:453
  701.0 339.5 %reduce-scatter.10.cloned.1.call-start = ((), (), s32[]{:S(2)}) async-start(), calls=%async_computation.14 | async-start | bytes 5242880 | tf_op jit(solution)/shard_map/reduce_scatter | solution.py:458
  713.3 365.8 %reduce-scatter.20.cloned.1.call-start = ((), (), s32[]{:S(2)}) async-start(), calls=%async_computation.20 | async-start | bytes 2359296 | tf_op jit(solution)/shard_map/reduce_scatter | solution.py:482
  720.5 429.4 %reduce-scatter.26.cloned.1.call-start = ((), (), s32[]{:S(2)}) async-start(), calls=%async_computation.23 | async-start | bytes 7077888 | tf_op jit(solution)/shard_map/reduce_scatter | solution.py:453
  721.0 506.9 %reduce-scatter.18.cloned.1.call-start = ((), (), s32[]{:S(2)}) async-start(), calls=%async_computation.19 | async-start | bytes 4718592 | tf_op jit(solution)/shard_map/reduce_scatter | solution.py:509
  753.8 94.3 %copy-start.57 = (f32[1024]{0:T(1024)S(1)}, f32[1024]{0:T(1024)}, u32[]{:S(2)}) copy-start(f32[1024]{0:T(1024)} %copy-done.56) | copy-start | bytes 12292
  753.8 94.3 %copy-start.59 = (f32[1024]{0:T(1024)S(1)}, f32[1024]{0:T(1024)}, u32[]{:S(2)}) copy-start(f32[1024]{0:T(1024)} %copy-done.58) | copy-start | bytes 12292
  753.8 94.3 %copy-start.66 = (f32[128]{0:T(128)S(1)}, f32[128]{0:T(128)}, u32[]{:S(2)}) copy-start(f32[128]{0:T(128)} %copy-done.65) | copy-start | bytes 1540
  849.1 7.3 slice-start
  864.3 391.5 %reduce-scatter.16.cloned.1.call-start = ((), (), s32[]{:S(2)}) async-start(), calls=%async_computation.18 | async-start | bytes 5242880 | tf_op jit(solution)/shard_map/reduce_scatter | solution.py:511
  879.1 6.1 copy-start.64
  1046.1 104.7 %copy-start.27 = (f32[1536,256]{0,1:T(8,128)S(1)}, f32[1536,256]{0,1:T(8,128)}, u32[]{:S(2)}) copy-start(f32[1536,256]{0,1:T(8,128)} %copy-done.26) | copy-start | bytes 4718596
  1046.1 104.7 %copy-start.41 = (f32[1536,256]{0,1:T(8,128)S(1)}, f32[1536,256]{0,1:T(8,128)}, u32[]{:S(2)}) copy-start(f32[1536,256]{0,1:T(8,128)} %copy.131) | copy-start | bytes 4718596
  1160.4 58.8 %copy-start.55 = (f32[4352]{0:T(1024)S(1)}, f32[4352]{0:T(1024)}, u32[]{:S(2)}) copy-start(f32[4352]{0:T(1024)} %param.27) | copy-start | bytes 52228
  1160.4 58.8 %copy-start.62 = (f32[4352]{0:T(1024)S(1)}, f32[4352]{0:T(1024)}, u32[]{:S(2)}) copy-start(f32[4352]{0:T(1024)} %param.37) | copy-start | bytes 52228
  1160.4 58.8 %copy-start.63 = (f32[4352]{0:T(1024)S(1)}, f32[4352]{0:T(1024)}, u32[]{:S(2)}) copy-start(f32[4352]{0:T(1024)} %param.32) | copy-start | bytes 52228
  1160.4 60.5 %copy-start.29 = (f32[2,256,1536]{2,1,0:T(8,128)S(1)}, f32[2,256,1536]{2,1,0:T(8,128)}, u32[]{:S(2)}) copy-start(f32[2,256,1536]{2,1,0:T(8,128)} %param.25) | copy-start | bytes 9437188
  1227.9 27.9 %copy-start.61 = (f32[1024]{0:T(1024)S(1)}, f32[1024]{0:T(1024)}, u32[]{:S(2)}) copy-start(f32[1024]{0:T(1024)} %copy-done.60) | copy-start | bytes 12292
  (42 other events, 121.7 us)
Sparse Core Ops, SparseCore 0:
  10.2 49.8 all-gather.10
  73.2 45.7 all-gather.14
  121.3 63.4 all-gather.18
  186.8 45.7 all-gather.12
  234.6 29.5 all-gather.16
  266.3 63.7 all-gather.20
  333.4 102.4 all-reduce.2
  438.3 64.7 all-gather.22
  552.1 103.8 all-reduce.4
  686.2 97.8 reduce-scatter.11
  786.4 59.5 reduce-scatter.13
  848.1 67.9 reduce-scatter.21
  918.4 68.1 reduce-scatter.23
  989.4 51.0 reduce-scatter.9
  1043.3 35.7 reduce-scatter.19
  1081.4 68.4 reduce-scatter.25
  1152.1 49.3 reduce-scatter.17
  1204.6 51.2 reduce-scatter.15
where the time goes:
time: 1280 us; the launch traced here: 1270 us
  waiting for transfers between devices  774 us (60%)
  Pallas kernels  157 us (12%)
  other arithmetic  137 us (11%)
  local copies, waits for them, and re-layouts  88 us (7%)
  blocking collectives  49.5 us (4%)
  matrix products  43.8 us (3%)
  between operations  17.1 us (1%)
    reduce_scatter x3, waiting for transfers between devices, local(): lax.psum_scatter(weight_grad, 'dp', scatter_dimension=0)  147 us
    all_gather x3, waiting for transfers between devices, local(): previous = lax.all_gather(after(shard, previous), 'dp', axis=0)  121 us
    psum x1, waiting for transfers between devices, local(): grad_normed_two = lax.psum(part_two, 'tensor').astype(f32)  104 us
    psum x1, waiting for transfers between devices, local(): attn = lax.psum(attn_part, 'tensor').astype(f32)  99.3 us
    reduce_scatter x2, waiting for transfers between devices, local(): lax.psum_scatter(kv_grad, 'dp', scatter_dimension=0, tiled=True).astype(f32)  92.2 us
    pallas_call x3, Pallas kernels, mlp_chunk(): pl.pallas_call(mlp_kernel, grid=(width // block,), in_specs=[held(normed)...  77.1 us
    all_gather x2, waiting for transfers between devices, local(): kv_every.append(lax.all_gather(kv_local, 'dp', axis=0, tiled=True))  59.4 us
    unnamed x161, local copies, waits for them, and re-layouts  52.8 us
  transfers between devices with their start and end apart: 18, of which 16 were waited for; matrix products, arithmetic and copies ran while one was open for 18% of the time, Pallas kernels for 8%

commit v1 on v0

--- a/solution.py
+++ b/solution.py
@@ -87,6 +87,7 @@
             scratch_shapes=[pltpu.VMEM((2 * query_rows, head_dim), jnp.bfloat16), pltpu.VMEM((head_dim, 2 * query_rows), jnp.float32)],
         ),
         compiler_params=pltpu.CompilerParams(vmem_limit_bytes=48 * MIB),
+        cost_estimate=pl.CostEstimate(flops=8 * rows * kv_all.shape[0] * head_dim, bytes_accessed=2 * kv_all.size, transcendentals=2 * rows * kv_all.shape[0]),
     )(bounds, queries, begins, kv_all)
 
 def attend_back_kernel(head_dim, key_rows, bound_ref, query_ref, grad_ref, out_ref, total_ref, begin_ref, kv_ref, grad_q_ref, grad_kv_ref, q_two, g_two, dq_two, kv_sum):
@@ -182,6 +183,7 @@
             + [pltpu.VMEM((2 * query_rows, head_dim), jnp.float32), pltpu.VMEM(kv_all.shape, jnp.float32)],
         ),
         compiler_params=pltpu.CompilerParams(vmem_limit_bytes=56 * MIB),
+        cost_estimate=pl.CostEstimate(flops=20 * rows * kv_all.shape[0] * head_dim, bytes_accessed=2 * kv_all.size, transcendentals=2 * rows * kv_all.shape[0]),
     )(bounds, queries, grads, outs, totals, begin_rows, kv_all)
 
 
@@ -258,29 +260,273 @@
         for kind in range(kinds):
             part = matmul(refs[chunk * (kinds + 1) + kind][...], weight_ref[0, kind], NT)
             total = part if total is None else total + part
-    out_ref[...] = total.astype(out_ref.dtype)
-
-
-def back_product(groups_of, weights, kind_begin):
+    out_ref[0] = total.astype(out_ref.dtype)
+
+
+def back_product(groups_of, weights, kind_begin, pieces):
     kinds = len(groups_of[0])
     ways, _, shard, width = weights[0].shape
     rows = groups_of[0][0].shape[0]
+    per_piece = ways // pieces
     args, specs = [], []
     for lefts, weight in zip(groups_of, weights):
         for left in lefts:
             args.append(left)
             specs.append(pl.BlockSpec(left.shape, lambda i: (0, 0), pipeline_mode=pl.Buffered(1)))
         args.append(weight)
-        specs.append(pl.BlockSpec((1, kinds, shard, width), lambda i: (i, kind_begin // kinds, 0, 0)))
+        specs.append(pl.BlockSpec((1, kinds, shard, weight.shape[3]), lambda i: (i, kind_begin // kinds, 0, 0)))
     return pl.pallas_call(
         functools.partial(back_product_kernel, kinds),
         grid=(ways,),
         in_specs=specs,
-        out_specs=pl.BlockSpec((rows, shard), lambda i: (0, i)),
-        out_shape=jax.ShapeDtypeStruct((rows, ways * shard), jnp.bfloat16),
+        out_specs=pl.BlockSpec((1, rows, shard), lambda i: (i // per_piece, 0, i % per_piece)),
+        out_shape=jax.ShapeDtypeStruct((pieces, rows, per_piece * shard), jnp.bfloat16),
         compiler_params=pltpu.CompilerParams(vmem_limit_bytes=56 * MIB),
         cost_estimate=pl.CostEstimate(flops=2 * len(weights) * kinds * rows * width * ways * shard, bytes_accessed=2 * len(weights) * kinds * width * ways * shard, transcendentals=0),
     )(*args)
+
+
+MESH = pl.DeviceIdType.MESH
+SUM_BLOCKS = 4
+
+
+def flip(index, bit):
+    unit = 1 << bit
+    return index + unit - 2 * unit * ((index // unit) % 2)
+
+
+def picks(index, fixed, free):
+    base = 0
+    for bit in fixed:
+        unit = 1 << bit
+        base = base + unit * ((index // unit) % 2)
+    found = []
+    for choice in range(1 << len(free)):
+        offset = sum((1 << bit) for at, bit in enumerate(free) if (choice >> at) & 1)
+        found.append(base + offset)
+    return found
+
+
+def tensor_sum_kernel(bits, whole, part_ref, out_ref, sums, landed, send_sem, recv_sem, send_out, recv_out):
+    row_at = lax.axis_index("dp")
+    me = lax.axis_index("tensor")
+    barrier = pltpu.get_barrier_semaphore()
+    for bit in range(bits):
+        pl.semaphore_signal(barrier, inc=1, device_id=(row_at, flip(me, bit)), device_id_type=MESH)
+    pl.semaphore_wait(barrier, bits)
+    tensor_sum_steps(bits, whole, part_ref, out_ref, sums, landed, send_sem, recv_sem, send_out, recv_out)
+
+
+def tensor_sum_steps(bits, whole, part_ref, out_ref, sums, landed, send_sem, recv_sem, send_out, recv_out):
+    row_at = lax.axis_index("dp")
+    me = lax.axis_index("tensor")
+    rows = part_ref.shape[1] // SUM_BLOCKS
+    orders = [list(range(bits)) if b % 2 == 0 else list(range(bits))[::-1] for b in range(SUM_BLOCKS)]
+
+    def place(block):
+        return pl.ds(block * rows, rows)
+
+    def scatter(block, step):
+        order = orders[block]
+        bit = order[step]
+        there = flip(me, bit)
+        free = order[step + 1 :]
+        source = part_ref if step == 0 else sums
+        base = (1 << bits) - (1 << (bits - step))
+        copies = []
+        for at, piece in enumerate(picks(there, order[: step + 1], free)):
+            slot = base + at
+            copies.append(
+                pltpu.make_async_remote_copy(
+                    src_ref=source.at[piece, place(block)],
+                    dst_ref=landed.at[slot, place(block)],
+                    send_sem=send_sem.at[slot, block],
+                    recv_sem=recv_sem.at[slot, block],
+                    device_id=(row_at, there),
+                    device_id_type=MESH,
+                )
+            )
+        return copies
+
+    def gather(block, step):
+        order = orders[block][::-1]
+        bit = order[step]
+        there = flip(me, bit)
+        base = (1 << step) - 1
+        copies = []
+        for at, piece in enumerate(picks(me, order[step:], order[:step])):
+            slot = base + at
+            copies.append(
+                pltpu.make_async_remote_copy(
+                    src_ref=out_ref.at[piece, place(block)],
+                    dst_ref=out_ref.at[piece, place(block)],
+                    send_sem=send_out.at[slot, block],
+                    recv_sem=recv_out.at[slot, block],
+                    device_id=(row_at, there),
+                    device_id_type=MESH,
+                )
+            )
+        return copies
+
+    every = []
+    flying = []
+    for block in range(SUM_BLOCKS):
+        copies = scatter(block, 0)
+        for copy in copies:
+            copy.start()
+        flying.append(copies)
+    for step in range(bits):
+        for block in range(SUM_BLOCKS):
+            order = orders[block]
+            base = (1 << bits) - (1 << (bits - step))
+            for copy in flying[block]:
+                copy.wait_recv()
+            every += flying[block]
+            source = part_ref if step == 0 else sums
+            last = step == bits - 1
+            for at, piece in enumerate(picks(me, order[: step + 1], order[step + 1 :])):
+                total = source[piece, place(block)].astype(jnp.float32) + landed[base + at, place(block)].astype(jnp.float32)
+                if not last:
+                    sums[piece, place(block)] = total.astype(sums.dtype)
+                elif whole:
+                    out_ref[piece, place(block)] = total.astype(out_ref.dtype)
+                else:
+                    out_ref[place(block)] = total.astype(out_ref.dtype)
+            if not last:
+                flying[block] = scatter(block, step + 1)
+            elif whole:
+                flying[block] = gather(block, 0)
+            if not last or whole:
+                for copy in flying[block]:
+                    copy.start()
+    if whole:
+        for step in range(bits):
+            for block in range(SUM_BLOCKS):
+                for copy in flying[block]:
+                    copy.wait_recv()
+                every += flying[block]
+                if step < bits - 1:
+                    flying[block] = gather(block, step + 1)
+                    for copy in flying[block]:
+                        copy.start()
+    for copy in every:
+        copy.wait_send()
+
+
+def tensor_sum(part, collective_id, whole=True):
+    ways, rows, width = part.shape
+    bits = ways.bit_length() - 1
+    return pl.pallas_call(
+        functools.partial(tensor_sum_kernel, bits, whole),
+        out_shape=jax.ShapeDtypeStruct(part.shape if whole else part.shape[1:], part.dtype),
+        in_specs=[pl.BlockSpec(memory_space=pltpu.VMEM)],
+        out_specs=pl.BlockSpec(memory_space=pltpu.VMEM),
+        scratch_shapes=[
+            pltpu.VMEM(part.shape, part.dtype),
+            pltpu.VMEM((ways - 1, rows, width), part.dtype),
+            *[pltpu.SemaphoreType.DMA((ways - 1, SUM_BLOCKS))] * 4,
+        ],
+        compiler_params=pltpu.CompilerParams(
+            collective_id=collective_id, has_side_effects=True, vmem_limit_bytes=32 * MIB
+        ),
+        cost_estimate=pl.CostEstimate(flops=0, bytes_accessed=(256 if whole else 128) * MIB, transcendentals=0),
+    )(part)
+
+
+def spread_kernel(source, slots, me, ways, place, send_sem, recv_sem):
+    copies = []
+    for step in range(1, ways):
+        there = lax.rem(me + step, ways)
+        copies.append(
+            pltpu.make_async_remote_copy(
+                src_ref=source,
+                dst_ref=slots.at[me],
+                send_sem=send_sem.at[step - 1],
+                recv_sem=recv_sem.at[step - 1],
+                device_id=place(there),
+                device_id_type=MESH,
+            )
+        )
+    for copy in copies:
+        copy.start()
+    return copies
+
+
+def total_of(slots, ways):
+    total = slots[0]
+    for at in range(1, ways):
+        total = total + slots[at]
+    return total
+
+
+def last_sum_kernel(
+    bits, ways, part_ref, dots_ref, gains_ref, out_ref, dots_out_ref, gains_out_ref,
+    sums, landed, dots_land, gains_land, gains_far, gains_mid, send_sem, recv_sem, dots_send, dots_recv,
+    near_send, near_recv, far_send, far_recv,
+):
+    row_at = lax.axis_index("dp")
+    me = lax.axis_index("tensor")
+    pieces = 1 << bits
+
+    def beside(there):
+        return (row_at, there)
+
+    def along(there):
+        return (there, me)
+
+    barrier = pltpu.get_barrier_semaphore()
+    for step in range(1, pieces):
+        pl.semaphore_signal(barrier, inc=1, device_id=beside(lax.rem(me + step, pieces)), device_id_type=MESH)
+    for step in range(1, ways):
+        pl.semaphore_signal(barrier, inc=1, device_id=along(lax.rem(row_at + step, ways)), device_id_type=MESH)
+    pl.semaphore_wait(barrier, pieces + ways - 2)
+    gains_land[me] = gains_ref[...]
+    dots_land[me] = dots_ref[...]
+    near = spread_kernel(gains_ref, gains_land, me, pieces, beside, near_send, near_recv)
+    dots = spread_kernel(dots_ref, dots_land, me, pieces, beside, dots_send, dots_recv)
+    for copy in near:
+        copy.wait()
+    gains_mid[...] = total_of(gains_land, pieces)
+    gains_far[row_at] = gains_mid[...]
+    far = spread_kernel(gains_mid, gains_far, row_at, ways, along, far_send, far_recv)
+    tensor_sum_steps(bits, False, part_ref, out_ref, sums, landed, send_sem, recv_sem, None, None)
+    for copy in dots:
+        copy.wait()
+    dots_out_ref[...] = total_of(dots_land, pieces)
+    for copy in far:
+        copy.wait()
+    gains_out_ref[...] = total_of(gains_far, ways)
+
+
+def last_sum(part, dots, gains, data_ways, collective_id):
+    pieces, rows, width = part.shape
+    bits = pieces.bit_length() - 1
+    near = pltpu.SemaphoreType.DMA((pieces - 1,))
+    far = pltpu.SemaphoreType.DMA((data_ways - 1,))
+    return pl.pallas_call(
+        functools.partial(last_sum_kernel, bits, data_ways),
+        out_shape=(
+            jax.ShapeDtypeStruct(part.shape[1:], part.dtype),
+            jax.ShapeDtypeStruct(dots.shape, dots.dtype),
+            jax.ShapeDtypeStruct(gains.shape, gains.dtype),
+        ),
+        in_specs=[pl.BlockSpec(memory_space=pltpu.VMEM)] * 3,
+        out_specs=[pl.BlockSpec(memory_space=pltpu.VMEM)] * 3,
+        scratch_shapes=[
+            pltpu.VMEM(part.shape, part.dtype),
+            pltpu.VMEM((pieces - 1, rows, width), part.dtype),
+            pltpu.VMEM((pieces, *dots.shape), dots.dtype),
+            pltpu.VMEM((pieces, *gains.shape), gains.dtype),
+            pltpu.VMEM((data_ways, *gains.shape), gains.dtype),
+            pltpu.VMEM(gains.shape, gains.dtype),
+            *[pltpu.SemaphoreType.DMA((pieces - 1, SUM_BLOCKS))] * 2,
+            near, near, near, near, far, far,
+        ],
+        compiler_params=pltpu.CompilerParams(
+            collective_id=collective_id, has_side_effects=True, vmem_limit_bytes=32 * MIB
+        ),
+        cost_estimate=pl.CostEstimate(flops=0, bytes_accessed=128 * MIB, transcendentals=0),
+    )(part, dots, gains)
 
 
 def rms_scale(values_in):
@@ -325,8 +571,8 @@
     return lax.dot_general(a, b, dims, preferred_element_type=jnp.float32)
 
 
-def after(value, *others):
-    return lax.optimization_barrier((value, *others))[0]
+def tie(*values):
+    return lax.optimization_barrier(values)
 
 
 def local(
@@ -367,9 +613,13 @@
     def columns_of(values_in):
         return lax.dynamic_slice_in_dim(values_in, col_begin, width_cols, values_in.ndim - 1)
 
+    def across(pieces):
+        return jnp.concatenate([pieces[piece] for piece in range(tensor_ways)], axis=1)
+
     qkv_full = lax.all_gather(w_qkv.astype(bf16), "dp", axis=0, tiled=True)
-    out_shard_t = after(w_out.astype(bf16).T, qkv_full)
-    out_full_t = lax.all_gather(out_shard_t, "dp", axis=0, tiled=True)
+
+    out_turned, qkv_full = tie(w_out.astype(bf16).T, qkv_full)
+    out_blocks = lax.all_gather(out_turned, "dp", axis=0)
 
     ends_at = jnp.cumsum(doc_lengths)
     starts_at = ends_at - doc_lengths
@@ -413,19 +663,25 @@
         raw_keys.append(key_raw)
         queries.append(query.reshape(row_count, 2 * head_dim).astype(bf16))
         kv_local = jnp.concatenate([key, value], axis=1).astype(bf16)
+        if group:
+            kv_local, kv_every[-1] = tie(kv_local, kv_every[-1])
+        else:
+            kv_local, out_blocks = tie(kv_local, out_blocks)
         kv_every.append(lax.all_gather(kv_local, "dp", axis=0, tiled=True))
 
     down_t = w_down.T
     chunk_weights = []
-    previous = kv_every[-1]
-    for chunk in range(CHUNKS):
+    out_full_t = out_blocks.reshape(model_dim, w_out.shape[0])
+
+    def chunk_shard(chunk):
         units = slice(chunk * ff_chunk, (chunk + 1) * ff_chunk)
-        shard = jnp.stack(
-            [w_gate_up[0, :, units], w_gate_up[1, :, units], down_t[:, units]]
-        ).astype(bf16)
-        previous = lax.all_gather(after(shard, previous), "dp", axis=0)
-        chunk_weights.append(previous)
-
+        return jnp.stack([w_gate_up[0, :, units], w_gate_up[1, :, units], down_t[:, units]]).astype(bf16)
+
+    def chunk_gather(shard):
+        return lax.all_gather(shard, "dp", axis=0)
+
+    shard, kv_every[-1] = tie(chunk_shard(0), kv_every[-1])
+    chunk_weights.append(chunk_gather(shard))
     mixed, totals = [], []
     for group in range(groups):
         mixed_rows, total_rows = attend(
@@ -434,8 +690,13 @@
         mixed.append(mixed_rows)
         totals.append(total_rows)
     mixed_b = jnp.concatenate(mixed, axis=1)
-    attn_part = dot(mixed_b, out_full_t, NT).astype(bf16)
-    attn = lax.psum(attn_part, "tensor").astype(f32)
+    shard, chunk_weights[0], mixed_b = tie(chunk_shard(1), chunk_weights[0], mixed_b)
+    chunk_weights.append(chunk_gather(shard))
+    attn_part = back_product([(mixed_b,)], [out_blocks[:, None]], 0, tensor_ways)
+    attn_sum = tensor_sum(attn_part, 0)
+    shard, chunk_weights[1], attn_sum = tie(chunk_shard(2), chunk_weights[1], attn_sum)
+    chunk_weights.append(chunk_gather(shard))
+    attn = across(attn_sum).astype(f32)
     resid_one = hidden_in + attn
     scale_two = rms_scale(resid_one)
     normal_two = resid_one * scale_two
@@ -452,10 +713,9 @@
         back_pairs.append((gate_grad, up_grad))
         weight_grads.append(lax.psum_scatter(weight_grad, "dp", scatter_dimension=0))
 
-    part_two = back_product(back_pairs, chunk_weights, 0)
-    grad_normed_two = lax.psum(part_two, "tensor").astype(f32)
-    mlp_part = back_product(hiddens, chunk_weights, 2)
-    mlp_cols = lax.psum_scatter(mlp_part, "tensor", scatter_dimension=1, tiled=True).astype(f32)
+    part_two = back_product(back_pairs, chunk_weights, 0, tensor_ways)
+    part_two, weight_grads[0] = tie(part_two, weight_grads[0])
+    grad_normed_two = across(tensor_sum(part_two, 1)).astype(f32)
     gain_mlp_part = jnp.sum(columns_of(grad_normed_two * normal_two), axis=0)
     grad_resid = cotangent.astype(f32) + norm_back(grad_normed_two, normal_two, scale_two, gain_mlp)
     grad_attn_b = grad_resid.astype(bf16)
@@ -464,10 +724,11 @@
     grad_queries, kv_grads = [], []
     for group in range(groups):
         cols = slice(group * 2 * head_dim, (group + 1) * 2 * head_dim)
+        grad_rows, weight_grads[group + 1] = tie(grad_mixed_b[:, cols], weight_grads[group + 1])
         grad_query, kv_grad = attend_back(
             bounds,
             queries[group],
-            grad_mixed_b[:, cols],
+            grad_rows,
             mixed[group],
             totals[group],
             begin_rows,
@@ -479,7 +740,13 @@
         grad_queries.append(grad_query)
         kv_grads.append(lax.psum_scatter(kv_grad, "dp", scatter_dimension=0, tiled=True).astype(f32))
     grad_out_t = dot(grad_attn_b, mixed_b, TN).astype(bf16)
+    grad_out_t, kv_grads[-1] = tie(grad_out_t, kv_grads[-1])
     out_shard = lax.psum_scatter(grad_out_t, "dp", scatter_dimension=0, tiled=True).astype(f32).T
+
+    hidden_first, grad_queries[-1] = tie(hiddens[0][0], grad_queries[-1])
+    hiddens[0] = (hidden_first,)
+    mlp_part = back_product(hiddens, chunk_weights, 2, tensor_ways)
+    mlp_cols = tensor_sum(mlp_part, 2, False).astype(f32)
 
     grad_parts = []
     gain_query_part = jnp.zeros((head_dim,), f32)
@@ -508,18 +775,12 @@
     grad_qkv = dot(normed_one_b, grad_projected_b, TN).astype(bf16)
     qkv_shard = lax.psum_scatter(grad_qkv, "dp", scatter_dimension=0, tiled=True).astype(f32)
     part_one = dot(grad_projected_b, qkv_full, NT)
-    grad_one_cols = lax.psum_scatter(
-        part_one.astype(bf16), "tensor", scatter_dimension=1, tiled=True
-    ).astype(f32)
-    row_dots = lax.psum(
-        jnp.sum(part_one * (normal_one * gain_attn), axis=1, keepdims=True), "tensor"
-    )
+    part_one_b = jnp.stack(
+        [part_one[:, at * width_cols : (at + 1) * width_cols] for at in range(tensor_ways)]
+    ).astype(bf16)
+    dots_part = jnp.sum(part_one * (normal_one * gain_attn), axis=1).reshape(row_count // 128, 128)
     gain_attn_part = jnp.sum(part_one * normal_one, axis=0)
 
-    grad_cols = columns_of(grad_resid) + scale_one * (
-        grad_one_cols * columns_of(gain_attn)
-        - columns_of(normal_one) * (row_dots / model_dim)
-    )
     attn_cols = columns_of(attn)
     mixed_cols = columns_of(resid_one) + mlp_cols
     mask_rows = valid_mask.astype(f32)[:, None]
@@ -542,7 +803,15 @@
     gains_part = jnp.concatenate(
         [gain_attn_part, gain_mlp_wide, gain_query_part, gain_key_part, stats_part]
     )
-    gains_sum = lax.psum(gains_part, ("dp", "tensor"))
+    gains_count = gains_part.shape[0]
+    gains_rows = -(-gains_count // 1024) * 8
+    gains_part = jnp.pad(gains_part, (0, gains_rows * 128 - gains_count)).reshape(gains_rows, 128)
+    grad_one_cols, row_dots, gains_sum = last_sum(part_one_b, dots_part, gains_part, data_ways, 3)
+    gains_sum = gains_sum.reshape(-1)[:gains_count]
+    grad_cols = columns_of(grad_resid) + scale_one * (
+        grad_one_cols.astype(f32) * columns_of(gain_attn)
+        - columns_of(normal_one) * (row_dots.reshape(row_count, 1) / model_dim)
+    )
     grad_gains = gains_sum[: norm_gains.shape[0]]
     stats_sum = gains_sum[norm_gains.shape[0] :]
     branch_rms = jnp.sqrt(stats_sum[:3] / (stats_sum[3] * model_dim))

time: 1280 us -> 934 us (0.73); the launches traced: 1270 us -> 941 us
  waiting for transfers between devices: 774 us -> 284 us
  Pallas kernels: 157 us -> 374 us
  blocking collectives: 49.5 us -> 0 us
    pallas_call x0 -> x4, Pallas kernels: none -> 220 us  [the longest x3 179 us: tensor_sum(): pl.pallas_call(functools.partial(tensor_sum_kernel, bits, whole), out_sha...]
    psum x2 -> x0, waiting for transfers between devices: 203 us -> none  [the longest x1 104 us: local(): grad_normed_two = lax.psum(part_two, 'tensor').astype(f32)]
    reduce_scatter x3, waiting for transfers between devices: 147 us -> 35.9 us  [local(): lax.psum_scatter(weight_grad, 'dp', scatter_dimension=0)]
    reduce_scatter x2 -> x0, waiting for transfers between devices: 66.2 us -> none  [the longest x1 42.7 us: local(): lax.psum_scatter(mlp_part, 'tensor', scatter_dimension=1, tiled=True)]
    all_gather x4, waiting for transfers between devices: 133 us -> 67.8 us  [the longest x3 49.2 us: chunk_gather(): return lax.all_gather(shard, 'dp', axis=0)]
    psum x2 -> x0, blocking collectives: 49.5 us -> none  [the longest x1 39.5 us: local(): gains_sum = lax.psum(gains_part, ('dp', 'tensor'))]
    reduce_scatter x2, waiting for transfers between devices: 92.2 us -> 52.6 us  [local(): lax.psum_scatter(kv_grad, 'dp', scatter_dimension=0, tiled=True).astype(f32)]
    reduce_scatter x1, waiting for transfers between devices: 33 us -> 0.01 us  [local(): lax.psum_scatter(grad_out_t, 'dp', scatter_dimension=0, tiled=True)]
  transfers between devices with their start and end apart: 18 -> 14, of which waited for: 16 -> 9; matrix products, arithmetic and copies ran while one was open for 18% -> 25% of each run, Pallas kernels for 8% -> 40%
where the time goes in v1:
time: 934 us; the launch traced here: 941 us
  Pallas kernels  374 us (40%)
  waiting for transfers between devices  284 us (30%)
  other arithmetic  132 us (14%)
  local copies, waits for them, and re-layouts  96.8 us (10%)
  matrix products  35.4 us (4%)
  between operations  17.1 us (2%)
    pallas_call x3, Pallas kernels, tensor_sum(): pl.pallas_call(functools.partial(tensor_sum_kernel, bits, whole), out_sha...  179 us
    all_gather x2, waiting for transfers between devices, local(): kv_every.append(lax.all_gather(kv_local, 'dp', axis=0, tiled=True))  86.1 us
    pallas_call x3, Pallas kernels, mlp_chunk(): pl.pallas_call(mlp_kernel, grid=(width // block,), in_specs=[held(normed)...  77.2 us
    unnamed x244, local copies, waits for them, and re-layouts  55.8 us
    reduce_scatter x2, waiting for transfers between devices, local(): lax.psum_scatter(kv_grad, 'dp', scatter_dimension=0, tiled=True).astype(f32)  52.6 us
    all_gather x3, waiting for transfers between devices, chunk_gather(): return lax.all_gather(shard, 'dp', axis=0)  49.2 us
    pallas_call x1, Pallas kernels, last_sum(): pl.pallas_call(functools.partial(last_sum_kernel, bits, data_ways), out_s...  41.9 us
    all_gather x1, waiting for transfers between devices, local(): qkv_full = lax.all_gather(w_qkv.astype(bf16), 'dp', axis=0, tiled=True)  41.4 us
  transfers between devices with their start and end apart: 14, of which 9 were waited for; matrix products, arithmetic and copies ran while one was open for 25% of the time, Pallas kernels for 40%

profile of v1, /device:TPU:0, one launch (start us, length us, event | category | flops | bytes accessed | tf_op | source)
XLA Modules:
  0.0 940.8 jit_solution(14649615902374571873)
XLA Ops:
  11.9 4.1 multiply_reduce_fusion.4
  18.7 41.4 %all-gather.12.cloned.1.call-done = bf16[2048,1024]{1,0:T(8,128)(2,1)} async-done(((bf16[256,1024]{1,0:T(8,128)(2,1)}), bf16[2048,1024]{1,0:T(8,128)(2,1)}) %all-gather.12.cloned.1.call-update) | async-done | bytes 4194320 | tf_op jit(solution)/shard_map/all_gather | solution.py:619
  60.2 4.1 broadcast_multiply_fusion.1
  64.7 4.5 fusion.65
  73.1 18.7 %all-gather.18.cloned.1.call-done = bf16[2048,512]{0,1:T(8,128)(2,1)} async-done(((bf16[256,512]{0,1:T(8,128)(2,1)}), bf16[2048,512]{0,1:T(8,128)(2,1)}) %all-gather.18.cloned.1.call-update) | async-done | bytes 2097168 | tf_op jit(solution)/shard_map/all_gather | solution.py:622
  91.8 3.9 copy.98
  96.6 45.5 %all-gather.14.cloned.1.call-done.kv_ref = bf16[8192,256]{1,0:T(8,128)(2,1)} async-done(((bf16[1024,256]{1,0:T(8,128)(2,1)}), bf16[8192,256]{1,0:T(8,128)(2,1)}) %all-gather.14.cloned.1.call-update) | async-done | bytes 4194320 | tf_op jit(solution)/shard_map/all_gather | solution.py:670
  149.4 40.6 %all-gather.16.cloned.1.call-done.kv_ref = bf16[8192,256]{1,0:T(8,128)(2,1)} async-done(((bf16[1024,256]{1,0:T(8,128)(2,1)}), bf16[8192,256]{1,0:T(8,128)(2,1)}) %all-gather.16.cloned.1.call-update) | async-done | bytes 4194320 | tf_op jit(solution)/shard_map/all_gather | solution.py:670
  200.2 3.3 multiply_multiply_fusion.4
  214.2 4.9 shard_map.362
  219.2 5.4 shard_map.363
  226.4 29.2 %all-gather.20.cloned.1.call-done = bf16[24,256,512]{2,1,0:T(8,128)(2,1)} async-done(((bf16[3,256,512]{2,1,0:T(8,128)(2,1)}), bf16[24,256,512]{2,1,0:T(8,128)(2,1)}) %all-gather.20.cloned.1.call-update) | async-done | bytes 6291472 | tf_op jit(solution)/shard_map/all_gather | solution.py:681
  256.6 8.2 shard_map.364.part_ref
  267.0 71.6 %shard_map.365 = bf16[4,1024,512]{2,1,0:T(8,128)(2,1)S(1)} custom-call(bf16[4,1024,512]{2,1,0:T(8,128)(2,1)S(1)} %copy-done.3), custom_call_target="tpu_custom_call" | custom-call | bytes 268435456 | tf_op jit(solution)/shard_map/pallas_call | solution.py:419
  341.0 6.4 copy.101
  349.9 5.6 multiply_reduce_fusion.3
  355.6 6.0 multiply_convert_fusion
  363.2 6.4 copy.102.normed_t_ref
  369.6 25.7 %shard_map.366 = (bf16[1024,512]{1,0:T(8,128)(2,1)}, bf16[1024,512]{1,0:T(8,128)(2,1)}, bf16[1024,512]{1,0:T(8,128)(2,1)}, bf16[8,3,256,512]{3,2,1,0:T(8,128)(2,1)}) custom-call(bf16[1024,2048]{1,0:T(8,128)(2,1)} %get-tuple-element.225.normed_ref, bf16[1024,2048]{1,0:T(8,128)(2,1)} %cot_ref.5, bf16[2048,1024]{1,0:T(8,128)(2,1)} %copy.102.normed_t_ref, ...), custom_call_target="tpu_custom_call" | custom-call | flops 12884901888 | bytes 12582912 | tf_op jit(solution)/shard_map/pallas_call | solution.py:243
  395.4 19.6 %all-gather.24.cloned.1.call-done = bf16[24,256,512]{2,1,0:T(8,128)(2,1)} async-done(((bf16[3,256,512]{2,1,0:T(8,128)(2,1)}), bf16[24,256,512]{2,1,0:T(8,128)(2,1)}) %all-gather.24.cloned.1.call-update) | async-done | bytes 6291472 | tf_op jit(solution)/shard_map/all_gather | solution.py:681
  415.0 25.5 %shard_map.368 = (bf16[1024,512]{1,0:T(8,128)(2,1)}, bf16[1024,512]{1,0:T(8,128)(2,1)}, bf16[1024,512]{1,0:T(8,128)(2,1)}, bf16[8,3,256,512]{3,2,1,0:T(8,128)(2,1)}) custom-call(bf16[1024,2048]{1,0:T(8,128)(2,1)} %get-tuple-element.225.normed_ref, bf16[1024,2048]{1,0:T(8,128)(2,1)} %cot_ref.5, bf16[2048,1024]{1,0:T(8,128)(2,1)} %copy.102.normed_t_ref, ...), custom_call_target="tpu_custom_call" | custom-call | flops 12884901888 | bytes 12582912 | tf_op jit(solution)/shard_map/pallas_call | solution.py:243
  440.6 26.0 %shard_map.367 = (bf16[1024,512]{1,0:T(8,128)(2,1)}, bf16[1024,512]{1,0:T(8,128)(2,1)}, bf16[1024,512]{1,0:T(8,128)(2,1)}, bf16[8,3,256,512]{3,2,1,0:T(8,128)(2,1)}) custom-call(bf16[1024,2048]{1,0:T(8,128)(2,1)} %get-tuple-element.225.normed_ref, bf16[1024,2048]{1,0:T(8,128)(2,1)} %cot_ref.5, bf16[2048,1024]{1,0:T(8,128)(2,1)} %copy.102.normed_t_ref, ...), custom_call_target="tpu_custom_call" | custom-call | flops 12884901888 | bytes 12582912 | tf_op jit(solution)/shard_map/pallas_call | solution.py:243
  466.6 19.3 %shard_map.369.part_ref = bf16[4,1024,512]{2,1,0:T(8,128)(2,1)} custom-call(bf16[1024,512]{1,0:T(8,128)(2,1)} %get-tuple-element.85.refs_0_, bf16[1024,512]{1,0:T(8,128)(2,1)} %get-tuple-element.86.refs_1_, bf16[8,3,256,512]{3,2,1,0:T(8,128)(2,1)} %bitcast.230, bf16[1024,512]{1,0:T(8,128)(2,1)} %get-tuple-element.88.refs_3_, ...), custom_call_target="tpu_custom_call" | custom-call | flops 12884901888 | bytes 12582912 | tf_op jit(solution)/shard_map/pallas_call | solution.py:278
  488.2 71.6 %shard_map.370 = bf16[4,1024,512]{2,1,0:T(8,128)(2,1)S(1)} custom-call(bf16[4,1024,512]{2,1,0:T(8,128)(2,1)S(1)} %copy-done.2), custom_call_target="tpu_custom_call" | custom-call | bytes 268435456 | tf_op jit(solution)/shard_map/pallas_call | solution.py:419
  560.1 3.4 slice-done.1
  565.7 5.2 multiply_add_fusion
  570.9 5.8 fusion.12
  577.8 13.0 %shard_map.371 = (f32[1024,256]{1,0:T(8,128)}, bf16[8192,256]{1,0:T(8,128)(2,1)}) custom-call(s32[3,2]{1,0:T(4,128)} %copy-done.9, bf16[1024,256]{1,0:T(8,128)(2,1)} %copy-done.5, bf16[1024,256]{1,0:T(8,128)(2,1)} %get-tuple-element.96.grad_ref, bf16[1024,256]{1,0:T(8,128)(2,1)} %copy-done.7, f32[2,1,1024]{2,1,0:T(1,128)} %copy-done.13, ...), custom_call_target="tpu_custom_call" | custom-call | flops 21474836480 | bytes 4194304 | tf_op jit(solution)/shard_map/pallas_call | solution.py:171
  590.8 35.9 %reduce-scatter.12.cloned.1.call-done = bf16[1,3,256,512]{3,2,1,0:T(8,128)(2,1)} async-done(((bf16[8,3,256,512]{3,2,1,0:T(8,128)(2,1)}), bf16[1,3,256,512]{3,2,1,0:T(8,128)(2,1)}) %reduce-scatter.12.cloned.1.call-update) | async-done | bytes 786448 | tf_op jit(solution)/shard_map/reduce_scatter | solution.py:714
  626.7 13.3 %shard_map.374 = (f32[1024,256]{1,0:T(8,128)}, bf16[8192,256]{1,0:T(8,128)(2,1)}) custom-call(s32[3,2]{1,0:T(4,128)} %copy-done.9, bf16[1024,256]{1,0:T(8,128)(2,1)} %copy-done.4, bf16[1024,256]{1,0:T(8,128)(2,1)} %get-tuple-element.103.grad_ref, bf16[1024,256]{1,0:T(8,128)(2,1)} %copy-done.6, f32[2,1,1024]{2,1,0:T(1,128)} %copy-done.12, ...), custom_call_target="tpu_custom_call" | custom-call | flops 21474836480 | bytes 4194304 | tf_op jit(solution)/shard_map/pallas_call | solution.py:171
  644.1 3.0 copy.110
  647.1 3.1 copy.108
  652.0 7.8 convolution_convert_fusion.1
  666.9 19.8 %multiply_reduce_fusion.7 = (f32[1024,2]{1,0:T(8,128)}, f32[1024,2]{1,0:T(8,128)S(1)}, f32[1024,2,128]{2,1,0:T(2,128)S(1)}, f32[1024,2,128]{2,1,0:T(2,128)}) fusion(f32[1024,2,128]{2,1,0:T(2,128)S(1)} %copy-done.47, f32[1024,2,128]{2,1,0:T(2,128)S(1)} %copy-done.27, f32[1024,2]{1,0:T(8,128)S(1)} %copy-done.55, f32[128]{0:T(128)S(1)} %copy-done.106, ...), kind=kLoop, calls=%fused_computation.81 | loop fusion | flops 3665920 | bytes 8946176 | tf_op jit(solution)/shard_map/reduce_sum | solution.py:551
  694.9 52.6 %reduce-scatter.14.cloned.1.call-done = bf16[1024,256]{1,0:T(8,128)(2,1)} async-done(((bf16[8192,256]{1,0:T(8,128)(2,1)}), bf16[1024,256]{1,0:T(8,128)(2,1)}) %reduce-scatter.14.cloned.1.call-update) | async-done | bytes 524304 | tf_op jit(solution)/shard_map/reduce_scatter | solution.py:741
  758.0 7.8 convolution_convert_fusion
  765.9 5.5 maximum_convert_fusion
  778.4 12.3 %shard_map.372.part_ref = bf16[4,1024,512]{2,1,0:T(8,128)(2,1)} custom-call(bf16[1024,512]{1,0:T(8,128)(2,1)} %get-tuple-element.99.refs_0_, bf16[8,3,256,512]{3,2,1,0:T(8,128)(2,1)} %bitcast.231, bf16[1024,512]{1,0:T(8,128)(2,1)} %get-tuple-element.100.refs_2_, bf16[8,3,256,512]{3,2,1,0:T(8,128)(2,1)} %bitcast.234, ...), custom_call_target="tpu_custom_call" | custom-call | flops 6442450944 | bytes 6291456 | tf_op jit(solution)/shard_map/pallas_call | solution.py:278
  793.1 35.4 %shard_map.373 = bf16[1024,512]{1,0:T(8,128)(2,1)S(1)} custom-call(bf16[4,1024,512]{2,1,0:T(8,128)(2,1)S(1)} %copy-done), custom_call_target="tpu_custom_call" | custom-call | bytes 134217728 | tf_op jit(solution)/shard_map/pallas_call | solution.py:419
  835.4 3.0 copy.116
  838.4 3.0 copy.117
  843.7 3.9 multiply_reduce_fusion.5
  847.7 5.6 fusion.4
  853.4 5.5 fusion.47
  859.2 9.4 %multiply_reduce_fusion = (f32[2048]{0:T(1024)S(1)}, f32[1024]{0:T(1024)S(1)}, bf16[1024,2048]{1,0:T(8,128)(2,1)}) fusion(f32[1024,2048]{1,0:T(8,128)S(1)} %bitcast.224, f32[2048]{0:T(1024)S(1)} %copy-done.102, bf16[1024,1024]{1,0:T(8,128)(2,1)S(1)} %copy-done.87, bf16[2048,1024]{1,0:T(8,128)(2,1)} %all-gather.12.cloned.1.call-done), kind=kOutput, calls=%fused_computation | convolution fusion | flops 4307547136 | bytes 18894848 | tf_op jit(solution)/shard_map/dot_general | solution.py:571
  873.8 41.9 %shard_map.375 = (bf16[1024,512]{1,0:T(8,128)(2,1)S(1)}, f32[8,128]{1,0:T(8,128)S(1)}, f32[40,128]{1,0:T(8,128)S(1)}) custom-call(bf16[4,1024,512]{2,1,0:T(8,128)(2,1)S(1)} %pad_maximum_fusion.part_ref, f32[8,128]{1,0:T(8,128)S(1)} %bitcast.207, f32[40,128]{1,0:T(8,128)S(1)} %pad_bitcast_fusion.gains_ref), custom_call_target="tpu_custom_call" | custom-call | bytes 134217728 | tf_op jit(solution)/shard_map/pallas_call | solution.py:506
  918.1 4.1 multiply_add_fusion.1
  930.5 3.6 fusion.51
  (377 shorter events, 122.1 us)
Async XLA Ops:
  7.2 52.9 %all-gather.12.cloned.1.call-start = ((), (), s32[]{:S(2)}) async-start(), calls=%async_computation.7 | async-start | bytes 4718592 | tf_op jit(solution)/shard_map/all_gather | solution.py:619
  9.4 82.4 %all-gather.18.cloned.1.call-start = ((), (), s32[]{:S(2)}) async-start(), calls=%async_computation.17 | async-start | bytes 2359296 | tf_op jit(solution)/shard_map/all_gather | solution.py:622
  11.1 208.1 %copy-start.8 = (s32[1024]{0:T(1024)}, s32[1024]{0:T(1024)S(1)}, u32[]{:S(2)}) copy-start(s32[1024]{0:T(1024)S(1)} %select_reduce_fusion) | copy-start | bytes 12292
  11.9 58.9 %copy-start.99 = (f32[128]{0:T(128)}, f32[128]{0:T(128)S(1)}, u32[]{:S(2)}) copy-start(f32[128]{0:T(128)S(1)} %get-tuple-element.288) | copy-start | bytes 1540
  11.9 188.3 %copy-start.105 = (f32[128]{0:T(128)}, f32[128]{0:T(128)S(1)}, u32[]{:S(2)}) copy-start(f32[128]{0:T(128)S(1)} %get-tuple-element.287) | copy-start | bytes 1540
  16.0 48.4 %copy-start.94 = (f32[1024]{0:T(1024)}, f32[1024]{0:T(1024)S(1)}, u32[]{:S(2)}) copy-start(f32[1024]{0:T(1024)S(1)} %add_rsqrt_fusion.5) | copy-start | bytes 12292
  16.0 48.3 %copy-start.101 = (f32[2048]{0:T(1024)}, f32[2048]{0:T(1024)S(1)}, u32[]{:S(2)}) copy-start(f32[2048]{0:T(1024)S(1)} %get-tuple-element.289) | copy-start | bytes 24580
  18.7 52.9 %copy-start.61 = (f32[1024,64]{1,0:T(8,128)}, f32[1024,64]{1,0:T(8,128)S(1)}, u32[]{:S(2)}) copy-start(f32[1024,64]{1,0:T(8,128)S(1)} %get-tuple-element.291) | copy-start | bytes 786436
  18.7 52.9 %copy-start.63 = (f32[1024,64]{1,0:T(8,128)}, f32[1024,64]{1,0:T(8,128)S(1)}, u32[]{:S(2)}) copy-start(f32[1024,64]{1,0:T(8,128)S(1)} %get-tuple-element.292) | copy-start | bytes 786436
  60.1 82.0 %all-gather.14.cloned.1.call-start = ((), (), s32[]{:S(2)}) async-start(), calls=%async_computation.8 | async-start | bytes 4718592 | tf_op jit(solution)/shard_map/all_gather | solution.py:670
  72.2 133.7 %copy-start.64 = (f32[1024,128]{1,0:T(8,128)}, f32[1024,128]{1,0:T(8,128)S(1)}, u32[]{:S(2)}) copy-start(f32[1024,128]{1,0:T(8,128)S(1)} %get-tuple-element.282) | copy-start | bytes 1572868
  72.2 136.1 %copy-start.59 = (f32[1024,128]{1,0:T(8,128)}, f32[1024,128]{1,0:T(8,128)S(1)}, u32[]{:S(2)}) copy-start(f32[1024,128]{1,0:T(8,128)S(1)} %get-tuple-element.281) | copy-start | bytes 1572868
  72.2 23.6 %copy-start.81 = (bf16[1024,128]{1,0:T(8,128)(2,1)S(1)}, bf16[1024,128]{1,0:T(8,128)(2,1)}, u32[]{:S(2)}) copy-start(bf16[1024,128]{1,0:T(8,128)(2,1)} %get-tuple-element.250) | copy-start | bytes 786436
  95.7 94.3 %all-gather.16.cloned.1.call-start = ((), (), s32[]{:S(2)}) async-start(), calls=%async_computation.9 | async-start | bytes 4718592 | tf_op jit(solution)/shard_map/all_gather | solution.py:670
  142.1 113.5 %all-gather.20.cloned.1.call-start = ((), (), s32[]{:S(2)}) async-start(), calls=%async_computation.18 | async-start | bytes 7077888 | tf_op jit(solution)/shard_map/all_gather | solution.py:681
  190.0 150.9 %all-gather.22.cloned.1.call-start = ((), (), s32[]{:S(2)}) async-start(), calls=%async_computation.19 | async-start | bytes 7077888 | tf_op jit(solution)/shard_map/all_gather | solution.py:681
  190.4 28.7 %copy-start.9 = (s32[3,2]{1,0:T(4,128)}, s32[3,2]{1,0:T(4,128)S(1)}, u32[]{:S(2)}) copy-start(s32[3,2]{1,0:T(4,128)S(1)} %pad_add_fusion.bound_ref) | copy-start | bytes 76
  192.4 18.8 %copy-start.103 = (f32[256]{0:T(256)}, f32[256]{0:T(256)S(1)}, u32[]{:S(2)}) copy-start(f32[256]{0:T(256)S(1)} %broadcast_bitcast_fusion) | copy-start | bytes 3076
  200.2 9.7 %copy-start.54 = (f32[1024,2]{1,0:T(8,128)}, f32[1024,2]{1,0:T(8,128)S(1)}, u32[]{:S(2)}) copy-start(f32[1024,2]{1,0:T(8,128)S(1)} %add_rsqrt_fusion) | copy-start | bytes 24580
  219.2 36.5 %copy-start.78 = (bf16[2,256,512]{2,1,0:T(8,128)(2,1)S(1)}, bf16[2,256,512]{2,1,0:T(8,128)(2,1)}, u32[]{:S(2)}) copy-start(bf16[2,256,512]{2,1,0:T(8,128)(2,1)} %get-tuple-element.253) | copy-start | bytes 1572868
  225.2 39.6 %copy-start.7 = (bf16[1024,256]{1,0:T(8,128)(2,1)}, bf16[1024,256]{1,0:T(8,128)(2,1)S(1)}, u32[]{:S(2)}) copy-start(bf16[1024,256]{1,0:T(8,128)(2,1)S(1)} %get-tuple-element.78.out_ref) | copy-start | bytes 1572868
  255.6 159.4 %all-gather.24.cloned.1.call-start = ((), (), s32[]{:S(2)}) async-start(), calls=%async_computation.20 | async-start | bytes 7077888 | tf_op jit(solution)/shard_map/all_gather | solution.py:681
  341.0 145.0 %reduce-scatter.8.cloned.1.call-start = ((), (), s32[]{:S(2)}) async-start(), calls=%async_computation.10 | async-start | bytes 7077888 | tf_op jit(solution)/shard_map/reduce_scatter | solution.py:714
  395.4 182.4 %reduce-scatter.10.cloned.1.call-start = ((), (), s32[]{:S(2)}) async-start(), calls=%async_computation.11 | async-start | bytes 7077888 | tf_op jit(solution)/shard_map/reduce_scatter | solution.py:714
  440.5 186.1 %reduce-scatter.12.cloned.1.call-start = ((), (), s32[]{:S(2)}) async-start(), calls=%async_computation.12 | async-start | bytes 7077888 | tf_op jit(solution)/shard_map/reduce_scatter | solution.py:714
  466.6 224.1 %reduce-scatter.16.cloned.1.call-start = ((), (), s32[]{:S(2)}) async-start(), calls=%async_computation.14 | async-start | bytes 4718592 | tf_op jit(solution)/shard_map/reduce_scatter | solution.py:741
  488.2 72.0 %slice-start = ((s8[8388608]{0:T(1024)(128)(4,1)}), s8[4194304]{0:T(1024)(128)(4,1)S(1)}, s32[]{:S(2)}) async-start(s8[8388608]{0:T(1024)(128)(4,1)} %bitcast.208), calls=%async_computation.21 | async-start | bytes 8388608
  590.7 156.7 %reduce-scatter.14.cloned.1.call-start = ((), (), s32[]{:S(2)}) async-start(), calls=%async_computation.13 | async-start | bytes 4718592 | tf_op jit(solution)/shard_map/reduce_scatter | solution.py:741
  640.0 282.1 %reduce-scatter.20.cloned.1.call-start = ((), (), s32[]{:S(2)}) async-start(), calls=%async_computation.16 | async-start | bytes 2359296 | tf_op jit(solution)/shard_map/reduce_scatter | solution.py:744
  666.9 21.1 %copy-start.19 = (f32[1024,2,128]{2,1,0:T(2,128)S(1)}, f32[1024,2,128]{2,1,0:T(2,128)}, u32[]{:S(2)}) copy-start(f32[1024,2,128]{2,1,0:T(2,128)} %copy-done.18) | copy-start | bytes 3145732
  666.9 21.1 %copy-start.21 = (f32[1024,2,128]{2,1,0:T(2,128)S(1)}, f32[1024,2,128]{2,1,0:T(2,128)}, u32[]{:S(2)}) copy-start(f32[1024,2,128]{2,1,0:T(2,128)} %copy-done.20) | copy-start | bytes 3145732
  666.9 21.1 %copy-start.44 = (f32[1024,256]{1,0:T(8,128)S(1)}, f32[1024,256]{1,0:T(8,128)}, u32[]{:S(2)}) copy-start(f32[1024,256]{1,0:T(8,128)} %get-tuple-element.105) | copy-start | bytes 3145732
  666.9 21.1 %copy-start.104 = (f32[256]{0:T(256)S(1)}, f32[256]{0:T(256)}, u32[]{:S(2)}) copy-start(f32[256]{0:T(256)} %copy-done.103) | copy-start | bytes 3076
  692.8 56.9 %copy-start.91 = (f32[1024]{0:T(1024)S(1)}, f32[1024]{0:T(1024)}, u32[]{:S(2)}) copy-start(f32[1024]{0:T(1024)} %copy-done.90) | copy-start | bytes 12292
  692.8 56.9 %copy-start.93 = (f32[1024]{0:T(1024)S(1)}, f32[1024]{0:T(1024)}, u32[]{:S(2)}) copy-start(f32[1024]{0:T(1024)} %copy-done.92) | copy-start | bytes 12292
  692.8 56.9 %copy-start.100 = (f32[128]{0:T(128)S(1)}, f32[128]{0:T(128)}, u32[]{:S(2)}) copy-start(f32[128]{0:T(128)} %copy-done.99) | copy-start | bytes 1540
  692.8 237.7 %reduce-scatter.18.cloned.1.call-start = ((), (), s32[]{:S(2)}) async-start(), calls=%async_computation.15 | async-start | bytes 4718592 | tf_op jit(solution)/shard_map/reduce_scatter | solution.py:776
  778.3 50.2 %copy-start.83 = (bf16[1,3,256,512]{3,2,1,0:T(8,128)(2,1)S(1)}, bf16[1,3,256,512]{3,2,1,0:T(8,128)(2,1)}, u32[]{:S(2)}) copy-start(bf16[1,3,256,512]{3,2,1,0:T(8,128)(2,1)} %reduce-scatter.10.cloned.1.call-done) | copy-start | bytes 2359300
  793.1 36.2 %copy-start.36 = (f32[1536,256]{0,1:T(8,128)S(1)}, f32[1536,256]{0,1:T(8,128)}, u32[]{:S(2)}) copy-start(f32[1536,256]{0,1:T(8,128)} %copy-done.35) | copy-start | bytes 4718596
  793.1 36.2 %copy-start.56 = (f32[1536,256]{0,1:T(8,128)S(1)}, f32[1536,256]{0,1:T(8,128)}, u32[]{:S(2)}) copy-start(f32[1536,256]{0,1:T(8,128)} %copy.110) | copy-start | bytes 4718596
  793.1 36.2 %copy-start.57 = (f32[1536,256]{0,1:T(8,128)S(1)}, f32[1536,256]{0,1:T(8,128)}, u32[]{:S(2)}) copy-start(f32[1536,256]{0,1:T(8,128)} %copy.108) | copy-start | bytes 4718596
  843.7 9.6 %copy-start.66 = (f32[2,256,1536]{2,1,0:T(8,128)S(1)}, f32[2,256,1536]{2,1,0:T(8,128)}, u32[]{:S(2)}) copy-start(f32[2,256,1536]{2,1,0:T(8,128)} %param.35) | copy-start | bytes 9437188
  843.7 9.6 %copy-start.67 = (f32[2,256,1536]{2,1,0:T(8,128)S(1)}, f32[2,256,1536]{2,1,0:T(8,128)}, u32[]{:S(2)}) copy-start(f32[2,256,1536]{2,1,0:T(8,128)} %param.30) | copy-start | bytes 9437188
  847.7 11.2 %slice-start.4 = ((s8[8388608]{0:T(1024)(128)(4,1)}), s8[4194304]{0:T(1024)(128)(4,1)S(1)}, s32[]{:S(2)}) async-start(s8[8388608]{0:T(1024)(128)(4,1)} %bitcast.223), calls=%async_computation.25 | async-start | bytes 8388608
  873.7 43.7 %copy-start.89 = (f32[4352]{0:T(1024)S(1)}, f32[4352]{0:T(1024)}, u32[]{:S(2)}) copy-start(f32[4352]{0:T(1024)} %param.27) | copy-start | bytes 52228
  873.7 43.7 %copy-start.96 = (f32[4352]{0:T(1024)S(1)}, f32[4352]{0:T(1024)}, u32[]{:S(2)}) copy-start(f32[4352]{0:T(1024)} %param.37) | copy-start | bytes 52228
  873.7 43.7 %copy-start.97 = (f32[4352]{0:T(1024)S(1)}, f32[4352]{0:T(1024)}, u32[]{:S(2)}) copy-start(f32[4352]{0:T(1024)} %param.32) | copy-start | bytes 52228
  873.7 44.3 %copy-start.95 = (f32[1024]{0:T(1024)S(1)}, f32[1024]{0:T(1024)}, u32[]{:S(2)}) copy-start(f32[1024]{0:T(1024)} %copy-done.94) | copy-start | bytes 12292
  (80 other events, 365.3 us)
Sparse Core Ops, SparseCore 0:
  10.2 49.8 all-gather.11
  62.3 29.4 all-gather.17
  95.8 46.2 all-gather.13
  144.1 45.8 all-gather.15
  192.1 63.4 all-gather.19
  257.6 83.2 all-gather.21
  343.1 71.8 all-gather.23
  417.3 68.4 reduce-scatter.7
  488.1 68.1 reduce-scatter.9
  558.5 68.1 reduce-scatter.11
  629.0 56.6 reduce-scatter.15
  687.8 59.6 reduce-scatter.13
  749.7 36.2 reduce-scatter.19
  788.1 48.4 reduce-scatter.17

commit v2 on v1

--- a/solution.py
+++ b/solution.py
@@ -199,19 +199,21 @@
 CHUNKS = 3
 
 
-def mlp_kernel(normed_ref, cot_ref, normed_t_ref, cot_t_ref, weight_ref, hidden_ref, gate_grad_ref, up_grad_ref, weight_grad_ref):
-    ways, _, shard, width = weight_ref.shape
+def mlp_kernel(normed_ref, cot_ref, normed_t_ref, cot_t_ref, weight_ref, hidden_ref, gate_grad_ref, up_grad_ref, grads_ref, wide):
+    ways, kinds, shard, _ = weight_ref.shape
     rows = normed_ref.shape[0]
-    depth = ways * shard
     row_tile = min(512, rows)
+
+    for at in range(ways):
+        wide[:, at * shard : (at + 1) * shard, :] = weight_ref[at]
 
     @pl.loop(0, rows // row_tile)
     def _(tile):
         place = pl.ds(pl.multiple_of(tile * row_tile, row_tile), row_tile)
         x = normed_ref[place, :]
-        gate = matmul(x, weight_ref[:, 0].reshape(depth, width), NN)
-        up = matmul(x, weight_ref[:, 1].reshape(depth, width), NN)
-        grad_hidden = matmul(cot_ref[place, :], weight_ref[:, 2].reshape(depth, width), NN)
+        gate = matmul(x, wide[0], NN)
+        up = matmul(x, wide[1], NN)
+        grad_hidden = matmul(cot_ref[place, :], wide[2], NN)
         sigmoid = 1.0 / (1.0 + jnp.exp(-gate))
         silu = gate * sigmoid
         hidden_ref[place, :] = (silu * up).astype(hidden_ref.dtype)
@@ -220,24 +222,23 @@
         ).astype(gate_grad_ref.dtype)
         up_grad_ref[place, :] = (grad_hidden * silu).astype(up_grad_ref.dtype)
 
-    @pl.loop(0, ways)
-    def _(way):
-        place = pl.ds(pl.multiple_of(way * shard, shard), shard)
+    for at in range(ways):
+        place = slice(at * shard, (at + 1) * shard)
         left = normed_t_ref[place, :]
-        weight_grad_ref[way, 0] = matmul(left, gate_grad_ref[...], NN).astype(weight_grad_ref.dtype)
-        weight_grad_ref[way, 1] = matmul(left, up_grad_ref[...], NN).astype(weight_grad_ref.dtype)
-        weight_grad_ref[way, 2] = matmul(cot_t_ref[place, :], hidden_ref[...], NN).astype(weight_grad_ref.dtype)
+        grads_ref[at, 0] = matmul(left, gate_grad_ref[...], NN).astype(grads_ref.dtype)
+        grads_ref[at, 1] = matmul(left, up_grad_ref[...], NN).astype(grads_ref.dtype)
+        grads_ref[at, 2] = matmul(cot_t_ref[place, :], hidden_ref[...], NN).astype(grads_ref.dtype)
 
 
 def mlp_chunk(normed, cotangent, normed_t, cotangent_t, weights):
-    ways, kinds, shard, width = weights.shape
+    ways, _, shard, width = weights.shape
     rows, depth = normed.shape
     block = min(FF_BLOCK, width)
 
     def held(array):
         return pl.BlockSpec(array.shape, lambda i: (0, 0), pipeline_mode=pl.Buffered(1))
 
-    weight_spec = pl.BlockSpec((ways, kinds, shard, block), lambda i: (0, 0, 0, i))
+    weight_spec = pl.BlockSpec((ways, 3, shard, block), lambda i: (0, 0, 0, i))
     row_spec = pl.BlockSpec((rows, block), lambda i: (0, i))
     row_shape = jax.ShapeDtypeStruct((rows, width), jnp.bfloat16)
     return pl.pallas_call(
@@ -245,9 +246,10 @@
         grid=(width // block,),
         in_specs=[held(normed), held(cotangent), held(normed_t), held(cotangent_t), weight_spec],
         out_specs=[row_spec, row_spec, row_spec, weight_spec],
-        out_shape=(row_shape, row_shape, row_shape, jax.ShapeDtypeStruct(weights.shape, jnp.bfloat16)),
+        out_shape=(row_shape, row_shape, row_shape, jax.ShapeDtypeStruct((ways, 3, shard, width), jnp.bfloat16)),
+        scratch_shapes=[pltpu.VMEM((3, depth, block), jnp.bfloat16)],
         compiler_params=pltpu.CompilerParams(vmem_limit_bytes=56 * MIB),
-        cost_estimate=pl.CostEstimate(flops=12 * rows * depth * width, bytes_accessed=12 * depth * width, transcendentals=rows * width),
+        cost_estimate=pl.CostEstimate(flops=24 * rows * depth * width, bytes_accessed=12 * depth * width, transcendentals=rows * width),
     )(normed, cotangent, normed_t, cotangent_t, weights)
 
 
@@ -529,26 +531,297 @@
     )(part, dots, gains)
 
 
+def turned_by(values, signs):
+    return pltpu.roll(values, values.shape[1] // 2, 1) * signs
+
+
+def half_signs(head_dim, first):
+    lanes = lax.broadcasted_iota(jnp.int32, (1, head_dim), 1)
+    return jnp.where(lanes < head_dim // 2, first, -first)
+
+
+def front_kernel(groups, head_dim, normed_ref, weight_ref, cos_ref, sin_ref, gains_ref, raw_ref, *outs):
+    raw_ref[...] = matmul(normed_ref[...], weight_ref[...], NN)
+    cosine = cos_ref[...]
+    sine = sin_ref[...] * half_signs(head_dim, -1.0)
+    for group in range(groups):
+        for at in range(4):
+            base = (group * 4 + at) * head_dim
+            raw = raw_ref[:, base : base + head_dim]
+            if at < 3:
+                gain = gains_ref[at // 2 : at // 2 + 1]
+                scale = lax.rsqrt(jnp.mean(raw * raw, axis=1, keepdims=True) + EPSILON)
+                raw = raw * scale * gain
+                raw = raw * cosine + turned_by(raw, sine)
+            out = outs[group] if at < 2 else outs[groups + group]
+            out[:, at % 2 * head_dim : (at % 2 + 1) * head_dim] = raw.astype(out.dtype)
+
+
+def front(normed, weight, cosine, sine, gains, head_dim):
+    rows, depth = normed.shape
+    width = weight.shape[1]
+    groups = width // (4 * head_dim)
+    block = min(256, rows)
+    narrow = pl.BlockSpec((block, 2 * head_dim), lambda i: (i, 0))
+    table = pl.BlockSpec((block, head_dim), lambda i: (i, 0))
+    found = pl.pallas_call(
+        functools.partial(front_kernel, groups, head_dim),
+        grid=(rows // block,),
+        in_specs=[
+            pl.BlockSpec((block, depth), lambda i: (i, 0)),
+            pl.BlockSpec(weight.shape, lambda i: (0, 0), pipeline_mode=pl.Buffered(1)),
+            table,
+            table,
+            pl.BlockSpec(gains.shape, lambda i: (0, 0)),
+        ],
+        out_specs=[pl.BlockSpec((block, width), lambda i: (i, 0))] + [narrow] * (2 * groups),
+        out_shape=[jax.ShapeDtypeStruct((rows, width), jnp.float32)]
+        + [jax.ShapeDtypeStruct((rows, 2 * head_dim), jnp.bfloat16)] * (2 * groups),
+        compiler_params=pltpu.CompilerParams(vmem_limit_bytes=32 * MIB),
+        cost_estimate=pl.CostEstimate(flops=4 * rows * depth * width, bytes_accessed=2 * depth * width, transcendentals=0),
+    )(normed, weight, cosine, sine, gains)
+    return found[0], found[1 : 1 + groups], found[1 + groups :]
+
+
+def front_back_kernel(groups, head_dim, raw_ref, cos_ref, sin_ref, gains_ref, *refs):
+    queries, keys = refs[:groups], refs[groups : 2 * groups]
+    out_ref, sums_ref = refs[2 * groups :]
+
+    @pl.when(pl.program_id(0) == 0)
+    def _():
+        sums_ref[...] = jnp.zeros_like(sums_ref)
+
+    cosine = cos_ref[...]
+    sine = sin_ref[...] * half_signs(head_dim, 1.0)
+    for group in range(groups):
+        for at in range(4):
+            base = (group * 4 + at) * head_dim
+            source = queries[group] if at < 2 else keys[group]
+            grads = source[:, at % 2 * head_dim : (at % 2 + 1) * head_dim].astype(jnp.float32)
+            if at < 3:
+                gain = gains_ref[at // 2 : at // 2 + 1]
+                raw = raw_ref[:, base : base + head_dim]
+                scale = lax.rsqrt(jnp.mean(raw * raw, axis=1, keepdims=True) + EPSILON)
+                normal = raw * scale
+                grads = grads * cosine + turned_by(grads, sine)
+                sums_ref[at // 2 : at // 2 + 1] += jnp.sum(grads * normal, axis=0, keepdims=True)
+                grads = grads * gain
+                grads = scale * (grads - normal * jnp.mean(grads * normal, axis=1, keepdims=True))
+            out_ref[:, base : base + head_dim] = grads.astype(out_ref.dtype)
+
+
+def front_back(raw, cosine, sine, gains, grad_queries, grad_kv, head_dim):
+    rows, width = raw.shape
+    groups = width // (4 * head_dim)
+    block = min(256, rows)
+    narrow = pl.BlockSpec((block, 2 * head_dim), lambda i: (i, 0))
+    table = pl.BlockSpec((block, head_dim), lambda i: (i, 0))
+    wide = pl.BlockSpec((block, width), lambda i: (i, 0))
+    return pl.pallas_call(
+        functools.partial(front_back_kernel, groups, head_dim),
+        grid=(rows // block,),
+        in_specs=[wide, table, table, pl.BlockSpec(gains.shape, lambda i: (0, 0))] + [narrow] * (2 * groups),
+        out_specs=[wide, pl.BlockSpec((8, head_dim), lambda i: (0, 0))],
+        out_shape=[
+            jax.ShapeDtypeStruct((rows, width), jnp.bfloat16),
+            jax.ShapeDtypeStruct((8, head_dim), jnp.float32),
+        ],
+        compiler_params=pltpu.CompilerParams(vmem_limit_bytes=32 * MIB),
+        cost_estimate=pl.CostEstimate(flops=60 * rows * width, bytes_accessed=10 * rows * width, transcendentals=0),
+    )(raw, cosine, sine, gains, *grad_queries, *grad_kv)
+
+
+def last_product_kernel(grad_ref, weight_ref, hidden_ref, scale_ref, gain_ref, out_ref, dots_ref, gain_out_ref):
+    part = matmul(grad_ref[...], weight_ref[...], NT)
+    out_ref[0] = part.astype(out_ref.dtype)
+    product = part * (hidden_ref[...] * scale_ref[...])
+    gain_out_ref[...] = jnp.sum(product, axis=0, keepdims=True)
+    dots = jnp.sum(product * gain_ref[...], axis=1, keepdims=True)
+
+    @pl.when(pl.program_id(0) == 0)
+    def _():
+        dots_ref[...] = dots
+
+    @pl.when(pl.program_id(0) > 0)
+    def _():
+        dots_ref[...] += dots
+
+
+def last_product(grads, weight, hidden, scale, gain, pieces):
+    rows, width = grads.shape
+    depth = weight.shape[0]
+    block = depth // pieces // 2
+    return pl.pallas_call(
+        last_product_kernel,
+        grid=(depth // block,),
+        in_specs=[
+            pl.BlockSpec((rows, width), lambda i: (0, 0), pipeline_mode=pl.Buffered(1)),
+            pl.BlockSpec((block, width), lambda i: (i, 0)),
+            pl.BlockSpec((rows, block), lambda i: (0, i)),
+            pl.BlockSpec((rows, 1), lambda i: (0, 0)),
+            pl.BlockSpec((1, block), lambda i: (0, i)),
+        ],
+        out_specs=[
+            pl.BlockSpec((1, rows, block), lambda i: (i // 2, 0, i % 2)),
+            pl.BlockSpec((rows, 1), lambda i: (0, 0)),
+            pl.BlockSpec((1, block), lambda i: (0, i)),
+        ],
+        out_shape=[
+            jax.ShapeDtypeStruct((pieces, rows, depth // pieces), jnp.bfloat16),
+            jax.ShapeDtypeStruct((rows, 1), jnp.float32),
+            jax.ShapeDtypeStruct((1, depth), jnp.float32),
+        ],
+        compiler_params=pltpu.CompilerParams(vmem_limit_bytes=32 * MIB),
+        cost_estimate=pl.CostEstimate(flops=4 * rows * depth * width, bytes_accessed=2 * depth * width, transcendentals=0),
+    )(grads, weight, hidden, scale, gain)
+
+
+def resid_kernel(sum_ref, hidden_ref, gain_ref, resid_ref, normed_ref, normed_t_ref, scale_ref):
+    total = jnp.concatenate([sum_ref[at] for at in range(sum_ref.shape[0])], axis=1)
+    resid = hidden_ref[...] + total.astype(jnp.float32)
+    scale = lax.rsqrt(jnp.mean(resid * resid, axis=1, keepdims=True) + EPSILON)
+    normed = resid * scale * gain_ref[...]
+    resid_ref[...] = resid
+    scale_ref[...] = scale
+    normed_ref[...] = normed.astype(normed_ref.dtype)
+    normed_t_ref[...] = jnp.transpose(normed).astype(normed_t_ref.dtype)
+
+
+def add_and_norm(total, hidden, gain):
+    pieces, rows, width = total.shape
+    depth = pieces * width
+    block = min(256, rows)
+    wide = pl.BlockSpec((block, depth), lambda i: (i, 0))
+    return pl.pallas_call(
+        resid_kernel,
+        grid=(rows // block,),
+        in_specs=[
+            pl.BlockSpec((pieces, block, width), lambda i: (0, i, 0)),
+            wide,
+            pl.BlockSpec((1, depth), lambda i: (0, 0)),
+        ],
+        out_specs=[
+            wide,
+            wide,
+            pl.BlockSpec((depth, block), lambda i: (0, i)),
+            pl.BlockSpec((block, 1), lambda i: (i, 0)),
+        ],
+        out_shape=[
+            jax.ShapeDtypeStruct((rows, depth), jnp.float32),
+            jax.ShapeDtypeStruct((rows, depth), jnp.bfloat16),
+            jax.ShapeDtypeStruct((depth, rows), jnp.bfloat16),
+            jax.ShapeDtypeStruct((rows, 1), jnp.float32),
+        ],
+        compiler_params=pltpu.CompilerParams(vmem_limit_bytes=40 * MIB),
+        cost_estimate=pl.CostEstimate(flops=10 * rows * depth, bytes_accessed=18 * rows * depth, transcendentals=0),
+    )(total, hidden, gain)
+
+
+def resid_back_kernel(sum_ref, cot_ref, resid_ref, scale_ref, gain_ref, grad_ref, rounded_ref, gain_out_ref):
+    grads = jnp.concatenate([sum_ref[at] for at in range(sum_ref.shape[0])], axis=1).astype(jnp.float32)
+    scale = scale_ref[...]
+    normal = resid_ref[...] * scale
+    sums = jnp.sum(grads * normal, axis=0, keepdims=True)
+    grads = grads * gain_ref[...]
+    grads = scale * (grads - normal * jnp.mean(grads * normal, axis=1, keepdims=True))
+    grads = cot_ref[...].astype(jnp.float32) + grads
+    grad_ref[...] = grads
+    rounded_ref[...] = grads.astype(rounded_ref.dtype)
+
+    @pl.when(pl.program_id(0) == 0)
+    def _():
+        gain_out_ref[...] = sums
+
+    @pl.when(pl.program_id(0) > 0)
+    def _():
+        gain_out_ref[...] += sums
+
+
+def norm_and_add_back(total, cotangent, resid, scale, gain):
+    pieces, rows, width = total.shape
+    depth = pieces * width
+    block = min(256, rows)
+    wide = pl.BlockSpec((block, depth), lambda i: (i, 0))
+    whole = pl.BlockSpec((1, depth), lambda i: (0, 0))
+    return pl.pallas_call(
+        resid_back_kernel,
+        grid=(rows // block,),
+        in_specs=[
+            pl.BlockSpec((pieces, block, width), lambda i: (0, i, 0)),
+            wide,
+            wide,
+            pl.BlockSpec((block, 1), lambda i: (i, 0)),
+            whole,
+        ],
+        out_specs=[wide, wide, whole],
+        out_shape=[
+            jax.ShapeDtypeStruct((rows, depth), jnp.float32),
+            jax.ShapeDtypeStruct((rows, depth), jnp.bfloat16),
+            jax.ShapeDtypeStruct((1, depth), jnp.float32),
+        ],
+        compiler_params=pltpu.CompilerParams(vmem_limit_bytes=40 * MIB),
+        cost_estimate=pl.CostEstimate(flops=10 * rows * depth, bytes_accessed=16 * rows * depth, transcendentals=0),
+    )(total, cotangent, resid, scale, gain)
+
+
+def step_of(rate, weight, moment, average, gradient, outs):
+    moment = MOMENTUM * moment + gradient
+    weight = weight - rate * (gradient + MOMENTUM * moment)
+    average = EMA_DECAY * average + (1.0 - EMA_DECAY) * weight
+    for out, value in zip(outs, (weight, moment, average, average)):
+        out[...] = value.astype(out.dtype)
+
+
+def mlp_step_kernel(rate, chunks, *refs):
+    grads, held, outs = refs[:chunks], refs[chunks : chunks + 6], refs[chunks + 6 :]
+    for chunk in range(chunks):
+
+        @pl.when(pl.program_id(0) == chunk)
+        def _():
+            both = grads[chunk][:2].astype(jnp.float32)
+            step_of(rate, *(ref[...] for ref in held[:3]), both, outs[:4])
+            down = jnp.transpose(grads[chunk][2].astype(jnp.float32))
+            step_of(rate, *(ref[...] for ref in held[3:]), down, outs[4:])
+
+
+def mlp_step(rate, grads, gate_up, down):
+    chunks = len(grads)
+    kinds, depth, width = grads[0].shape
+    gate_up_spec = pl.BlockSpec((2, depth, width), lambda i: (0, 0, i))
+    down_spec = pl.BlockSpec((width, depth), lambda i: (i, 0))
+    types = (jnp.float32,) * 3 + (jnp.bfloat16,)
+    return pl.pallas_call(
+        functools.partial(mlp_step_kernel, rate, chunks),
+        grid=(chunks,),
+        in_specs=[pl.BlockSpec((kinds, depth, width), lambda i: (0, 0, 0), pipeline_mode=pl.Buffered(1))] * chunks
+        + [gate_up_spec] * 3
+        + [down_spec] * 3,
+        out_specs=[gate_up_spec] * 4 + [down_spec] * 4,
+        out_shape=[jax.ShapeDtypeStruct(gate_up[0].shape, kind) for kind in types]
+        + [jax.ShapeDtypeStruct(down[0].shape, kind) for kind in types],
+        compiler_params=pltpu.CompilerParams(vmem_limit_bytes=40 * MIB),
+        cost_estimate=pl.CostEstimate(flops=0, bytes_accessed=26 * chunks * kinds * depth * width, transcendentals=0),
+    )(*grads, *gate_up, *down)
+
+
+def turned_step_kernel(rate, grad_ref, *refs):
+    step_of(rate, *(ref[...] for ref in refs[:3]), jnp.transpose(grad_ref[...].astype(jnp.float32)), refs[3:])
+
+
+def turned_step(rate, grad_t, held):
+    types = (jnp.float32,) * 3 + (jnp.bfloat16,)
+    return pl.pallas_call(
+        functools.partial(turned_step_kernel, rate),
+        in_specs=[pl.BlockSpec(memory_space=pltpu.VMEM)] * 4,
+        out_specs=[pl.BlockSpec(memory_space=pltpu.VMEM)] * 4,
+        out_shape=[jax.ShapeDtypeStruct(held[0].shape, kind) for kind in types],
+        compiler_params=pltpu.CompilerParams(vmem_limit_bytes=24 * MIB),
+        cost_estimate=pl.CostEstimate(flops=0, bytes_accessed=28 * grad_t.size, transcendentals=0),
+    )(grad_t, *held)
+
+
 def rms_scale(values_in):
     return lax.rsqrt(jnp.mean(values_in * values_in, axis=-1, keepdims=True) + EPSILON)
-
-
-def rotate_half(values_in, cosine, sine):
-    half_dim = values_in.shape[-1] // 2
-    turned = jnp.concatenate([-values_in[..., half_dim:], values_in[..., :half_dim]], axis=-1)
-    return values_in * cosine + turned * sine
-
-
-def rotate_back(grads, cosine, sine):
-    half_dim = grads.shape[-1] // 2
-    scaled = grads * sine
-    turned = jnp.concatenate([scaled[..., half_dim:], -scaled[..., :half_dim]], axis=-1)
-    return grads * cosine + turned
-
-
-def norm_back(grads, normal, scale_rows, gain):
-    grad_hat = grads * gain
-    return scale_rows * (grad_hat - normal * jnp.mean(grad_hat * normal, axis=-1, keepdims=True))
 
 
 def rope_tables(offsets, head_dim):
@@ -613,13 +886,7 @@
     def columns_of(values_in):
         return lax.dynamic_slice_in_dim(values_in, col_begin, width_cols, values_in.ndim - 1)
 
-    def across(pieces):
-        return jnp.concatenate([pieces[piece] for piece in range(tensor_ways)], axis=1)
-
     qkv_full = lax.all_gather(w_qkv.astype(bf16), "dp", axis=0, tiled=True)
-
-    out_turned, qkv_full = tie(w_out.astype(bf16).T, qkv_full)
-    out_blocks = lax.all_gather(out_turned, "dp", axis=0)
 
     ends_at = jnp.cumsum(doc_lengths)
     starts_at = ends_at - doc_lengths
@@ -647,63 +914,47 @@
     scale_one = rms_scale(hidden_in)
     normal_one = hidden_in * scale_one
     normed_one_b = (normal_one * gain_attn).astype(bf16)
-    projected = dot(normed_one_b, qkv_full, NN)
-
-    raw_queries, raw_keys, queries, kv_every = [], [], [], []
+    gains_two = jnp.stack([gain_query, gain_key])
+    projected, queries, kv_local = front(normed_one_b, qkv_full, cosine, sine, gains_two, head_dim)
+    kv_every = []
     for group in range(groups):
-        base = group * 4 * head_dim
-        query_raw = projected[:, base : base + 2 * head_dim].reshape(row_count, 2, head_dim)
-        key_raw = projected[:, base + 2 * head_dim : base + 3 * head_dim]
-        value = projected[:, base + 3 * head_dim : base + 4 * head_dim]
-        query = rotate_half(
-            query_raw * rms_scale(query_raw) * gain_query, cosine[:, None], sine[:, None]
-        )
-        key = rotate_half(key_raw * rms_scale(key_raw) * gain_key, cosine, sine)
-        raw_queries.append(query_raw)
-        raw_keys.append(key_raw)
-        queries.append(query.reshape(row_count, 2 * head_dim).astype(bf16))
-        kv_local = jnp.concatenate([key, value], axis=1).astype(bf16)
+        value = kv_local[group]
         if group:
-            kv_local, kv_every[-1] = tie(kv_local, kv_every[-1])
-        else:
-            kv_local, out_blocks = tie(kv_local, out_blocks)
-        kv_every.append(lax.all_gather(kv_local, "dp", axis=0, tiled=True))
+            value, kv_every[-1] = tie(value, kv_every[-1])
+        kv_every.append(lax.all_gather(value, "dp", axis=0, tiled=True))
 
     down_t = w_down.T
-    chunk_weights = []
-    out_full_t = out_blocks.reshape(model_dim, w_out.shape[0])
 
     def chunk_shard(chunk):
         units = slice(chunk * ff_chunk, (chunk + 1) * ff_chunk)
-        return jnp.stack([w_gate_up[0, :, units], w_gate_up[1, :, units], down_t[:, units]]).astype(bf16)
+        kinds = [w_gate_up[0, :, units], w_gate_up[1, :, units], down_t[:, units]]
+        return jnp.stack(kinds + ([w_out.T] if chunk == 0 else [])).astype(bf16)
 
     def chunk_gather(shard):
         return lax.all_gather(shard, "dp", axis=0)
 
-    shard, kv_every[-1] = tie(chunk_shard(0), kv_every[-1])
-    chunk_weights.append(chunk_gather(shard))
-    mixed, totals = [], []
+    mixed, totals, chunk_weights = [], [], []
     for group in range(groups):
         mixed_rows, total_rows = attend(
             bounds, queries[group], begin_rows, kv_every[group], head_dim, query_rows, min(1024, tokens_all)
         )
+        if group == 0:
+            shard, kv_every[-1], mixed_rows, cotangent_t = tie(
+                chunk_shard(0), kv_every[-1], mixed_rows, cotangent.T
+            )
+            chunk_weights.append(chunk_gather(shard))
         mixed.append(mixed_rows)
         totals.append(total_rows)
     mixed_b = jnp.concatenate(mixed, axis=1)
     shard, chunk_weights[0], mixed_b = tie(chunk_shard(1), chunk_weights[0], mixed_b)
     chunk_weights.append(chunk_gather(shard))
-    attn_part = back_product([(mixed_b,)], [out_blocks[:, None]], 0, tensor_ways)
+    out_full_t = chunk_weights[0][:, 3].reshape(model_dim, w_out.shape[0])
+    attn_part = back_product([(mixed_b,)], chunk_weights[:1], 3, tensor_ways)
     attn_sum = tensor_sum(attn_part, 0)
     shard, chunk_weights[1], attn_sum = tie(chunk_shard(2), chunk_weights[1], attn_sum)
     chunk_weights.append(chunk_gather(shard))
-    attn = across(attn_sum).astype(f32)
-    resid_one = hidden_in + attn
-    scale_two = rms_scale(resid_one)
-    normal_two = resid_one * scale_two
-    normed_two_b = (normal_two * gain_mlp).astype(bf16)
-
-    normed_two_t = normed_two_b.T
-    cotangent_t = cotangent.T
+    resid_one, normed_two_b, normed_two_t, scale_two = add_and_norm(attn_sum, hidden_in, gain_mlp[None])
+
     weight_grads, hiddens, back_pairs = [], [], []
     for chunk in range(CHUNKS):
         hidden_b, gate_grad, up_grad, weight_grad = mlp_chunk(
@@ -714,18 +965,20 @@
         weight_grads.append(lax.psum_scatter(weight_grad, "dp", scatter_dimension=0))
 
     part_two = back_product(back_pairs, chunk_weights, 0, tensor_ways)
-    part_two, weight_grads[0] = tie(part_two, weight_grads[0])
-    grad_normed_two = across(tensor_sum(part_two, 1)).astype(f32)
-    gain_mlp_part = jnp.sum(columns_of(grad_normed_two * normal_two), axis=0)
-    grad_resid = cotangent.astype(f32) + norm_back(grad_normed_two, normal_two, scale_two, gain_mlp)
-    grad_attn_b = grad_resid.astype(bf16)
+    mlp_part = back_product(hiddens, chunk_weights, 2, tensor_ways)
+    part_two, mlp_part, weight_grads[0] = tie(part_two, mlp_part, weight_grads[0])
+    part_two_sum = tensor_sum(part_two, 1)
+    grad_resid, grad_attn_b, gain_mlp_part = norm_and_add_back(
+        part_two_sum, cotangent, resid_one, scale_two, gain_mlp[None]
+    )
     grad_mixed_b = dot(grad_attn_b, out_full_t, NN).astype(bf16)
 
-    grad_queries, kv_grads = [], []
+    grad_out_t = dot(grad_attn_b, mixed_b, TN).astype(bf16)
+    grad_queries, kv_sums = [], []
     for group in range(groups):
-        cols = slice(group * 2 * head_dim, (group + 1) * 2 * head_dim)
-        grad_rows, weight_grads[group + 1] = tie(grad_mixed_b[:, cols], weight_grads[group + 1])
-        grad_query, kv_grad = attend_back(
+        grad_rows = grad_mixed_b[:, group * 2 * head_dim : (group + 1) * 2 * head_dim]
+        grad_rows, weight_grads[group + 1] = tie(grad_rows, weight_grads[group + 1])
+        grad_query, kv_sum = attend_back(
             bounds,
             queries[group],
             grad_rows,
@@ -738,75 +991,50 @@
             min(512, tokens_all),
         )
         grad_queries.append(grad_query)
-        kv_grads.append(lax.psum_scatter(kv_grad, "dp", scatter_dimension=0, tiled=True).astype(f32))
-    grad_out_t = dot(grad_attn_b, mixed_b, TN).astype(bf16)
-    grad_out_t, kv_grads[-1] = tie(grad_out_t, kv_grads[-1])
-    out_shard = lax.psum_scatter(grad_out_t, "dp", scatter_dimension=0, tiled=True).astype(f32).T
-
-    hidden_first, grad_queries[-1] = tie(hiddens[0][0], grad_queries[-1])
-    hiddens[0] = (hidden_first,)
-    mlp_part = back_product(hiddens, chunk_weights, 2, tensor_ways)
-    mlp_cols = tensor_sum(mlp_part, 2, False).astype(f32)
-
-    grad_parts = []
-    gain_query_part = jnp.zeros((head_dim,), f32)
-    gain_key_part = jnp.zeros((head_dim,), f32)
-    for group in range(groups):
-        query_raw = raw_queries[group]
-        key_raw = raw_keys[group]
-        query_scale = rms_scale(query_raw)
-        query_normal = query_raw * query_scale
-        key_scale = rms_scale(key_raw)
-        key_normal = key_raw * key_scale
-        grad_query_norm = rotate_back(
-            grad_queries[group].reshape(row_count, 2, head_dim), cosine[:, None], sine[:, None]
-        )
-        gain_query_part += jnp.sum(grad_query_norm * query_normal, axis=(0, 1))
-        grad_query_raw = norm_back(grad_query_norm, query_normal, query_scale, gain_query)
-        grad_key_norm = rotate_back(kv_grads[group][:, :head_dim], cosine, sine)
-        gain_key_part += jnp.sum(grad_key_norm * key_normal, axis=0)
-        grad_key_raw = norm_back(grad_key_norm, key_normal, key_scale, gain_key)
-        grad_parts += [
-            grad_query_raw.reshape(row_count, 2 * head_dim),
-            grad_key_raw,
-            kv_grads[group][:, head_dim:],
-        ]
-    grad_projected_b = jnp.concatenate([part.astype(bf16) for part in grad_parts], axis=1)
+        kv_sums.append(kv_sum)
+    grad_out_t, weight_grads[groups] = tie(grad_out_t, weight_grads[groups])
+    out_grad = lax.psum_scatter(grad_out_t, "dp", scatter_dimension=0, tiled=True)
+    kv_sums[0], out_grad = tie(kv_sums[0], out_grad)
+    kv_grads = [lax.psum_scatter(kv_sum, "dp", scatter_dimension=0, tiled=True) for kv_sum in kv_sums]
+    mlp_part, grad_queries[-1] = tie(mlp_part, grad_queries[-1])
+    rate_matrix = LR_MATRIX / math.sqrt(tokens_all)
+    mlp_sum = tensor_sum(mlp_part, 2, False)
+    updates = (
+        *turned_step(rate_matrix, out_grad, (w_out, m_out, a_out)),
+        *mlp_step(rate_matrix, weight_grads, (w_gate_up, m_gate_up, a_gate_up), (w_down, m_down, a_down)),
+    )
+    mlp_cols = mlp_sum.astype(f32)
+    resid_cols = columns_of(resid_one)
+    attn_cols = lax.dynamic_index_in_dim(attn_sum, tensor_at, 0, False).astype(f32)
+    mask_rows = valid_mask.astype(f32)[:, None]
+    stats_part = [
+        jnp.sum(mask_rows * columns * columns) for columns in (columns_of(hidden_in), attn_cols, mlp_cols)
+    ]
+    stats_part.append(jnp.where(tensor_at == 0, jnp.sum(valid_mask.astype(f32)), 0.0))
+    gain_mlp_wide = lax.dynamic_update_slice_in_dim(
+        jnp.zeros((model_dim,), f32), columns_of(gain_mlp_part[0]), col_begin, 0
+    )
+    mixed_cols, gain_mlp_wide, stats_part, kv_grads[-1], updates = tie(
+        resid_cols + mlp_cols, gain_mlp_wide, jnp.stack(stats_part), kv_grads[-1], updates
+    )
+    grad_projected_b, gains_found = front_back(
+        projected, cosine, sine, gains_two, grad_queries, kv_grads, head_dim
+    )
     grad_qkv = dot(normed_one_b, grad_projected_b, TN).astype(bf16)
     qkv_shard = lax.psum_scatter(grad_qkv, "dp", scatter_dimension=0, tiled=True).astype(f32)
-    part_one = dot(grad_projected_b, qkv_full, NT)
-    part_one_b = jnp.stack(
-        [part_one[:, at * width_cols : (at + 1) * width_cols] for at in range(tensor_ways)]
-    ).astype(bf16)
-    dots_part = jnp.sum(part_one * (normal_one * gain_attn), axis=1).reshape(row_count // 128, 128)
-    gain_attn_part = jnp.sum(part_one * normal_one, axis=0)
-
-    attn_cols = columns_of(attn)
-    mixed_cols = columns_of(resid_one) + mlp_cols
-    mask_rows = valid_mask.astype(f32)[:, None]
-
-    def column_squares(columns):
-        return jnp.sum(mask_rows * columns * columns)
-
-    count_part = jnp.where(tensor_at == 0, jnp.sum(valid_mask.astype(f32)), 0.0)
-    stats_part = jnp.stack(
-        [
-            column_squares(columns_of(hidden_in)),
-            column_squares(attn_cols),
-            column_squares(mlp_cols),
-            count_part,
-        ]
-    )
-    gain_mlp_wide = lax.dynamic_update_slice_in_dim(
-        jnp.zeros((model_dim,), f32), gain_mlp_part, col_begin, 0
-    )
+    part_one, dots_part, gain_attn_part = last_product(
+        grad_projected_b, qkv_full, hidden_in, scale_one, gain_attn[None], tensor_ways
+    )
+
     gains_part = jnp.concatenate(
-        [gain_attn_part, gain_mlp_wide, gain_query_part, gain_key_part, stats_part]
+        [gain_attn_part[0], gain_mlp_wide, gains_found[0], gains_found[1], stats_part]
     )
     gains_count = gains_part.shape[0]
     gains_rows = -(-gains_count // 1024) * 8
     gains_part = jnp.pad(gains_part, (0, gains_rows * 128 - gains_count)).reshape(gains_rows, 128)
-    grad_one_cols, row_dots, gains_sum = last_sum(part_one_b, dots_part, gains_part, data_ways, 3)
+    grad_one_cols, row_dots, gains_sum = last_sum(
+        part_one, dots_part.reshape(row_count // 128, 128), gains_part, data_ways, 3
+    )
     gains_sum = gains_sum.reshape(-1)[:gains_count]
     grad_cols = columns_of(grad_resid) + scale_one * (
         grad_one_cols.astype(f32) * columns_of(gain_attn)
@@ -816,18 +1044,13 @@
     stats_sum = gains_sum[norm_gains.shape[0] :]
     branch_rms = jnp.sqrt(stats_sum[:3] / (stats_sum[3] * model_dim))
 
-    rate_matrix = LR_MATRIX / math.sqrt(tokens_all)
     rate_gain = LR_GAIN / math.sqrt(tokens_all)
-    gate_up_shard = jnp.concatenate([grad[:2] for grad in weight_grads], axis=2).astype(f32)
-    down_shard = jnp.concatenate([grad[2] for grad in weight_grads], axis=1).astype(f32).T
     return (
         mixed_cols,
         grad_cols,
         branch_rms,
         *nesterov(w_qkv, m_qkv, a_qkv, qkv_shard, rate_matrix),
-        *nesterov(w_out, m_out, a_out, out_shard, rate_matrix),
-        *nesterov(w_gate_up, m_gate_up, a_gate_up, gate_up_shard, rate_matrix),
-        *nesterov(w_down, m_down, a_down, down_shard, rate_matrix),
+        *updates,
         *nesterov(norm_gains, m_gains, a_gains, grad_gains, rate_gain),
     )
 

time: 934 us -> 859 us (0.920); the launches traced: 941 us -> 850 us
  other arithmetic: 132 us -> 40.7 us
  Pallas kernels: 374 us -> 411 us
  matrix products: 35.4 us -> 12.3 us
  local copies, waits for them, and re-layouts: 96.8 us -> 82.2 us
    all_gather x3, waiting for transfers between devices: 49.2 us -> 96.3 us  [chunk_gather(): return lax.all_gather(shard, 'dp', axis=0)]
    pallas_call x0 -> x7, Pallas kernels: none -> 46.6 us  [the longest x1 10.2 us: norm_and_add_back(): pl.pallas_call(resid_back_kernel, grid=(rows // block,), in_specs=[pl.Blo...]
    all_gather x3 -> x2, waiting for transfers between devices: 105 us -> 66.5 us  [local(): kv_every.append(lax.all_gather(value, 'dp', axis=0, tiled=True))]
    reduce_sum x9 -> x2, other arithmetic: 34.2 us -> 5.83 us  [the longest x1 5.23 us: local(): jnp.sum(mask_rows * columns * columns)]
    reduce_scatter x1, waiting for transfers between devices: 0.01 us -> 23.8 us  [local(): lax.psum_scatter(grad_out_t, 'dp', scatter_dimension=0, tiled=True)]
    dot_general x5 -> x3, matrix products: 35.4 us -> 12.3 us  [dot(): return lax.dot_general(a, b, dims, preferred_element_type=jnp.float32)]
    unnamed x244 -> x143, local copies, waits for them, and re-layouts: 55.8 us -> 71.5 us
    mul x6 -> x0, other arithmetic: 14.2 us -> none  [the longest x1 4.14 us: local(): normal_one = hidden_in * scale_one]
  transfers between devices with their start and end apart: 14 -> 13, of which waited for: 9 -> 8; matrix products, arithmetic and copies ran while one was open for 25% -> 7% of each run, Pallas kernels for 40% -> 47%
where the time goes in v2:
time: 859 us; the launch traced here: 850 us
  Pallas kernels  411 us (48%)
  waiting for transfers between devices  286 us (33%)
  local copies, waits for them, and re-layouts  82.2 us (10%)
  other arithmetic  40.7 us (5%)
  between operations  16.3 us (2%)
  matrix products  12.3 us (1%)
    pallas_call x3, Pallas kernels, tensor_sum(): pl.pallas_call(functools.partial(tensor_sum_kernel, bits, whole), out_sha...  178 us
    all_gather x3, waiting for transfers between devices, chunk_gather(): return lax.all_gather(shard, 'dp', axis=0)  96.3 us
    unnamed x143, local copies, waits for them, and re-layouts  71.5 us
    pallas_call x3, Pallas kernels, mlp_chunk(): pl.pallas_call(mlp_kernel, grid=(width // block,), in_specs=[held(normed)...  69.7 us
    all_gather x2, waiting for transfers between devices, local(): kv_every.append(lax.all_gather(value, 'dp', axis=0, tiled=True))  66.5 us
    pallas_call x1, Pallas kernels, last_sum(): pl.pallas_call(functools.partial(last_sum_kernel, bits, data_ways), out_s...  40.2 us
    pallas_call x3, Pallas kernels, back_product(): pl.pallas_call(functools.partial(back_product_kernel, kinds), grid=(ways,...  39.8 us
    reduce_scatter x2, waiting for transfers between devices, local(): lax.psum_scatter(kv_sum, 'dp', scatter_dimension=0, tiled=True)  39.2 us
  transfers between devices with their start and end apart: 13, of which 8 were waited for; matrix products, arithmetic and copies ran while one was open for 7% of the time, Pallas kernels for 47%

profile of v2, /device:TPU:0, one launch (start us, length us, event | category | flops | bytes accessed | tf_op | source)
XLA Modules:
  0.0 849.6 jit_solution(1986677205735121667)
XLA Ops:
  14.2 4.4 multiply_reduce_fusion
  20.5 5.6 multiply_convert_fusion
  26.1 34.0 %all-gather.10.cloned.1.call-done.weight_ref = bf16[2048,1024]{1,0:T(8,128)(2,1)} async-done(((bf16[256,1024]{1,0:T(8,128)(2,1)}), bf16[2048,1024]{1,0:T(8,128)(2,1)}) %all-gather.10.cloned.1.call-update) | async-done | bytes 4194320 | tf_op jit(solution)/shard_map/all_gather | solution.py:889
  60.1 2.2 copy-done.14
  62.3 2.2 copy-done.45
  64.5 5.9 shard_map.362
  75.6 46.0 %all-gather.12.cloned.1.call-done.kv_ref = bf16[8192,256]{1,0:T(8,128)(2,1)} async-done(((bf16[1024,256]{1,0:T(8,128)(2,1)}), bf16[8192,256]{1,0:T(8,128)(2,1)}) %all-gather.12.cloned.1.call-update) | async-done | bytes 4194320 | tf_op jit(solution)/shard_map/all_gather | solution.py:924
  123.7 2.6 copy.57
  127.6 6.4 copy.59
  136.0 2.4 fusion.12
  139.5 2.2 copy-done.47
  142.8 4.9 shard_map.363
  149.1 20.6 %all-gather.14.cloned.1.call-done.kv_ref = bf16[8192,256]{1,0:T(8,128)(2,1)} async-done(((bf16[1024,256]{1,0:T(8,128)(2,1)}), bf16[8192,256]{1,0:T(8,128)(2,1)}) %all-gather.14.cloned.1.call-update) | async-done | bytes 4194320 | tf_op jit(solution)/shard_map/all_gather | solution.py:924
  175.3 4.9 shard_map.364
  182.7 72.6 %all-gather.16.cloned.1.call-done = bf16[32,256,512]{2,1,0:T(8,128)(2,1)} async-done(((bf16[4,256,512]{2,1,0:T(8,128)(2,1)}), bf16[32,256,512]{2,1,0:T(8,128)(2,1)}) %all-gather.16.cloned.1.call-update) | async-done | bytes 8388624 | tf_op jit(solution)/shard_map/all_gather | solution.py:934
  257.3 8.3 shard_map.365.part_ref
  267.8 71.7 %shard_map.366.sum_ref = bf16[4,1024,512]{2,1,0:T(8,128)(2,1)S(1)} custom-call(bf16[4,1024,512]{2,1,0:T(8,128)(2,1)S(1)} %copy-done.5), custom_call_target="tpu_custom_call" | custom-call | bytes 268435456 | tf_op jit(solution)/shard_map/pallas_call | solution.py:421
  343.7 8.5 shard_map.367
  357.0 23.3 %shard_map.368 = (bf16[1024,512]{1,0:T(8,128)(2,1)}, bf16[1024,512]{1,0:T(8,128)(2,1)}, bf16[1024,512]{1,0:T(8,128)(2,1)}, bf16[8,3,256,512]{3,2,1,0:T(8,128)(2,1)}) custom-call(bf16[1024,2048]{1,0:T(8,128)(2,1)} %copy-done.49, bf16[1024,2048]{1,0:T(8,128)(2,1)} %cot_ref.7, bf16[2048,1024]{1,0:T(8,128)(2,1)} %copy-done.50, bf16[2048,1024]{1,0:T(8,128)(2,1)} %bitcast.95, ...), custom_call_target="tpu_custom_call" | custom-call | flops 25769803776 | bytes 12582912 | tf_op jit(solution)/shard_map/pallas_call | solution.py:244
  380.7 23.8 %all-gather.20.cloned.1.call-done = bf16[24,256,512]{2,1,0:T(8,128)(2,1)} async-done(((bf16[3,256,512]{2,1,0:T(8,128)(2,1)}), bf16[24,256,512]{2,1,0:T(8,128)(2,1)}) %all-gather.20.cloned.1.call-update) | async-done | bytes 6291472 | tf_op jit(solution)/shard_map/all_gather | solution.py:934
  404.5 23.1 %shard_map.370 = (bf16[1024,512]{1,0:T(8,128)(2,1)}, bf16[1024,512]{1,0:T(8,128)(2,1)}, bf16[1024,512]{1,0:T(8,128)(2,1)}, bf16[8,3,256,512]{3,2,1,0:T(8,128)(2,1)}) custom-call(bf16[1024,2048]{1,0:T(8,128)(2,1)} %copy-done.49, bf16[1024,2048]{1,0:T(8,128)(2,1)} %cot_ref.7, bf16[2048,1024]{1,0:T(8,128)(2,1)} %copy-done.50, bf16[2048,1024]{1,0:T(8,128)(2,1)} %bitcast.96, ...), custom_call_target="tpu_custom_call" | custom-call | flops 25769803776 | bytes 12582912 | tf_op jit(solution)/shard_map/pallas_call | solution.py:244
  427.7 23.3 %shard_map.369 = (bf16[1024,512]{1,0:T(8,128)(2,1)}, bf16[1024,512]{1,0:T(8,128)(2,1)}, bf16[1024,512]{1,0:T(8,128)(2,1)}, bf16[8,3,256,512]{3,2,1,0:T(8,128)(2,1)}) custom-call(bf16[1024,2048]{1,0:T(8,128)(2,1)} %copy-done.49, bf16[1024,2048]{1,0:T(8,128)(2,1)} %cot_ref.7, bf16[2048,1024]{1,0:T(8,128)(2,1)} %copy-done.50, bf16[2048,1024]{1,0:T(8,128)(2,1)} %bitcast.97, ...), custom_call_target="tpu_custom_call" | custom-call | flops 25769803776 | bytes 12582912 | tf_op jit(solution)/shard_map/pallas_call | solution.py:244
  451.2 3.1 slice.93
  454.3 12.2 %shard_map.372.part_ref = bf16[4,1024,512]{2,1,0:T(8,128)(2,1)} custom-call(bf16[1024,512]{1,0:T(8,128)(2,1)} %get-tuple-element.143.refs_0_, bf16[8,4,256,512]{3,2,1,0:T(8,128)(2,1)} %bitcast.87, bf16[1024,512]{1,0:T(8,128)(2,1)} %get-tuple-element.144.refs_2_, bf16[8,3,256,512]{3,2,1,0:T(8,128)(2,1)} %bitcast.90, ...), custom_call_target="tpu_custom_call" | custom-call | flops 6442450944 | bytes 6291456 | tf_op jit(solution)/shard_map/pallas_call | solution.py:280
  466.6 19.3 %shard_map.371.part_ref = bf16[4,1024,512]{2,1,0:T(8,128)(2,1)} custom-call(bf16[1024,512]{1,0:T(8,128)(2,1)} %get-tuple-element.135.refs_0_, bf16[1024,512]{1,0:T(8,128)(2,1)} %get-tuple-element.136.refs_1_, bf16[8,4,256,512]{3,2,1,0:T(8,128)(2,1)} %bitcast.88, bf16[1024,512]{1,0:T(8,128)(2,1)} %get-tuple-element.138.refs_3_, ...), custom_call_target="tpu_custom_call" | custom-call | flops 12884901888 | bytes 12582912 | tf_op jit(solution)/shard_map/pallas_call | solution.py:280
  488.0 71.7 %shard_map.373.sum_ref = bf16[4,1024,512]{2,1,0:T(8,128)(2,1)S(1)} custom-call(bf16[4,1024,512]{2,1,0:T(8,128)(2,1)S(1)} %copy-done.13), custom_call_target="tpu_custom_call" | custom-call | bytes 268435456 | tf_op jit(solution)/shard_map/pallas_call | solution.py:421
  559.8 10.2 %shard_map.374 = (f32[1024,2048]{1,0:T(8,128)}, bf16[1024,2048]{1,0:T(8,128)(2,1)S(1)}, f32[1,2048]{1,0:T(1,128)S(1)}) custom-call(bf16[4,1024,512]{2,1,0:T(8,128)(2,1)S(1)} %shard_map.373.sum_ref, bf16[1024,2048]{1,0:T(8,128)(2,1)S(1)} %copy-done.6, f32[1024,2048]{1,0:T(8,128)} %get-tuple-element.131.resid_ref, f32[1024,1]{1,0:T(8,128)S(1)} %copy-done.34, ...), custom_call_target="tpu_custom_call" | custom-call | flops 20971520 | bytes 33554432 | tf_op jit(solution)/shard_map/pallas_call | solution.py:746
  570.0 2.3 convolution_convert_fusion.2
  573.4 3.7 convolution_convert_fusion.1
  577.3 13.1 %shard_map.375 = (f32[1024,256]{1,0:T(8,128)}, bf16[8192,256]{1,0:T(8,128)(2,1)}) custom-call(s32[3,2]{1,0:T(4,128)} %copy-done.44, bf16[1024,256]{1,0:T(8,128)(2,1)} %copy-done.53, bf16[1024,256]{1,0:T(8,128)(2,1)} %get-tuple-element.152.grad_ref, bf16[1024,256]{1,0:T(8,128)(2,1)} %copy-done.39, f32[2,1,1024]{2,1,0:T(1,128)} %copy-done.56, ...), custom_call_target="tpu_custom_call" | custom-call | flops 21474836480 | bytes 4194304 | tf_op jit(solution)/shard_map/pallas_call | solution.py:171
  590.5 25.8 %reduce-scatter.14.cloned.1.call-done = bf16[1,3,256,512]{3,2,1,0:T(8,128)(2,1)} async-done(((bf16[8,3,256,512]{3,2,1,0:T(8,128)(2,1)}), bf16[1,3,256,512]{3,2,1,0:T(8,128)(2,1)}) %reduce-scatter.14.cloned.1.call-update) | async-done | bytes 786448 | tf_op jit(solution)/shard_map/reduce_scatter | solution.py:965
  616.3 13.0 %shard_map.377 = (f32[1024,256]{1,0:T(8,128)}, bf16[8192,256]{1,0:T(8,128)(2,1)}) custom-call(s32[3,2]{1,0:T(4,128)} %copy-done.44, bf16[1024,256]{1,0:T(8,128)(2,1)} %copy-done.51, bf16[1024,256]{1,0:T(8,128)(2,1)} %get-tuple-element.159.grad_ref, bf16[1024,256]{1,0:T(8,128)(2,1)} %copy-done.37, f32[2,1,1024]{2,1,0:T(1,128)} %copy-done.55, ...), custom_call_target="tpu_custom_call" | custom-call | flops 21474836480 | bytes 4194304 | tf_op jit(solution)/shard_map/pallas_call | solution.py:171
  629.4 23.8 %reduce-scatter.16.cloned.1.call-done.grad_ref = bf16[256,512]{1,0:T(8,128)(2,1)} async-done(((bf16[2048,512]{1,0:T(8,128)(2,1)}), bf16[256,512]{1,0:T(8,128)(2,1)}) %reduce-scatter.16.cloned.1.call-update) | async-done | bytes 262160 | tf_op jit(solution)/shard_map/reduce_scatter | solution.py:996
  655.1 2.2 copy-done.4
  657.3 34.9 %shard_map.376 = bf16[1024,512]{1,0:T(8,128)(2,1)S(1)} custom-call(bf16[4,1024,512]{2,1,0:T(8,128)(2,1)S(1)} %copy-done.4), custom_call_target="tpu_custom_call" | custom-call | bytes 134217728 | tf_op jit(solution)/shard_map/pallas_call | solution.py:421
  698.5 8.1 shard_map.379
  706.7 5.2 fusion
  715.4 39.2 %reduce-scatter.18.cloned.1.call-done.refs_2_ = bf16[1024,256]{1,0:T(8,128)(2,1)} async-done(((bf16[8192,256]{1,0:T(8,128)(2,1)}), bf16[1024,256]{1,0:T(8,128)(2,1)}) %reduce-scatter.18.cloned.1.call-update) | async-done | bytes 524304 | tf_op jit(solution)/shard_map/reduce_scatter | solution.py:998
  754.6 2.2 copy-done.10
  762.2 4.0 shard_map.380
  766.2 6.3 convolution_convert_fusion
  773.5 3.4 copy-done.1
  776.9 2.2 copy-done.46
  779.1 8.5 shard_map.381
  789.8 2.2 copy-done.12
  792.1 40.2 %shard_map.382 = (bf16[1024,512]{1,0:T(8,128)(2,1)S(1)}, f32[8,128]{1,0:T(8,128)S(1)}, f32[40,128]{1,0:T(8,128)S(1)}) custom-call(bf16[4,1024,512]{2,1,0:T(8,128)(2,1)S(1)} %copy-done.12, f32[8,128]{1,0:T(8,128)S(1)} %bitcast.82, f32[40,128]{1,0:T(8,128)S(1)} %pad_bitcast_fusion.gains_ref), custom_call_target="tpu_custom_call" | custom-call | bytes 134217728 | tf_op jit(solution)/shard_map/pallas_call | solution.py:508
  834.7 4.0 multiply_add_fusion
  838.7 3.9 fusion.10
  (205 shorter events, 69.8 us)
Async XLA Ops:
  7.2 52.9 %all-gather.10.cloned.1.call-start = ((), (), s32[]{:S(2)}) async-start(), calls=%async_computation.7 | async-start | bytes 4718592 | tf_op jit(solution)/shard_map/all_gather | solution.py:889
  9.4 112.3 %all-gather.12.cloned.1.call-start = ((), (), s32[]{:S(2)}) async-start(), calls=%async_computation.8 | async-start | bytes 4718592 | tf_op jit(solution)/shard_map/all_gather | solution.py:924
  11.9 160.2 %copy-start.43 = (s32[1024]{0:T(1024)}, s32[1024]{0:T(1024)S(1)}, u32[]{:S(2)}) copy-start(s32[1024]{0:T(1024)S(1)} %select_reduce_fusion) | copy-start | bytes 12292
  13.8 4.8 copy-start.61
  14.1 45.9 %copy-start.18 = (f32[1024,128]{1,0:T(8,128)}, f32[1024,128]{1,0:T(8,128)S(1)}, u32[]{:S(2)}) copy-start(f32[1024,128]{1,0:T(8,128)S(1)} %get-tuple-element.237.cos_ref) | copy-start | bytes 1572868
  14.2 45.9 %copy-start.20 = (f32[1024,128]{1,0:T(8,128)}, f32[1024,128]{1,0:T(8,128)S(1)}, u32[]{:S(2)}) copy-start(f32[1024,128]{1,0:T(8,128)S(1)} %get-tuple-element.238.sin_ref) | copy-start | bytes 1572868
  14.2 6.3 copy-start
  18.6 7.5 copy-start.63
  18.6 7.5 copy-start.41
  60.1 2.2 copy-start.14
  75.6 50.7 %copy-start.7 = (f32[2,256,1536]{2,1,0:T(8,128)S(1)}, f32[2,256,1536]{2,1,0:T(8,128)}, u32[]{:S(2)}) copy-start(f32[2,256,1536]{2,1,0:T(8,128)} %refs_3_.1) | copy-start | bytes 9437188
  75.6 94.1 %all-gather.14.cloned.1.call-start = ((), (), s32[]{:S(2)}) async-start(), calls=%async_computation.9 | async-start | bytes 4718592 | tf_op jit(solution)/shard_map/all_gather | solution.py:924
  121.6 133.6 %all-gather.16.cloned.1.call-start = ((), (), s32[]{:S(2)}) async-start(), calls=%async_computation.17 | async-start | bytes 9437184 | tf_op jit(solution)/shard_map/all_gather | solution.py:934
  134.1 4.4 copy-start.60
  134.1 38.0 %copy-start.44 = (s32[3,2]{1,0:T(4,128)}, s32[3,2]{1,0:T(4,128)S(1)}, u32[]{:S(2)}) copy-start(s32[3,2]{1,0:T(4,128)S(1)} %pad_add_fusion.bound_ref) | copy-start | bytes 76
  139.5 2.2 copy-start.47
  169.7 171.8 %all-gather.18.cloned.1.call-start = ((), (), s32[]{:S(2)}) async-start(), calls=%async_computation.18 | async-start | bytes 7077888 | tf_op jit(solution)/shard_map/all_gather | solution.py:934
  172.1 2.2 copy-start.48
  175.3 6.3 copy-start.38
  255.3 149.2 %all-gather.20.cloned.1.call-start = ((), (), s32[]{:S(2)}) async-start(), calls=%async_computation.19 | async-start | bytes 7077888 | tf_op jit(solution)/shard_map/all_gather | solution.py:934
  341.5 144.3 %reduce-scatter.8.cloned.1.call-start = ((), (), s32[]{:S(2)}) async-start(), calls=%async_computation.10 | async-start | bytes 7077888 | tf_op jit(solution)/shard_map/reduce_scatter | solution.py:965
  341.6 2.2 copy-start.3
  380.3 196.8 %reduce-scatter.10.cloned.1.call-start = ((), (), s32[]{:S(2)}) async-start(), calls=%async_computation.11 | async-start | bytes 7077888 | tf_op jit(solution)/shard_map/reduce_scatter | solution.py:965
  427.6 188.7 %reduce-scatter.14.cloned.1.call-start = ((), (), s32[]{:S(2)}) async-start(), calls=%async_computation.13 | async-start | bytes 7077888 | tf_op jit(solution)/shard_map/reduce_scatter | solution.py:965
  451.0 202.2 %reduce-scatter.16.cloned.1.call-start = ((), (), s32[]{:S(2)}) async-start(), calls=%async_computation.14 | async-start | bytes 2359296 | tf_op jit(solution)/shard_map/reduce_scatter | solution.py:996
  488.0 71.7 %copy-start.6 = (bf16[1024,2048]{1,0:T(8,128)(2,1)S(1)}, bf16[1024,2048]{1,0:T(8,128)(2,1)}, u32[]{:S(2)}) copy-start(bf16[1024,2048]{1,0:T(8,128)(2,1)} %cot_ref.7) | copy-start | bytes 12582916
  488.0 71.7 %copy-start.34 = (f32[1024,1]{1,0:T(8,128)S(1)}, f32[1024,1]{1,0:T(8,128)}, u32[]{:S(2)}) copy-start(f32[1024,1]{1,0:T(8,128)} %copy-done.33) | copy-start | bytes 12292
  559.8 10.2 %copy-start.59 = (bf16[8,1,256,512]{3,2,1,0:T(8,128)(2,1)S(1)}, bf16[8,1,256,512]{3,2,1,0:T(8,128)(2,1)}, u32[]{:S(2)}) copy-start(bf16[8,1,256,512]{3,2,1,0:T(8,128)(2,1)} %slice.93) | copy-start | bytes 6291460
  570.0 3.4 copy-start.58
  577.1 138.3 %reduce-scatter.12.cloned.1.call-start = ((), (), s32[]{:S(2)}) async-start(), calls=%async_computation.12 | async-start | bytes 4718592 | tf_op jit(solution)/shard_map/reduce_scatter | solution.py:998
  590.5 164.1 %reduce-scatter.18.cloned.1.call-start = ((), (), s32[]{:S(2)}) async-start(), calls=%async_computation.15 | async-start | bytes 4718592 | tf_op jit(solution)/shard_map/reduce_scatter | solution.py:998
  629.4 24.2 %copy-start.67 = (s32[1024]{0:T(1024)S(1)}, s32[1024]{0:T(1024)}, u32[]{:S(2)}) copy-start(s32[1024]{0:T(1024)} %param.22) | copy-start | bytes 12292
  653.2 185.5 %reduce-scatter.20.cloned.1.call-start = ((), (), s32[]{:S(2)}) async-start(), calls=%async_computation.16 | async-start | bytes 4718592 | tf_op jit(solution)/shard_map/reduce_scatter | solution.py:1024
  657.3 34.9 %copy-start.8 = (f32[1536,256]{1,0:T(8,128)S(1)}, f32[1536,256]{1,0:T(8,128)}, u32[]{:S(2)}) copy-start(f32[1536,256]{1,0:T(8,128)} %refs_6_.1) | copy-start | bytes 4718596
  657.3 34.9 %copy-start.16 = (f32[2,256,1536]{2,1,0:T(8,128)S(1)}, f32[2,256,1536]{2,1,0:T(8,128)}, u32[]{:S(2)}) copy-start(f32[2,256,1536]{2,1,0:T(8,128)} %refs_4_.1) | copy-start | bytes 9437188
  706.6 7.3 copy-start.17
  706.6 7.3 copy-start.29
  706.6 7.3 copy-start.30
  706.6 7.3 copy-start.40
  706.6 47.9 %copy-start.25 = (f32[1024,256]{1,0:T(8,128)S(1)}, f32[1024,256]{1,0:T(8,128)}, u32[]{:S(2)}) copy-start(f32[1024,256]{1,0:T(8,128)} %get-tuple-element.183.refs_0_) | copy-start | bytes 3145732
  762.2 4.0 copy-start.15
  773.4 3.5 copy-start.1
  776.9 2.2 copy-start.46
  789.5 44.5 %copy-start.62 = (f32[4352]{0:T(1024)S(1)}, f32[4352]{0:T(1024)}, u32[]{:S(2)}) copy-start(f32[4352]{0:T(1024)} %param.27) | copy-start | bytes 52228
  789.5 44.5 %copy-start.65 = (f32[4352]{0:T(1024)S(1)}, f32[4352]{0:T(1024)}, u32[]{:S(2)}) copy-start(f32[4352]{0:T(1024)} %param.37) | copy-start | bytes 52228
  789.5 44.5 %copy-start.66 = (f32[4352]{0:T(1024)S(1)}, f32[4352]{0:T(1024)}, u32[]{:S(2)}) copy-start(f32[4352]{0:T(1024)} %param.32) | copy-start | bytes 52228
  789.8 2.2 copy-start.12
  832.3 6.4 copy-start.57
  (33 other events, 42.8 us)
Sparse Core Ops, SparseCore 0:
  10.2 49.8 all-gather.9
  75.7 45.8 all-gather.11
  123.8 45.8 all-gather.13
  171.7 83.4 all-gather.15
  257.3 63.2 all-gather.17
  341.6 62.8 all-gather.19
  406.8 68.4 reduce-scatter.7
  477.6 68.1 reduce-scatter.9
  548.1 68.1 reduce-scatter.13
  619.0 34.1 reduce-scatter.15
  655.5 48.7 reduce-scatter.11
  706.4 48.1 reduce-scatter.17
  772.6 50.7 reduce-scatter.19

commit v3 on v2

--- a/solution.py
+++ b/solution.py
@@ -66,7 +66,7 @@
     out_ref[:, head_dim:] = out[rows:].astype(out_ref.dtype)
     total_ref[0] = top + jnp.log2(total)
 
-def attend(bounds, queries, begins, kv_all, head_dim, query_rows, key_rows):
+def attend(bounds, queries, begins, kv_all, group, head_dim, query_rows, key_rows):
     rows = queries.shape[0]
     blocks = rows // query_rows
     return pl.pallas_call(
@@ -78,7 +78,7 @@
             in_specs=[
                 pl.BlockSpec((query_rows, 2 * head_dim), lambda i, *_: (i, 0)),
                 pl.BlockSpec((1, 1, query_rows), lambda i, *_: (i, 0, 0)),
-                pl.BlockSpec(kv_all.shape, lambda i, *_: (0, 0)),
+                pl.BlockSpec((kv_all.shape[0], 2 * head_dim), lambda i, *_: (0, group)),
             ],
             out_specs=[
                 pl.BlockSpec((query_rows, 2 * head_dim), lambda i, *_: (i, 0)),
@@ -163,24 +163,25 @@
     def _():
         grad_kv_ref[...] = kv_sum[...].astype(grad_kv_ref.dtype)
 
-def attend_back(bounds, queries, grads, outs, totals, begin_rows, kv_all, head_dim, query_rows, key_rows):
+def attend_back(bounds, queries, grads, outs, totals, begin_rows, kv_all, group, head_dim, query_rows, key_rows):
     rows = queries.shape[0]
     blocks = rows // query_rows
     wide = pl.BlockSpec((query_rows, 2 * head_dim), lambda i, *_: (i, 0))
-    whole = pl.BlockSpec(kv_all.shape, lambda i, *_: (0, 0))
+    kv_shape = (kv_all.shape[0], 2 * head_dim)
+    whole = pl.BlockSpec(kv_shape, lambda i, *_: (0, 0))
     return pl.pallas_call(
         functools.partial(attend_back_kernel, head_dim, key_rows),
-        out_shape=(jax.ShapeDtypeStruct(queries.shape, jnp.float32), jax.ShapeDtypeStruct(kv_all.shape, jnp.bfloat16)),
+        out_shape=(jax.ShapeDtypeStruct(queries.shape, jnp.float32), jax.ShapeDtypeStruct(kv_shape, jnp.bfloat16)),
         grid_spec=pltpu.PrefetchScalarGridSpec(
             num_scalar_prefetch=1,
             grid=(blocks,),
             in_specs=[wide, wide, wide,
                 pl.BlockSpec((1, 1, 2 * query_rows), lambda i, *_: (i, 0, 0)),
                 pl.BlockSpec((1, 1, query_rows), lambda i, *_: (i, 0, 0)),
-                whole],
+                pl.BlockSpec(kv_shape, lambda i, *_: (0, group))],
             out_specs=[wide, whole],
             scratch_shapes=[pltpu.VMEM((2 * query_rows, head_dim), jnp.bfloat16)] * 2
-            + [pltpu.VMEM((2 * query_rows, head_dim), jnp.float32), pltpu.VMEM(kv_all.shape, jnp.float32)],
+            + [pltpu.VMEM((2 * query_rows, head_dim), jnp.float32), pltpu.VMEM(kv_shape, jnp.float32)],
         ),
         compiler_params=pltpu.CompilerParams(vmem_limit_bytes=56 * MIB),
         cost_estimate=pl.CostEstimate(flops=20 * rows * kv_all.shape[0] * head_dim, bytes_accessed=2 * kv_all.size, transcendentals=2 * rows * kv_all.shape[0]),
@@ -196,7 +197,7 @@
 LR_MATRIX = 0.08
 LR_GAIN = 0.5
 FF_BLOCK = 256
-CHUNKS = 3
+CHUNK_ENDS = (0, 1, 3)
 
 
 def mlp_kernel(normed_ref, cot_ref, normed_t_ref, cot_t_ref, weight_ref, hidden_ref, gate_grad_ref, up_grad_ref, grads_ref, wide):
@@ -553,13 +554,13 @@
                 scale = lax.rsqrt(jnp.mean(raw * raw, axis=1, keepdims=True) + EPSILON)
                 raw = raw * scale * gain
                 raw = raw * cosine + turned_by(raw, sine)
-            out = outs[group] if at < 2 else outs[groups + group]
-            out[:, at % 2 * head_dim : (at % 2 + 1) * head_dim] = raw.astype(out.dtype)
-
-
-def front(normed, weight, cosine, sine, gains, head_dim):
+            out = outs[group] if at < 2 else outs[groups]
+            place = at % 2 * head_dim + (0 if at < 2 else group * 2 * head_dim)
+            out[:, place : place + head_dim] = raw.astype(out.dtype)
+
+
+def front(normed, weight, width, cosine, sine, gains, head_dim):
     rows, depth = normed.shape
-    width = weight.shape[1]
     groups = width // (4 * head_dim)
     block = min(256, rows)
     narrow = pl.BlockSpec((block, 2 * head_dim), lambda i: (i, 0))
@@ -569,18 +570,21 @@
         grid=(rows // block,),
         in_specs=[
             pl.BlockSpec((block, depth), lambda i: (i, 0)),
-            pl.BlockSpec(weight.shape, lambda i: (0, 0), pipeline_mode=pl.Buffered(1)),
+            pl.BlockSpec((depth, width), lambda i: (0, 0), pipeline_mode=pl.Buffered(1)),
             table,
             table,
             pl.BlockSpec(gains.shape, lambda i: (0, 0)),
         ],
-        out_specs=[pl.BlockSpec((block, width), lambda i: (i, 0))] + [narrow] * (2 * groups),
+        out_specs=[pl.BlockSpec((block, width), lambda i: (i, 0))]
+        + [narrow] * groups
+        + [pl.BlockSpec((block, groups * 2 * head_dim), lambda i: (i, 0))],
         out_shape=[jax.ShapeDtypeStruct((rows, width), jnp.float32)]
-        + [jax.ShapeDtypeStruct((rows, 2 * head_dim), jnp.bfloat16)] * (2 * groups),
+        + [jax.ShapeDtypeStruct((rows, 2 * head_dim), jnp.bfloat16)] * groups
+        + [jax.ShapeDtypeStruct((rows, groups * 2 * head_dim), jnp.bfloat16)],
         compiler_params=pltpu.CompilerParams(vmem_limit_bytes=32 * MIB),
         cost_estimate=pl.CostEstimate(flops=4 * rows * depth * width, bytes_accessed=2 * depth * width, transcendentals=0),
     )(normed, weight, cosine, sine, gains)
-    return found[0], found[1 : 1 + groups], found[1 + groups :]
+    return found[0], found[1 : 1 + groups], found[1 + groups]
 
 
 def front_back_kernel(groups, head_dim, raw_ref, cos_ref, sin_ref, gains_ref, *refs):
@@ -772,35 +776,43 @@
         out[...] = value.astype(out.dtype)
 
 
-def mlp_step_kernel(rate, chunks, *refs):
+def mlp_step_kernel(rate, steps_of, *refs):
+    chunks = len(steps_of)
     grads, held, outs = refs[:chunks], refs[chunks : chunks + 6], refs[chunks + 6 :]
-    for chunk in range(chunks):
-
-        @pl.when(pl.program_id(0) == chunk)
+    begin = 0
+    for chunk, steps in enumerate(steps_of):
+
+        @pl.when((pl.program_id(0) >= begin) & (pl.program_id(0) < begin + steps))
         def _():
             both = grads[chunk][:2].astype(jnp.float32)
             step_of(rate, *(ref[...] for ref in held[:3]), both, outs[:4])
             down = jnp.transpose(grads[chunk][2].astype(jnp.float32))
             step_of(rate, *(ref[...] for ref in held[3:]), down, outs[4:])
 
+        begin += steps
+
 
 def mlp_step(rate, grads, gate_up, down):
-    chunks = len(grads)
-    kinds, depth, width = grads[0].shape
-    gate_up_spec = pl.BlockSpec((2, depth, width), lambda i: (0, 0, i))
-    down_spec = pl.BlockSpec((width, depth), lambda i: (i, 0))
+    kinds, depth, _ = grads[0].shape
+    block = min(FF_BLOCK, grads[0].shape[2])
+    steps_of = [grad.shape[2] // block for grad in grads]
+
+    def grad_spec(chunk):
+        begin, last = sum(steps_of[:chunk]), steps_of[chunk] - 1
+        return pl.BlockSpec((kinds, depth, block), lambda i: (0, 0, jnp.clip(i - begin, 0, last)))
+
+    gate_up_spec = pl.BlockSpec((2, depth, block), lambda i: (0, 0, i))
+    down_spec = pl.BlockSpec((block, depth), lambda i: (i, 0))
     types = (jnp.float32,) * 3 + (jnp.bfloat16,)
     return pl.pallas_call(
-        functools.partial(mlp_step_kernel, rate, chunks),
-        grid=(chunks,),
-        in_specs=[pl.BlockSpec((kinds, depth, width), lambda i: (0, 0, 0), pipeline_mode=pl.Buffered(1))] * chunks
-        + [gate_up_spec] * 3
-        + [down_spec] * 3,
+        functools.partial(mlp_step_kernel, rate, steps_of),
+        grid=(sum(steps_of),),
+        in_specs=[grad_spec(chunk) for chunk in range(len(grads))] + [gate_up_spec] * 3 + [down_spec] * 3,
         out_specs=[gate_up_spec] * 4 + [down_spec] * 4,
         out_shape=[jax.ShapeDtypeStruct(gate_up[0].shape, kind) for kind in types]
         + [jax.ShapeDtypeStruct(down[0].shape, kind) for kind in types],
         compiler_params=pltpu.CompilerParams(vmem_limit_bytes=40 * MIB),
-        cost_estimate=pl.CostEstimate(flops=0, bytes_accessed=26 * chunks * kinds * depth * width, transcendentals=0),
+        cost_estimate=pl.CostEstimate(flops=0, bytes_accessed=26 * sum(grad.size for grad in grads), transcendentals=0),
     )(*grads, *gate_up, *down)
 
 
@@ -818,6 +830,28 @@
         compiler_params=pltpu.CompilerParams(vmem_limit_bytes=24 * MIB),
         cost_estimate=pl.CostEstimate(flops=0, bytes_accessed=28 * grad_t.size, transcendentals=0),
     )(grad_t, *held)
+
+
+def out_product_kernel(left_ref, weight_ref, out_ref):
+    out_ref[0] = matmul(left_ref[...], weight_ref[...], NT).astype(out_ref.dtype)
+
+
+def out_product(left, weight, column, pieces):
+    rows, width = left.shape
+    depth = weight.shape[0]
+    block = depth // pieces // 2
+    return pl.pallas_call(
+        out_product_kernel,
+        grid=(depth // block,),
+        in_specs=[
+            pl.BlockSpec((rows, width), lambda i: (0, 0), pipeline_mode=pl.Buffered(1)),
+            pl.BlockSpec((block, width), lambda i: (i, column)),
+        ],
+        out_specs=pl.BlockSpec((1, rows, block), lambda i: (i // 2, 0, i % 2)),
+        out_shape=jax.ShapeDtypeStruct((pieces, rows, depth // pieces), jnp.bfloat16),
+        compiler_params=pltpu.CompilerParams(vmem_limit_bytes=32 * MIB),
+        cost_estimate=pl.CostEstimate(flops=2 * rows * depth * width, bytes_accessed=2 * depth * width, transcendentals=0),
+    )(left, weight)
 
 
 def rms_scale(values_in):
@@ -879,14 +913,15 @@
     col_begin = tensor_at * width_cols
     groups = w_qkv.shape[1] // (4 * head_dim)
     ff_local = w_down.shape[0]
-    ff_chunk = ff_local // CHUNKS
+    ff_unit = ff_local // CHUNK_ENDS[-1]
     bf16 = jnp.bfloat16
     f32 = jnp.float32
 
     def columns_of(values_in):
         return lax.dynamic_slice_in_dim(values_in, col_begin, width_cols, values_in.ndim - 1)
 
-    qkv_full = lax.all_gather(w_qkv.astype(bf16), "dp", axis=0, tiled=True)
+    qkv_cols, out_rows = w_qkv.shape[1], w_out.shape[0]
+    qkv_out = lax.all_gather(jnp.concatenate([w_qkv, w_out.T], axis=1).astype(bf16), "dp", axis=0, tiled=True)
 
     ends_at = jnp.cumsum(doc_lengths)
     starts_at = ends_at - doc_lengths
@@ -915,50 +950,40 @@
     normal_one = hidden_in * scale_one
     normed_one_b = (normal_one * gain_attn).astype(bf16)
     gains_two = jnp.stack([gain_query, gain_key])
-    projected, queries, kv_local = front(normed_one_b, qkv_full, cosine, sine, gains_two, head_dim)
-    kv_every = []
-    for group in range(groups):
-        value = kv_local[group]
-        if group:
-            value, kv_every[-1] = tie(value, kv_every[-1])
-        kv_every.append(lax.all_gather(value, "dp", axis=0, tiled=True))
+    projected, queries, kv_local = front(
+        normed_one_b, qkv_out, qkv_cols, cosine, sine, gains_two, head_dim
+    )
+    kv_every = lax.all_gather(kv_local, "dp", axis=0, tiled=True)
 
     down_t = w_down.T
 
     def chunk_shard(chunk):
-        units = slice(chunk * ff_chunk, (chunk + 1) * ff_chunk)
-        kinds = [w_gate_up[0, :, units], w_gate_up[1, :, units], down_t[:, units]]
-        return jnp.stack(kinds + ([w_out.T] if chunk == 0 else [])).astype(bf16)
+        units = slice(CHUNK_ENDS[chunk] * ff_unit, CHUNK_ENDS[chunk + 1] * ff_unit)
+        return jnp.stack([w_gate_up[0, :, units], w_gate_up[1, :, units], down_t[:, units]]).astype(bf16)
 
     def chunk_gather(shard):
         return lax.all_gather(shard, "dp", axis=0)
 
-    mixed, totals, chunk_weights = [], [], []
+    shard, kv_every, cotangent_t = tie(chunk_shard(0), kv_every, cotangent.T)
+    chunk_weights = [chunk_gather(shard)]
+    mixed, totals = [], []
     for group in range(groups):
         mixed_rows, total_rows = attend(
-            bounds, queries[group], begin_rows, kv_every[group], head_dim, query_rows, min(1024, tokens_all)
+            bounds, queries[group], begin_rows, kv_every, group, head_dim, query_rows, min(1024, tokens_all)
         )
-        if group == 0:
-            shard, kv_every[-1], mixed_rows, cotangent_t = tie(
-                chunk_shard(0), kv_every[-1], mixed_rows, cotangent.T
-            )
-            chunk_weights.append(chunk_gather(shard))
         mixed.append(mixed_rows)
         totals.append(total_rows)
     mixed_b = jnp.concatenate(mixed, axis=1)
-    shard, chunk_weights[0], mixed_b = tie(chunk_shard(1), chunk_weights[0], mixed_b)
+    attn_part = out_product(mixed_b, qkv_out, qkv_cols // out_rows, tensor_ways)
+    shard, chunk_weights[0], attn_part = tie(chunk_shard(1), chunk_weights[0], attn_part)
     chunk_weights.append(chunk_gather(shard))
-    out_full_t = chunk_weights[0][:, 3].reshape(model_dim, w_out.shape[0])
-    attn_part = back_product([(mixed_b,)], chunk_weights[:1], 3, tensor_ways)
     attn_sum = tensor_sum(attn_part, 0)
-    shard, chunk_weights[1], attn_sum = tie(chunk_shard(2), chunk_weights[1], attn_sum)
-    chunk_weights.append(chunk_gather(shard))
     resid_one, normed_two_b, normed_two_t, scale_two = add_and_norm(attn_sum, hidden_in, gain_mlp[None])
 
     weight_grads, hiddens, back_pairs = [], [], []
-    for chunk in range(CHUNKS):
+    for weights in chunk_weights:
         hidden_b, gate_grad, up_grad, weight_grad = mlp_chunk(
-            normed_two_b, cotangent, normed_two_t, cotangent_t, chunk_weights[chunk]
+            normed_two_b, cotangent, normed_two_t, cotangent_t, weights
         )
         hiddens.append((hidden_b,))
         back_pairs.append((gate_grad, up_grad))
@@ -966,18 +991,48 @@
 
     part_two = back_product(back_pairs, chunk_weights, 0, tensor_ways)
     mlp_part = back_product(hiddens, chunk_weights, 2, tensor_ways)
-    part_two, mlp_part, weight_grads[0] = tie(part_two, mlp_part, weight_grads[0])
-    part_two_sum = tensor_sum(part_two, 1)
+    part_two, mlp_part = tie(part_two, mlp_part)
+    part_two_sum, weight_grads[0] = tie(tensor_sum(part_two, 1), weight_grads[0])
     grad_resid, grad_attn_b, gain_mlp_part = norm_and_add_back(
         part_two_sum, cotangent, resid_one, scale_two, gain_mlp[None]
     )
-    grad_mixed_b = dot(grad_attn_b, out_full_t, NN).astype(bf16)
+    grad_mixed_b = dot(grad_attn_b, qkv_out[:, qkv_cols:], NN).astype(bf16)
 
     grad_out_t = dot(grad_attn_b, mixed_b, TN).astype(bf16)
+    lines = data_ways // 2
+    line_at, lane = lax.axis_index("dp") // 2, lax.axis_index("dp") % 2
+    out_pieces = grad_out_t.reshape(lines, 2, model_dim // data_ways, out_rows)
+
+    def chip_piece(step, of_lane):
+        return lax.dynamic_slice(
+            out_pieces, ((line_at + lines - step) % lines, of_lane, 0, 0), (1, 1, *out_pieces.shape[2:])
+        )[0, 0]
+
+    far_pieces = lax.ppermute(
+        jnp.stack([chip_piece(step, 1 - lane) for step in range(lines)]),
+        "dp",
+        [(at, at + 1 - 2 * (at % 2)) for at in range(data_ways)],
+    )
+
+    def chip_sum(step, *others):
+        return sum(value.astype(f32) for value in (chip_piece(step, lane), far_pieces[step], *others))
+
+    def hop(step, *others):
+        return lax.ppermute(
+            chip_sum(step, *others).astype(bf16), "dp", [(at, (at + 2) % data_ways) for at in range(data_ways)]
+        )
+
+    out_grad = hop(1)
     grad_queries, kv_sums = [], []
     for group in range(groups):
         grad_rows = grad_mixed_b[:, group * 2 * head_dim : (group + 1) * 2 * head_dim]
-        grad_rows, weight_grads[group + 1] = tie(grad_rows, weight_grads[group + 1])
+        if group and group == groups - 1:
+            grad_rows, weight_grads[1], out_grad, kv_sums[-1] = tie(
+                grad_rows, weight_grads[1], out_grad, kv_sums[-1]
+            )
+        if group == groups - 1:
+            for step in range(2, lines - 1):
+                out_grad = hop(step, out_grad)
         grad_query, kv_sum = attend_back(
             bounds,
             queries[group],
@@ -985,17 +1040,23 @@
             mixed[group],
             totals[group],
             begin_rows,
-            kv_every[group],
+            kv_every,
+            group,
             head_dim,
             query_rows,
             min(512, tokens_all),
         )
         grad_queries.append(grad_query)
         kv_sums.append(kv_sum)
-    grad_out_t, weight_grads[groups] = tie(grad_out_t, weight_grads[groups])
-    out_grad = lax.psum_scatter(grad_out_t, "dp", scatter_dimension=0, tiled=True)
-    kv_sums[0], out_grad = tie(kv_sums[0], out_grad)
-    kv_grads = [lax.psum_scatter(kv_sum, "dp", scatter_dimension=0, tiled=True) for kv_sum in kv_sums]
+    out_grad, kv_sums[-1] = tie(out_grad, kv_sums[-1])
+    if lines > 2:
+        out_grad = hop(lines - 1, out_grad)
+    out_grad = chip_sum(0, out_grad).astype(bf16)
+    kv_grads = []
+    for group in range(groups):
+        if group:
+            kv_grads[-1], kv_sums[group] = tie(kv_grads[-1], kv_sums[group])
+        kv_grads.append(lax.psum_scatter(kv_sums[group], "dp", scatter_dimension=0, tiled=True))
     mlp_part, grad_queries[-1] = tie(mlp_part, grad_queries[-1])
     rate_matrix = LR_MATRIX / math.sqrt(tokens_all)
     mlp_sum = tensor_sum(mlp_part, 2, False)
@@ -1023,7 +1084,7 @@
     grad_qkv = dot(normed_one_b, grad_projected_b, TN).astype(bf16)
     qkv_shard = lax.psum_scatter(grad_qkv, "dp", scatter_dimension=0, tiled=True).astype(f32)
     part_one, dots_part, gain_attn_part = last_product(
-        grad_projected_b, qkv_full, hidden_in, scale_one, gain_attn[None], tensor_ways
+        grad_projected_b, qkv_out, hidden_in, scale_one, gain_attn[None], tensor_ways
     )
 
     gains_part = jnp.concatenate(

time: 859 us -> 827 us (0.963)
  waiting for transfers between devices: 286 us -> 263 us
  local copies, waits for them, and re-layouts: 82.2 us -> 72 us
    all_gather x3 -> x2, waiting for transfers between devices: 96.3 us -> 53.8 us  [chunk_gather(): return lax.all_gather(shard, 'dp', axis=0)]
    ppermute x0 -> x4, waiting for transfers between devices: none -> 17.4 us  [the longest x3 17.4 us: hop(): lax.ppermute(chip_sum(step, *others).astype(bf16), 'dp', [(at, (at + 2) %...]
    all_gather x3 -> x2, waiting for transfers between devices: 101 us -> 117 us  [the longest x1 66.4 us: local(): kv_every = lax.all_gather(kv_local, 'dp', axis=0, tiled=True)]
    reduce_scatter x3 -> x2, waiting for transfers between devices: 25.8 us -> 15.3 us  [local(): lax.psum_scatter(weight_grad, 'dp', scatter_dimension=0)]
    pallas_call x3 -> x2, Pallas kernels: 69.7 us -> 61.3 us  [mlp_chunk(): pl.pallas_call(mlp_kernel, grid=(width // block,), in_specs=[held(normed)...]
    pallas_call x3 -> x2, Pallas kernels: 39.8 us -> 31.6 us  [back_product(): pl.pallas_call(functools.partial(back_product_kernel, kinds), grid=(ways,...]
    unnamed x143 -> x146, local copies, waits for them, and re-layouts: 71.5 us -> 66.4 us
    reduce_scatter x3 -> x2, waiting for transfers between devices: 63 us -> 59.1 us  [local(): lax.psum_scatter(kv_sums[group], 'dp', scatter_dimension=0, tiled=True)]
  transfers between devices with their start and end apart: 13 -> 13, of which waited for: 8 -> 9; matrix products, arithmetic and copies ran while one was open for 7% -> 8% of each run, Pallas kernels for 47% -> 48%
where the time goes in v3:
time: 827 us; the launch traced here: 819 us
  Pallas kernels  406 us (49%)
  waiting for transfers between devices  263 us (32%)
  local copies, waits for them, and re-layouts  72 us (9%)
  other arithmetic  45.3 us (5%)
  between operations  16.5 us (2%)
  matrix products  13.9 us (2%)
    pallas_call x3, Pallas kernels, tensor_sum(): pl.pallas_call(functools.partial(tensor_sum_kernel, bits, whole), out_sha...  178 us
    all_gather x1, waiting for transfers between devices, local(): kv_every = lax.all_gather(kv_local, 'dp', axis=0, tiled=True)  66.4 us
    unnamed x146, local copies, waits for them, and re-layouts  66.4 us
    pallas_call x2, Pallas kernels, mlp_chunk(): pl.pallas_call(mlp_kernel, grid=(width // block,), in_specs=[held(normed)...  61.3 us
    reduce_scatter x2, waiting for transfers between devices, local(): lax.psum_scatter(kv_sums[group], 'dp', scatter_dimension=0, tiled=True)  59.1 us
    all_gather x2, waiting for transfers between devices, chunk_gather(): return lax.all_gather(shard, 'dp', axis=0)  53.8 us
    all_gather x1, waiting for transfers between devices, local(): lax.all_gather(jnp.concatenate([w_qkv, w_out.T], axis=1).astype(bf16), 'd...  51 us
    pallas_call x1, Pallas kernels, last_sum(): pl.pallas_call(functools.partial(last_sum_kernel, bits, data_ways), out_s...  40.3 us
  transfers between devices with their start and end apart: 13, of which 9 were waited for; matrix products, arithmetic and copies ran while one was open for 8% of the time, Pallas kernels for 48%

profile of v3, /device:TPU:0, one launch (start us, length us, event | category | flops | bytes accessed | tf_op | source)
XLA Modules:
  0.0 819.1 jit_solution(4496312007238927797)
XLA Ops:
  13.5 4.4 multiply_reduce_fusion
  17.9 9.4 %multiply_convert_fusion = (bf16[1024,2048]{1,0:T(8,128)(2,1)}, f32[1024,2048]{1,0:T(8,128)}) fusion(f32[2048]{0:T(1024)S(1)} %get-tuple-element.210, f32[1024,2048]{1,0:T(8,128)} %hidden_ref.3, f32[1024]{0:T(1024)S(1)} %add_rsqrt_fusion), kind=kLoop, calls=%fused_computation | loop fusion | flops 6291456 | bytes 20983808 | tf_op jit(solution)/shard_map/convert_element_type | solution.py:951
  27.3 51.0 %all-gather.7.cloned.1.call-done.weight_ref = bf16[2048,1536]{1,0:T(8,128)(2,1)} async-done(((bf16[256,1536]{1,0:T(8,128)(2,1)}), bf16[2048,1536]{1,0:T(8,128)(2,1)}) %all-gather.7.cloned.1.call-update) | async-done | bytes 6291472 | tf_op jit(solution)/shard_map/all_gather | solution.py:924
  78.3 2.8 copy-done.9
  81.1 2.2 copy-done.17
  83.3 6.2 shard_map.362
  94.1 2.7 copy.55
  99.0 6.5 copy.57
  108.5 66.4 %all-gather.9.cloned.1.call-done.kv_ref = bf16[8192,512]{1,0:T(8,128)(2,1)} async-done(((bf16[1024,512]{1,0:T(8,128)(2,1)}), bf16[8192,512]{1,0:T(8,128)(2,1)}) %all-gather.9.cloned.1.call-update) | async-done | bytes 8388624 | tf_op jit(solution)/shard_map/all_gather | solution.py:956
  179.2 7.1 shard_map.363
  187.8 7.5 shard_map.364
  196.1 4.4 shard_map.365.part_ref
  203.6 36.9 %all-gather.11.cloned.1.call-done = bf16[24,256,512]{2,1,0:T(8,128)(2,1)} async-done(((bf16[3,256,512]{2,1,0:T(8,128)(2,1)}), bf16[24,256,512]{2,1,0:T(8,128)(2,1)}) %all-gather.11.cloned.1.call-update) | async-done | bytes 6291472 | tf_op jit(solution)/shard_map/all_gather | solution.py:965
  243.3 71.6 %shard_map.366.sum_ref = bf16[4,1024,512]{2,1,0:T(8,128)(2,1)S(1)} custom-call(bf16[4,1024,512]{2,1,0:T(8,128)(2,1)S(1)} %copy-done.5), custom_call_target="tpu_custom_call" | custom-call | bytes 268435456 | tf_op jit(solution)/shard_map/pallas_call | solution.py:422
  314.9 9.7 %shard_map.367 = (f32[1024,2048]{1,0:T(8,128)}, bf16[1024,2048]{1,0:T(8,128)(2,1)S(1)}, bf16[2048,1024]{1,0:T(8,128)(2,1)S(1)}, f32[1024,1]{1,0:T(8,128)S(1)}) custom-call(bf16[4,1024,512]{2,1,0:T(8,128)(2,1)S(1)} %shard_map.366.sum_ref, f32[1024,2048]{1,0:T(8,128)} %hidden_ref.3, f32[1,2048]{1,0:T(1,128)S(1)} %bitcast.107), custom_call_target="tpu_custom_call" | custom-call | flops 20971520 | bytes 37748736 | tf_op jit(solution)/shard_map/pallas_call | solution.py:699
  329.4 23.1 %shard_map.368 = (bf16[1024,512]{1,0:T(8,128)(2,1)}, bf16[1024,512]{1,0:T(8,128)(2,1)}, bf16[1024,512]{1,0:T(8,128)(2,1)}, bf16[8,3,256,512]{3,2,1,0:T(8,128)(2,1)}) custom-call(bf16[1024,2048]{1,0:T(8,128)(2,1)} %copy-done.47, bf16[1024,2048]{1,0:T(8,128)(2,1)} %cot_ref.5, bf16[2048,1024]{1,0:T(8,128)(2,1)} %copy-done.48, bf16[2048,1024]{1,0:T(8,128)(2,1)} %bitcast.124, ...), custom_call_target="tpu_custom_call" | custom-call | flops 25769803776 | bytes 12582912 | tf_op jit(solution)/shard_map/pallas_call | solution.py:245
  352.6 16.9 %all-gather.13.cloned.1.call-done = bf16[24,256,1024]{2,1,0:T(8,128)(2,1)} async-done(((bf16[3,256,1024]{2,1,0:T(8,128)(2,1)}), bf16[24,256,1024]{2,1,0:T(8,128)(2,1)}) %all-gather.13.cloned.1.call-update) | async-done | bytes 12582928 | tf_op jit(solution)/shard_map/all_gather | solution.py:965
  369.4 38.2 %shard_map.369 = (bf16[1024,1024]{1,0:T(8,128)(2,1)}, bf16[1024,1024]{1,0:T(8,128)(2,1)}, bf16[1024,1024]{1,0:T(8,128)(2,1)}, bf16[8,3,256,1024]{3,2,1,0:T(8,128)(2,1)}) custom-call(bf16[1024,2048]{1,0:T(8,128)(2,1)} %copy-done.47, bf16[1024,2048]{1,0:T(8,128)(2,1)} %cot_ref.5, bf16[2048,1024]{1,0:T(8,128)(2,1)} %copy-done.48, bf16[2048,1024]{1,0:T(8,128)(2,1)} %bitcast.125, ...), custom_call_target="tpu_custom_call" | custom-call | flops 51539607552 | bytes 25165824 | tf_op jit(solution)/shard_map/pallas_call | solution.py:245
  408.0 12.3 %shard_map.371.part_ref = bf16[4,1024,512]{2,1,0:T(8,128)(2,1)} custom-call(bf16[1024,512]{1,0:T(8,128)(2,1)} %get-tuple-element.124.refs_0_, bf16[8,3,256,512]{3,2,1,0:T(8,128)(2,1)} %bitcast.122, bf16[1024,1024]{1,0:T(8,128)(2,1)} %get-tuple-element.125.refs_2_, bf16[8,3,256,1024]{3,2,1,0:T(8,128)(2,1)} %bitcast.119), custom_call_target="tpu_custom_call" | custom-call | flops 4294967296 | bytes 4194304 | tf_op jit(solution)/shard_map/pallas_call | solution.py:281
  420.3 19.3 %shard_map.370.part_ref = bf16[4,1024,512]{2,1,0:T(8,128)(2,1)} custom-call(bf16[1024,512]{1,0:T(8,128)(2,1)} %get-tuple-element.119.refs_0_, bf16[1024,512]{1,0:T(8,128)(2,1)} %get-tuple-element.120.refs_1_, bf16[8,3,256,512]{3,2,1,0:T(8,128)(2,1)} %bitcast.123, bf16[1024,1024]{1,0:T(8,128)(2,1)} %get-tuple-element.122.refs_3_, ...), custom_call_target="tpu_custom_call" | custom-call | flops 8589934592 | bytes 8388608 | tf_op jit(solution)/shard_map/pallas_call | solution.py:281
  439.5 2.2 copy-done.16
  441.7 71.4 %shard_map.372.sum_ref = bf16[4,1024,512]{2,1,0:T(8,128)(2,1)S(1)} custom-call(bf16[4,1024,512]{2,1,0:T(8,128)(2,1)S(1)} %copy-done.16), custom_call_target="tpu_custom_call" | custom-call | bytes 268435456 | tf_op jit(solution)/shard_map/pallas_call | solution.py:422
  515.1 2.2 copy-done.3
  517.3 2.3 copy-done.7
  520.6 10.1 %shard_map.373 = (f32[1024,2048]{1,0:T(8,128)}, bf16[1024,2048]{1,0:T(8,128)(2,1)S(1)}, f32[1,2048]{1,0:T(1,128)S(1)}) custom-call(bf16[4,1024,512]{2,1,0:T(8,128)(2,1)S(1)} %copy-done.7, bf16[1024,2048]{1,0:T(8,128)(2,1)S(1)} %copy-done.3, f32[1024,2048]{1,0:T(8,128)} %get-tuple-element.114.resid_ref, f32[1024,1]{1,0:T(8,128)S(1)} %copy-done.37, ...), custom_call_target="tpu_custom_call" | custom-call | flops 20971520 | bytes 33554432 | tf_op jit(solution)/shard_map/pallas_call | solution.py:750
  530.8 2.4 convolution_convert_fusion.1
  535.7 5.2 fusion.5
  543.3 13.0 %shard_map.374 = (f32[1024,256]{1,0:T(8,128)}, bf16[8192,256]{1,0:T(8,128)(2,1)}) custom-call(s32[3,2]{1,0:T(4,128)} %copy-done.45, bf16[1024,256]{1,0:T(8,128)(2,1)} %copy-done.51, bf16[1024,256]{1,0:T(8,128)(2,1)} %get-tuple-element.207.grad_ref, bf16[1024,256]{1,0:T(8,128)(2,1)} %copy-done.41, f32[2,1,1024]{2,1,0:T(1,128)} %copy-done.54, ...), custom_call_target="tpu_custom_call" | custom-call | flops 21474836480 | bytes 8388608 | tf_op jit(solution)/shard_map/pallas_call | solution.py:172
  556.3 3.5 collective-permute-done.1
  559.8 15.3 %reduce-scatter.8.cloned.1.call-done = bf16[1,3,256,1024]{3,2,1,0:T(8,128)(2,1)} async-done(((bf16[8,3,256,1024]{3,2,1,0:T(8,128)(2,1)}), bf16[1,3,256,1024]{3,2,1,0:T(8,128)(2,1)}) %reduce-scatter.8.cloned.1.call-update) | async-done | bytes 1572880 | tf_op jit(solution)/shard_map/reduce_scatter | solution.py:990
  576.3 12.9 %shard_map.375 = (f32[1024,256]{1,0:T(8,128)}, bf16[8192,256]{1,0:T(8,128)(2,1)}) custom-call(s32[3,2]{1,0:T(4,128)} %copy-done.45, bf16[1024,256]{1,0:T(8,128)(2,1)} %copy-done.49, bf16[1024,256]{1,0:T(8,128)(2,1)} %get-tuple-element.135.grad_ref, bf16[1024,256]{1,0:T(8,128)(2,1)} %copy-done.40, f32[2,1,1024]{2,1,0:T(1,128)} %copy-done.53, ...), custom_call_target="tpu_custom_call" | custom-call | flops 21474836480 | bytes 8388608 | tf_op jit(solution)/shard_map/pallas_call | solution.py:172
  589.2 13.9 %collective-permute-done.2 = bf16[256,512]{1,0:T(8,128)(2,1)S(1)} collective-permute-done((bf16[256,512]{1,0:T(8,128)(2,1)S(1)}, bf16[256,512]{1,0:T(8,128)(2,1)S(1)}, u32[]{:S(2)}, u32[]{:S(2)}) %collective-permute-start.2) | collective-permute-done | bytes 262176 | tf_op jit(solution)/shard_map/ppermute | solution.py:1021
  603.1 52.0 %reduce-scatter.10.cloned.1.call-done.refs_2_ = bf16[1024,256]{1,0:T(8,128)(2,1)} async-done(((bf16[8192,256]{1,0:T(8,128)(2,1)}), bf16[1024,256]{1,0:T(8,128)(2,1)}) %reduce-scatter.10.cloned.1.call-update) | async-done | bytes 524304 | tf_op jit(solution)/shard_map/reduce_scatter | solution.py:1059
  656.9 2.2 copy-done.2
  659.0 35.4 %shard_map.376 = bf16[1024,512]{1,0:T(8,128)(2,1)S(1)} custom-call(bf16[4,1024,512]{2,1,0:T(8,128)(2,1)S(1)} %copy-done.2), custom_call_target="tpu_custom_call" | custom-call | bytes 134217728 | tf_op jit(solution)/shard_map/pallas_call | solution.py:422
  696.7 5.6 fusion
  702.4 9.2 %shard_map.378 = (f32[2,256,1536]{2,1,0:T(8,128)}, f32[2,256,1536]{2,1,0:T(8,128)}, f32[2,256,1536]{2,1,0:T(8,128)}, bf16[2,256,1536]{2,1,0:T(8,128)(2,1)}, f32[...) custom-call(bf16[3,256,512]{2,1,0:T(8,128)(2,1)S(1)} %bitcast.106, ...), custom_call_target="tpu_custom_call" | custom-call | bytes 30670848 | tf_op jit(solution)/shard_map/pallas_call | solution.py:807
  716.4 7.0 reduce-scatter.12.cloned.1.call-done.refs_3_
  723.4 2.2 copy-done.13
  731.0 4.0 shard_map.379
  735.0 6.3 convolution_convert_fusion
  742.3 3.4 copy-done
  745.8 2.8 copy-done.10
  748.6 8.4 %shard_map.380 = (bf16[4,1024,512]{2,1,0:T(8,128)(2,1)S(1)}, f32[1024,1]{1,0:T(8,128)S(1)}, f32[1,2048]{1,0:T(1,128)S(1)}) custom-call(bf16[1024,1024]{1,0:T(8,128)(2,1)S(1)} %get-tuple-element.167.grad_ref, bf16[2048,1536]{1,0:T(8,128)(2,1)S(1)} %copy-done.10, f32[1024,2048]{1,0:T(8,128)S(1)} %copy-done, f32[1024,1]{1,0:T(8,128)S(1)} %copy.58.scale_ref, ...), custom_call_target="tpu_custom_call" | custom-call | flops 8589934592 | bytes 4194304 | tf_op jit(solution)/shard_map/pallas_call | solution.py:658
  759.3 2.2 copy-done.15
  761.6 40.3 %shard_map.381 = (bf16[1024,512]{1,0:T(8,128)(2,1)S(1)}, f32[8,128]{1,0:T(8,128)S(1)}, f32[40,128]{1,0:T(8,128)S(1)}) custom-call(bf16[4,1024,512]{2,1,0:T(8,128)(2,1)S(1)} %copy-done.15, f32[8,128]{1,0:T(8,128)S(1)} %bitcast.116, f32[40,128]{1,0:T(8,128)S(1)} %pad_bitcast_fusion.gains_ref), custom_call_target="tpu_custom_call" | custom-call | bytes 134217728 | tf_op jit(solution)/shard_map/pallas_call | solution.py:509
  804.3 4.2 multiply_add_fusion
  808.5 3.7 fusion.22
  (212 shorter events, 60.6 us)
Async XLA Ops:
  7.2 3.6 copy-start.66
  7.2 3.8 copy-start.59
  7.2 71.1 %all-gather.7.cloned.1.call-start = ((), (), s32[]{:S(2)}) async-start(), calls=%async_computation.5 | async-start | bytes 7077888 | tf_op jit(solution)/shard_map/all_gather | solution.py:924
  10.7 164.2 %all-gather.9.cloned.1.call-start = ((), (), s32[]{:S(2)}) async-start(), calls=%async_computation.6 | async-start | bytes 9437184 | tf_op jit(solution)/shard_map/all_gather | solution.py:956
  11.2 176.6 %copy-start.44 = (s32[1024]{0:T(1024)}, s32[1024]{0:T(1024)S(1)}, u32[]{:S(2)}) copy-start(s32[1024]{0:T(1024)S(1)} %select_reduce_fusion) | copy-start | bytes 12292
  13.4 64.9 %copy-start.23 = (f32[1024,128]{1,0:T(8,128)}, f32[1024,128]{1,0:T(8,128)S(1)}, u32[]{:S(2)}) copy-start(f32[1024,128]{1,0:T(8,128)S(1)} %get-tuple-element.215.cos_ref) | copy-start | bytes 1572868
  13.5 64.9 %copy-start.25 = (f32[1024,128]{1,0:T(8,128)}, f32[1024,128]{1,0:T(8,128)S(1)}, u32[]{:S(2)}) copy-start(f32[1024,128]{1,0:T(8,128)S(1)} %get-tuple-element.216.sin_ref) | copy-start | bytes 1572868
  17.9 9.4 %copy-start.61 = (f32[1024]{0:T(1024)}, f32[1024]{0:T(1024)S(1)}, u32[]{:S(2)}) copy-start(f32[1024]{0:T(1024)S(1)} %add_rsqrt_fusion) | copy-start | bytes 12292
  17.9 9.4 %copy-start.42 = (f32[2048]{0:T(1024)}, f32[2048]{0:T(1024)S(1)}, u32[]{:S(2)}) copy-start(f32[2048]{0:T(1024)S(1)} %get-tuple-element.210) | copy-start | bytes 24580
  78.3 2.8 copy-start.9
  94.1 2.8 copy-start.8
  94.1 146.4 %all-gather.11.cloned.1.call-start = ((), (), s32[]{:S(2)}) async-start(), calls=%async_computation.12 | async-start | bytes 7077888 | tf_op jit(solution)/shard_map/all_gather | solution.py:965
  175.0 194.5 %all-gather.13.cloned.1.call-start = ((), (), s32[]{:S(2)}) async-start(), calls=%async_computation.13 | async-start | bytes 14155776 | tf_op jit(solution)/shard_map/all_gather | solution.py:965
  175.5 12.3 %copy-start.45 = (s32[3,2]{1,0:T(4,128)}, s32[3,2]{1,0:T(4,128)S(1)}, u32[]{:S(2)}) copy-start(s32[3,2]{1,0:T(4,128)S(1)} %pad_add_fusion.bound_ref) | copy-start | bytes 76
  179.2 8.6 %copy-start.50 = (bf16[1024,256]{1,0:T(8,128)(2,1)S(1)}, bf16[1024,256]{1,0:T(8,128)(2,1)}, u32[]{:S(2)}) copy-start(bf16[1024,256]{1,0:T(8,128)(2,1)} %copy-done.49) | copy-start | bytes 1572868
  187.8 8.3 %slice-start = ((s8[6291456]{0:T(1024)(128)(4,1)}), s8[4194304]{0:T(1024)(128)(4,1)S(1)}, s32[]{:S(2)}) async-start(s8[6291456]{0:T(1024)(128)(4,1)} %bitcast.103), calls=%async_computation.14 | async-start | bytes 8388608
  187.8 8.3 %slice-start.1 = ((s8[6291456]{0:T(1024)(128)(4,1)}), s8[2097152]{0:T(1024)(128)(4,1)S(1)}, s32[]{:S(2)}) async-start(s8[6291456]{0:T(1024)(128)(4,1)} %bitcast.103), calls=%async_computation.15 | async-start | bytes 4194304
  240.5 274.6 %reduce-scatter.6.cloned.1.call-start = ((), (), s32[]{:S(2)}) async-start(), calls=%async_computation.7 | async-start | bytes 7077888 | tf_op jit(solution)/shard_map/reduce_scatter | solution.py:990
  314.9 9.7 %copy-start.1 = (bf16[4,1024,512]{2,1,0:T(8,128)(2,1)}, bf16[4,1024,512]{2,1,0:T(8,128)(2,1)S(1)}, u32[]{:S(2)}) copy-start(bf16[4,1024,512]{2,1,0:T(8,128)(2,1)S(1)} %shard_map.366.sum_ref) | copy-start | bytes 12582916
  352.5 222.5 %reduce-scatter.8.cloned.1.call-start = ((), (), s32[]{:S(2)}) async-start(), calls=%async_computation.8 | async-start | bytes 14155776 | tf_op jit(solution)/shard_map/reduce_scatter | solution.py:990
  407.7 247.5 %reduce-scatter.10.cloned.1.call-start = ((), (), s32[]{:S(2)}) async-start(), calls=%async_computation.9 | async-start | bytes 4718592 | tf_op jit(solution)/shard_map/reduce_scatter | solution.py:1059
  520.6 10.1 %copy-start.21 = (bf16[1024,512]{1,0:T(8,128)(2,1)S(1)}, bf16[1024,512]{1,0:T(8,128)(2,1)}, u32[]{:S(2)}) copy-start(bf16[1024,512]{1,0:T(8,128)(2,1)} %copy-done.20) | copy-start | bytes 3145732
  530.8 2.4 copy-start.46
  535.7 6.3 collective-permute-start
  543.0 16.8 %collective-permute-start.1 = (bf16[256,512]{1,0:T(8,128)(2,1)S(1)}, bf16[256,512]{1,0:T(8,128)(2,1)S(1)}, u32[]{:S(2)}, u32[]{:S(2)}) collective-permute-start(bf16[256,512]{1,0:T(8,128)(2,1)S(1)} %fusion.16), channel_id=1, source_target_pairs={{0,8},{4,12},{8,16},{12,20},{16,24},{20,28},{24,0},{28,4},{1,9},{5... | collective-permute-start | bytes 786440 | tf_op jit(solution)/shard_map/ppermute | solution.py:1021
  575.1 148.3 %reduce-scatter.12.cloned.1.call-start = ((), (), s32[]{:S(2)}) async-start(), calls=%async_computation.10 | async-start | bytes 4718592 | tf_op jit(solution)/shard_map/reduce_scatter | solution.py:1059
  576.3 26.9 %collective-permute-start.2 = (bf16[256,512]{1,0:T(8,128)(2,1)S(1)}, bf16[256,512]{1,0:T(8,128)(2,1)S(1)}, u32[]{:S(2)}, u32[]{:S(2)}) collective-permute-start(bf16[256,512]{1,0:T(8,128)(2,1)S(1)} %fusion.15), channel_id=1, source_target_pairs={{0,8},{4,12},{8,16},{12,20},{16,24},{20,28},{24,0},{28,4},{1,9},{5... | collective-permute-start | bytes 786440 | tf_op jit(solution)/shard_map/ppermute | solution.py:1021
  589.2 66.0 %copy-start.65 = (s32[1024]{0:T(1024)S(1)}, s32[1024]{0:T(1024)}, u32[]{:S(2)}) copy-start(s32[1024]{0:T(1024)} %param.22) | copy-start | bytes 12292
  655.2 153.2 %reduce-scatter.14.cloned.1.call-start = ((), (), s32[]{:S(2)}) async-start(), calls=%async_computation.11 | async-start | bytes 4718592 | tf_op jit(solution)/shard_map/reduce_scatter | solution.py:1085
  659.0 43.3 %copy-start.33 = (bf16[1,3,256,512]{3,2,1,0:T(8,128)(2,1)S(1)}, bf16[1,3,256,512]{3,2,1,0:T(8,128)(2,1)}, u32[]{:S(2)}) copy-start(bf16[1,3,256,512]{3,2,1,0:T(8,128)(2,1)} %reduce-scatter.6.cloned.1.call-done) | copy-start | bytes 2359300
  694.5 7.9 copy-start.29
  695.8 6.6 copy-start.11
  695.8 6.6 copy-start.19
  695.8 6.6 copy-start.27
  695.8 6.6 copy-start.28
  695.8 17.9 %collective-permute-start.3 = (bf16[256,512]{1,0:T(8,128)(2,1)S(1)}, bf16[256,512]{1,0:T(8,128)(2,1)S(1)}, u32[]{:S(2)}, u32[]{:S(2)}) collective-permute-start(bf16[256,512]{1,0:T(8,128)(2,1)S(1)} %fusion.11), channel_id=1, source_target_pairs={{0,8},{4,12},{8,16},{12,20},{16,24},{20,28},{24,0},{28,4},{1,9},{5... | collective-permute-start | bytes 786440 | tf_op jit(solution)/shard_map/ppermute | solution.py:1021
  702.4 12.5 %copy-start.22 = (f32[512,256]{1,0:T(8,128)S(1)}, f32[512,256]{1,0:T(8,128)}, u32[]{:S(2)}) copy-start(f32[512,256]{1,0:T(8,128)} %refs_0_.1) | copy-start | bytes 1572868
  702.4 12.5 %copy-start.34 = (f32[512,256]{1,0:T(8,128)S(1)}, f32[512,256]{1,0:T(8,128)}, u32[]{:S(2)}) copy-start(f32[512,256]{1,0:T(8,128)} %refs_1_.1) | copy-start | bytes 1572868
  702.4 12.5 %copy-start.35 = (f32[512,256]{1,0:T(8,128)S(1)}, f32[512,256]{1,0:T(8,128)}, u32[]{:S(2)}) copy-start(f32[512,256]{1,0:T(8,128)} %refs_2_.2) | copy-start | bytes 1572868
  711.6 11.8 %copy-start.30 = (f32[1024,256]{1,0:T(8,128)S(1)}, f32[1024,256]{1,0:T(8,128)}, u32[]{:S(2)}) copy-start(f32[1024,256]{1,0:T(8,128)} %get-tuple-element.163.refs_0_) | copy-start | bytes 3145732
  731.0 4.0 copy-start.18
  742.3 3.5 copy-start
  745.8 2.8 copy-start.10
  759.0 44.6 %copy-start.60 = (f32[4352]{0:T(1024)S(1)}, f32[4352]{0:T(1024)}, u32[]{:S(2)}) copy-start(f32[4352]{0:T(1024)} %param.27) | copy-start | bytes 52228
  759.0 44.6 %copy-start.63 = (f32[4352]{0:T(1024)S(1)}, f32[4352]{0:T(1024)}, u32[]{:S(2)}) copy-start(f32[4352]{0:T(1024)} %param.37) | copy-start | bytes 52228
  759.0 44.6 %copy-start.64 = (f32[4352]{0:T(1024)S(1)}, f32[4352]{0:T(1024)}, u32[]{:S(2)}) copy-start(f32[4352]{0:T(1024)} %param.32) | copy-start | bytes 52228
  804.3 4.2 copy-start.56
  804.3 4.2 copy-start.58
  (35 other events, 49.8 us)
Sparse Core Ops, SparseCore 0:
  10.8 67.4 all-gather.6
  94.2 80.6 all-gather.8
  177.2 63.2 all-gather.10
  242.6 126.8 all-gather.12
  371.6 68.0 reduce-scatter.5
  441.8 133.2 reduce-scatter.7
  577.3 77.8 reduce-scatter.9
  657.5 65.8 reduce-scatter.11
  741.4 50.7 reduce-scatter.13

commit v4 on v3

--- a/solution.py
+++ b/solution.py
@@ -86,7 +86,7 @@
             ],
             scratch_shapes=[pltpu.VMEM((2 * query_rows, head_dim), jnp.bfloat16), pltpu.VMEM((head_dim, 2 * query_rows), jnp.float32)],
         ),
-        compiler_params=pltpu.CompilerParams(vmem_limit_bytes=48 * MIB),
+        compiler_params=pltpu.CompilerParams(vmem_limit_bytes=60 * MIB),
         cost_estimate=pl.CostEstimate(flops=8 * rows * kv_all.shape[0] * head_dim, bytes_accessed=2 * kv_all.size, transcendentals=2 * rows * kv_all.shape[0]),
     )(bounds, queries, begins, kv_all)
 
@@ -135,7 +135,7 @@
             probs = jnp.where(allowed, probs, 0.0)
         kv_sum[place, head_dim:] += matmul(probs.astype(jnp.bfloat16), g_two[...], NN)
         grad_probs = matmul(values, g_two[...], NT)
-        grad_scores = (probs * ((grad_probs - delta) * unit)).astype(jnp.bfloat16)
+        grad_scores = (probs * (grad_probs - delta)).astype(jnp.bfloat16)
         kv_sum[place, :head_dim] += matmul(grad_scores, q_two[...], NN)
         dq_two[...] += matmul(grad_scores, keys, TN)
 
@@ -156,12 +156,13 @@
     low = begin_first // key_rows
     high = (first + rows - 1) // key_rows + 1
     lax.fori_loop(low, high, either, 0)
-    grad_q_ref[:, :head_dim] = dq_two[:rows].astype(grad_q_ref.dtype)
-    grad_q_ref[:, head_dim:] = dq_two[rows:].astype(grad_q_ref.dtype)
+    grad_q_ref[:, :head_dim] = (dq_two[:rows] * unit).astype(grad_q_ref.dtype)
+    grad_q_ref[:, head_dim:] = (dq_two[rows:] * unit).astype(grad_q_ref.dtype)
 
     @pl.when(block == pl.num_programs(0) - 1)
     def _():
-        grad_kv_ref[...] = kv_sum[...].astype(grad_kv_ref.dtype)
+        grad_kv_ref[:, :head_dim] = (kv_sum[:, :head_dim] * unit).astype(grad_kv_ref.dtype)
+        grad_kv_ref[:, head_dim:] = kv_sum[:, head_dim:].astype(grad_kv_ref.dtype)
 
 def attend_back(bounds, queries, grads, outs, totals, begin_rows, kv_all, group, head_dim, query_rows, key_rows):
     rows = queries.shape[0]
@@ -183,7 +184,7 @@
             scratch_shapes=[pltpu.VMEM((2 * query_rows, head_dim), jnp.bfloat16)] * 2
             + [pltpu.VMEM((2 * query_rows, head_dim), jnp.float32), pltpu.VMEM(kv_shape, jnp.float32)],
         ),
-        compiler_params=pltpu.CompilerParams(vmem_limit_bytes=56 * MIB),
+        compiler_params=pltpu.CompilerParams(vmem_limit_bytes=60 * MIB),
         cost_estimate=pl.CostEstimate(flops=20 * rows * kv_all.shape[0] * head_dim, bytes_accessed=2 * kv_all.size, transcendentals=2 * rows * kv_all.shape[0]),
     )(bounds, queries, grads, outs, totals, begin_rows, kv_all)
 
@@ -249,7 +250,7 @@
         out_specs=[row_spec, row_spec, row_spec, weight_spec],
         out_shape=(row_shape, row_shape, row_shape, jax.ShapeDtypeStruct((ways, 3, shard, width), jnp.bfloat16)),
         scratch_shapes=[pltpu.VMEM((3, depth, block), jnp.bfloat16)],
-        compiler_params=pltpu.CompilerParams(vmem_limit_bytes=56 * MIB),
+        compiler_params=pltpu.CompilerParams(vmem_limit_bytes=60 * MIB),
         cost_estimate=pl.CostEstimate(flops=24 * rows * depth * width, bytes_accessed=12 * depth * width, transcendentals=rows * width),
     )(normed, cotangent, normed_t, cotangent_t, weights)
 
@@ -284,7 +285,7 @@
         in_specs=specs,
         out_specs=pl.BlockSpec((1, rows, shard), lambda i: (i // per_piece, 0, i % per_piece)),
         out_shape=jax.ShapeDtypeStruct((pieces, rows, per_piece * shard), jnp.bfloat16),
-        compiler_params=pltpu.CompilerParams(vmem_limit_bytes=56 * MIB),
+        compiler_params=pltpu.CompilerParams(vmem_limit_bytes=60 * MIB),
         cost_estimate=pl.CostEstimate(flops=2 * len(weights) * kinds * rows * width * ways * shard, bytes_accessed=2 * len(weights) * kinds * width * ways * shard, transcendentals=0),
     )(*args)
 
@@ -541,53 +542,50 @@
     return jnp.where(lanes < head_dim // 2, first, -first)
 
 
-def front_kernel(groups, head_dim, normed_ref, weight_ref, cos_ref, sin_ref, gains_ref, raw_ref, *outs):
-    raw_ref[...] = matmul(normed_ref[...], weight_ref[...], NN)
+def front_kernel(groups, head_dim, first, normed_ref, cos_ref, sin_ref, gains_ref, *refs):
+    weights, raw_ref, outs = refs[:groups], refs[groups], refs[groups + 1 :]
     cosine = cos_ref[...]
     sine = sin_ref[...] * half_signs(head_dim, -1.0)
     for group in range(groups):
-        for at in range(4):
-            base = (group * 4 + at) * head_dim
+        pair = slice(group * 2 * head_dim, (group + 1) * 2 * head_dim)
+        raw_ref[:, pair] = matmul(normed_ref[...], weights[group][...], NN)
+        for at in range(2):
+            base = (group * 2 + at) * head_dim
             raw = raw_ref[:, base : base + head_dim]
-            if at < 3:
-                gain = gains_ref[at // 2 : at // 2 + 1]
+            if first + at < 3:
+                gain = gains_ref[first // 2 : first // 2 + 1]
                 scale = lax.rsqrt(jnp.mean(raw * raw, axis=1, keepdims=True) + EPSILON)
                 raw = raw * scale * gain
                 raw = raw * cosine + turned_by(raw, sine)
-            out = outs[group] if at < 2 else outs[groups]
-            place = at % 2 * head_dim + (0 if at < 2 else group * 2 * head_dim)
+            out, place = (outs[group], at * head_dim) if first == 0 else (outs[0], base)
             out[:, place : place + head_dim] = raw.astype(out.dtype)
 
 
-def front(normed, weight, width, cosine, sine, gains, head_dim):
+def front(normed, weight, groups, first, cosine, sine, gains, head_dim):
     rows, depth = normed.shape
-    groups = width // (4 * head_dim)
     block = min(256, rows)
-    narrow = pl.BlockSpec((block, 2 * head_dim), lambda i: (i, 0))
+    width = groups * 2 * head_dim
     table = pl.BlockSpec((block, head_dim), lambda i: (i, 0))
+    outs = [2 * head_dim] * groups if first == 0 else [width]
+
+    def weight_spec(group):
+        return pl.BlockSpec((depth, 2 * head_dim), lambda i: (0, 2 * group + first // 2), pipeline_mode=pl.Buffered(1))
+
     found = pl.pallas_call(
-        functools.partial(front_kernel, groups, head_dim),
+        functools.partial(front_kernel, groups, head_dim, first),
         grid=(rows // block,),
-        in_specs=[
-            pl.BlockSpec((block, depth), lambda i: (i, 0)),
-            pl.BlockSpec((depth, width), lambda i: (0, 0), pipeline_mode=pl.Buffered(1)),
-            table,
-            table,
-            pl.BlockSpec(gains.shape, lambda i: (0, 0)),
-        ],
-        out_specs=[pl.BlockSpec((block, width), lambda i: (i, 0))]
-        + [narrow] * groups
-        + [pl.BlockSpec((block, groups * 2 * head_dim), lambda i: (i, 0))],
+        in_specs=[pl.BlockSpec((block, depth), lambda i: (i, 0)), table, table, pl.BlockSpec(gains.shape, lambda i: (0, 0))]
+        + [weight_spec(group) for group in range(groups)],
+        out_specs=[pl.BlockSpec((block, columns), lambda i: (i, 0)) for columns in [width] + outs],
         out_shape=[jax.ShapeDtypeStruct((rows, width), jnp.float32)]
-        + [jax.ShapeDtypeStruct((rows, 2 * head_dim), jnp.bfloat16)] * groups
-        + [jax.ShapeDtypeStruct((rows, groups * 2 * head_dim), jnp.bfloat16)],
-        compiler_params=pltpu.CompilerParams(vmem_limit_bytes=32 * MIB),
-        cost_estimate=pl.CostEstimate(flops=4 * rows * depth * width, bytes_accessed=2 * depth * width, transcendentals=0),
-    )(normed, weight, cosine, sine, gains)
-    return found[0], found[1 : 1 + groups], found[1 + groups]
-
-
-def front_back_kernel(groups, head_dim, raw_ref, cos_ref, sin_ref, gains_ref, *refs):
+        + [jax.ShapeDtypeStruct((rows, columns), jnp.bfloat16) for columns in outs],
+        compiler_params=pltpu.CompilerParams(vmem_limit_bytes=60 * MIB),
+        cost_estimate=pl.CostEstimate(flops=2 * rows * depth * width, bytes_accessed=2 * depth * width, transcendentals=0),
+    )(normed, cosine, sine, gains, *[weight] * groups)
+    return found[0], found[1:]
+
+
+def front_back_kernel(groups, head_dim, raw_query_ref, raw_key_ref, cos_ref, sin_ref, gains_ref, *refs):
     queries, keys = refs[:groups], refs[groups : 2 * groups]
     out_ref, sums_ref = refs[2 * groups :]
 
@@ -604,7 +602,8 @@
             grads = source[:, at % 2 * head_dim : (at % 2 + 1) * head_dim].astype(jnp.float32)
             if at < 3:
                 gain = gains_ref[at // 2 : at // 2 + 1]
-                raw = raw_ref[:, base : base + head_dim]
+                place = (group * 2 + at % 2) * head_dim
+                raw = (raw_query_ref if at < 2 else raw_key_ref)[:, place : place + head_dim]
                 scale = lax.rsqrt(jnp.mean(raw * raw, axis=1, keepdims=True) + EPSILON)
                 normal = raw * scale
                 grads = grads * cosine + turned_by(grads, sine)
@@ -614,25 +613,26 @@
             out_ref[:, base : base + head_dim] = grads.astype(out_ref.dtype)
 
 
-def front_back(raw, cosine, sine, gains, grad_queries, grad_kv, head_dim):
-    rows, width = raw.shape
+def front_back(raw_queries, raw_keys, cosine, sine, gains, grad_queries, grad_kv, head_dim):
+    rows, width = raw_queries.shape[0], 2 * raw_queries.shape[1]
     groups = width // (4 * head_dim)
     block = min(256, rows)
+    half = pl.BlockSpec((block, width // 2), lambda i: (i, 0))
     narrow = pl.BlockSpec((block, 2 * head_dim), lambda i: (i, 0))
     table = pl.BlockSpec((block, head_dim), lambda i: (i, 0))
     wide = pl.BlockSpec((block, width), lambda i: (i, 0))
     return pl.pallas_call(
         functools.partial(front_back_kernel, groups, head_dim),
         grid=(rows // block,),
-        in_specs=[wide, table, table, pl.BlockSpec(gains.shape, lambda i: (0, 0))] + [narrow] * (2 * groups),
+        in_specs=[half, half, table, table, pl.BlockSpec(gains.shape, lambda i: (0, 0))] + [narrow] * (2 * groups),
         out_specs=[wide, pl.BlockSpec((8, head_dim), lambda i: (0, 0))],
         out_shape=[
             jax.ShapeDtypeStruct((rows, width), jnp.bfloat16),
             jax.ShapeDtypeStruct((8, head_dim), jnp.float32),
         ],
-        compiler_params=pltpu.CompilerParams(vmem_limit_bytes=32 * MIB),
+        compiler_params=pltpu.CompilerParams(vmem_limit_bytes=60 * MIB),
         cost_estimate=pl.CostEstimate(flops=60 * rows * width, bytes_accessed=10 * rows * width, transcendentals=0),
-    )(raw, cosine, sine, gains, *grad_queries, *grad_kv)
+    )(raw_queries, raw_keys, cosine, sine, gains, *grad_queries, *grad_kv)
 
 
 def last_product_kernel(grad_ref, weight_ref, hidden_ref, scale_ref, gain_ref, out_ref, dots_ref, gain_out_ref):
@@ -675,7 +675,7 @@
             jax.ShapeDtypeStruct((rows, 1), jnp.float32),
             jax.ShapeDtypeStruct((1, depth), jnp.float32),
         ],
-        compiler_params=pltpu.CompilerParams(vmem_limit_bytes=32 * MIB),
+        compiler_params=pltpu.CompilerParams(vmem_limit_bytes=60 * MIB),
         cost_estimate=pl.CostEstimate(flops=4 * rows * depth * width, bytes_accessed=2 * depth * width, transcendentals=0),
     )(grads, weight, hidden, scale, gain)
 
@@ -716,7 +716,7 @@
             jax.ShapeDtypeStruct((depth, rows), jnp.bfloat16),
             jax.ShapeDtypeStruct((rows, 1), jnp.float32),
         ],
-        compiler_params=pltpu.CompilerParams(vmem_limit_bytes=40 * MIB),
+        compiler_params=pltpu.CompilerParams(vmem_limit_bytes=60 * MIB),
         cost_estimate=pl.CostEstimate(flops=10 * rows * depth, bytes_accessed=18 * rows * depth, transcendentals=0),
     )(total, hidden, gain)
 
@@ -763,7 +763,7 @@
             jax.ShapeDtypeStruct((rows, depth), jnp.bfloat16),
             jax.ShapeDtypeStruct((1, depth), jnp.float32),
         ],
-        compiler_params=pltpu.CompilerParams(vmem_limit_bytes=40 * MIB),
+        compiler_params=pltpu.CompilerParams(vmem_limit_bytes=60 * MIB),
         cost_estimate=pl.CostEstimate(flops=10 * rows * depth, bytes_accessed=16 * rows * depth, transcendentals=0),
     )(total, cotangent, resid, scale, gain)
 
@@ -827,7 +827,7 @@
         in_specs=[pl.BlockSpec(memory_space=pltpu.VMEM)] * 4,
         out_specs=[pl.BlockSpec(memory_space=pltpu.VMEM)] * 4,
         out_shape=[jax.ShapeDtypeStruct(held[0].shape, kind) for kind in types],
-        compiler_params=pltpu.CompilerParams(vmem_limit_bytes=24 * MIB),
+        compiler_params=pltpu.CompilerParams(vmem_limit_bytes=60 * MIB),
         cost_estimate=pl.CostEstimate(flops=0, bytes_accessed=28 * grad_t.size, transcendentals=0),
     )(grad_t, *held)
 
@@ -849,9 +849,35 @@
         ],
         out_specs=pl.BlockSpec((1, rows, block), lambda i: (i // 2, 0, i % 2)),
         out_shape=jax.ShapeDtypeStruct((pieces, rows, depth // pieces), jnp.bfloat16),
-        compiler_params=pltpu.CompilerParams(vmem_limit_bytes=32 * MIB),
+        compiler_params=pltpu.CompilerParams(vmem_limit_bytes=60 * MIB),
         cost_estimate=pl.CostEstimate(flops=2 * rows * depth * width, bytes_accessed=2 * depth * width, transcendentals=0),
     )(left, weight)
+
+
+def weight_products_kernel(normed_ref, grad_ref, left_ref, mixed_ref, out_ref):
+    width = grad_ref.shape[1]
+    out_ref[:, :width] = matmul(normed_ref[...], grad_ref[...], TN).astype(out_ref.dtype)
+    out_ref[:, width:] = matmul(left_ref[...], mixed_ref[...], TN).astype(out_ref.dtype)
+
+
+def weight_products(normed, grads, left, mixed):
+    rows, depth = normed.shape
+    block = min(256, depth)
+    width = grads.shape[1] + mixed.shape[1]
+    column = pl.BlockSpec((rows, block), lambda i: (0, i))
+
+    def held(array):
+        return pl.BlockSpec(array.shape, lambda i: (0, 0), pipeline_mode=pl.Buffered(1))
+
+    return pl.pallas_call(
+        weight_products_kernel,
+        grid=(depth // block,),
+        in_specs=[column, held(grads), column, held(mixed)],
+        out_specs=pl.BlockSpec((block, width), lambda i: (i, 0)),
+        out_shape=jax.ShapeDtypeStruct((depth, width), jnp.bfloat16),
+        compiler_params=pltpu.CompilerParams(vmem_limit_bytes=60 * MIB),
+        cost_estimate=pl.CostEstimate(flops=2 * rows * depth * width, bytes_accessed=2 * depth * width, transcendentals=0),
+    )(normed, grads, left, mixed)
 
 
 def rms_scale(values_in):
@@ -950,10 +976,14 @@
     normal_one = hidden_in * scale_one
     normed_one_b = (normal_one * gain_attn).astype(bf16)
     gains_two = jnp.stack([gain_query, gain_key])
-    projected, queries, kv_local = front(
-        normed_one_b, qkv_out, qkv_cols, cosine, sine, gains_two, head_dim
-    )
+    raw_keys, (kv_local,) = front(
+        normed_one_b, qkv_out, groups, 2, cosine, sine, gains_two, head_dim
+    )
+    normed_one_b, kv_local = tie(normed_one_b, kv_local)
     kv_every = lax.all_gather(kv_local, "dp", axis=0, tiled=True)
+    raw_queries, queries = front(
+        normed_one_b, qkv_out, groups, 0, cosine, sine, gains_two, head_dim
+    )
 
     down_t = w_down.T
 
@@ -964,7 +994,7 @@
     def chunk_gather(shard):
         return lax.all_gather(shard, "dp", axis=0)
 
-    shard, kv_every, cotangent_t = tie(chunk_shard(0), kv_every, cotangent.T)
+    shard, kv_every, cotangent_t, queries = tie(chunk_shard(0), kv_every, cotangent.T, queries)
     chunk_weights = [chunk_gather(shard)]
     mixed, totals = [], []
     for group in range(groups):
@@ -990,49 +1020,17 @@
         weight_grads.append(lax.psum_scatter(weight_grad, "dp", scatter_dimension=0))
 
     part_two = back_product(back_pairs, chunk_weights, 0, tensor_ways)
-    mlp_part = back_product(hiddens, chunk_weights, 2, tensor_ways)
-    part_two, mlp_part = tie(part_two, mlp_part)
     part_two_sum, weight_grads[0] = tie(tensor_sum(part_two, 1), weight_grads[0])
     grad_resid, grad_attn_b, gain_mlp_part = norm_and_add_back(
         part_two_sum, cotangent, resid_one, scale_two, gain_mlp[None]
     )
     grad_mixed_b = dot(grad_attn_b, qkv_out[:, qkv_cols:], NN).astype(bf16)
 
-    grad_out_t = dot(grad_attn_b, mixed_b, TN).astype(bf16)
-    lines = data_ways // 2
-    line_at, lane = lax.axis_index("dp") // 2, lax.axis_index("dp") % 2
-    out_pieces = grad_out_t.reshape(lines, 2, model_dim // data_ways, out_rows)
-
-    def chip_piece(step, of_lane):
-        return lax.dynamic_slice(
-            out_pieces, ((line_at + lines - step) % lines, of_lane, 0, 0), (1, 1, *out_pieces.shape[2:])
-        )[0, 0]
-
-    far_pieces = lax.ppermute(
-        jnp.stack([chip_piece(step, 1 - lane) for step in range(lines)]),
-        "dp",
-        [(at, at + 1 - 2 * (at % 2)) for at in range(data_ways)],
-    )
-
-    def chip_sum(step, *others):
-        return sum(value.astype(f32) for value in (chip_piece(step, lane), far_pieces[step], *others))
-
-    def hop(step, *others):
-        return lax.ppermute(
-            chip_sum(step, *others).astype(bf16), "dp", [(at, (at + 2) % data_ways) for at in range(data_ways)]
-        )
-
-    out_grad = hop(1)
     grad_queries, kv_sums = [], []
     for group in range(groups):
         grad_rows = grad_mixed_b[:, group * 2 * head_dim : (group + 1) * 2 * head_dim]
         if group and group == groups - 1:
-            grad_rows, weight_grads[1], out_grad, kv_sums[-1] = tie(
-                grad_rows, weight_grads[1], out_grad, kv_sums[-1]
-            )
-        if group == groups - 1:
-            for step in range(2, lines - 1):
-                out_grad = hop(step, out_grad)
+            grad_rows, weight_grads[1], kv_sums[-1] = tie(grad_rows, weight_grads[1], kv_sums[-1])
         grad_query, kv_sum = attend_back(
             bounds,
             queries[group],
@@ -1048,20 +1046,16 @@
         )
         grad_queries.append(grad_query)
         kv_sums.append(kv_sum)
-    out_grad, kv_sums[-1] = tie(out_grad, kv_sums[-1])
-    if lines > 2:
-        out_grad = hop(lines - 1, out_grad)
-    out_grad = chip_sum(0, out_grad).astype(bf16)
     kv_grads = []
     for group in range(groups):
         if group:
             kv_grads[-1], kv_sums[group] = tie(kv_grads[-1], kv_sums[group])
         kv_grads.append(lax.psum_scatter(kv_sums[group], "dp", scatter_dimension=0, tiled=True))
-    mlp_part, grad_queries[-1] = tie(mlp_part, grad_queries[-1])
+    hidden_b, grad_queries[-1] = tie(hiddens[0][0], grad_queries[-1])
+    mlp_part = back_product([(hidden_b,), *hiddens[1:]], chunk_weights, 2, tensor_ways)
     rate_matrix = LR_MATRIX / math.sqrt(tokens_all)
     mlp_sum = tensor_sum(mlp_part, 2, False)
     updates = (
-        *turned_step(rate_matrix, out_grad, (w_out, m_out, a_out)),
         *mlp_step(rate_matrix, weight_grads, (w_gate_up, m_gate_up, a_gate_up), (w_down, m_down, a_down)),
     )
     mlp_cols = mlp_sum.astype(f32)
@@ -1079,10 +1073,13 @@
         resid_cols + mlp_cols, gain_mlp_wide, jnp.stack(stats_part), kv_grads[-1], updates
     )
     grad_projected_b, gains_found = front_back(
-        projected, cosine, sine, gains_two, grad_queries, kv_grads, head_dim
-    )
-    grad_qkv = dot(normed_one_b, grad_projected_b, TN).astype(bf16)
-    qkv_shard = lax.psum_scatter(grad_qkv, "dp", scatter_dimension=0, tiled=True).astype(f32)
+        raw_queries, raw_keys, cosine, sine, gains_two, grad_queries, kv_grads, head_dim
+    )
+    both_grads, grad_projected_b = tie(
+        weight_products(normed_one_b, grad_projected_b, grad_attn_b, mixed_b), grad_projected_b
+    )
+    both_shard = lax.psum_scatter(both_grads, "dp", scatter_dimension=0, tiled=True)
+    qkv_shard = both_shard[:, :qkv_cols].astype(f32)
     part_one, dots_part, gain_attn_part = last_product(
         grad_projected_b, qkv_out, hidden_in, scale_one, gain_attn[None], tensor_ways
     )
@@ -1111,6 +1108,7 @@
         grad_cols,
         branch_rms,
         *nesterov(w_qkv, m_qkv, a_qkv, qkv_shard, rate_matrix),
+        *turned_step(rate_matrix, both_shard[:, qkv_cols:], (w_out, m_out, a_out)),
         *updates,
         *nesterov(norm_gains, m_gains, a_gains, grad_gains, rate_gain),
     )

time: 827 us -> 801 us (0.969); the launches traced: 819 us -> 804 us
  Pallas kernels: 406 us -> 447 us
  local copies, waits for them, and re-layouts: 72 us -> 45 us
  waiting for transfers between devices: 263 us -> 247 us
  matrix products: 13.9 us -> 5.18 us
    unnamed x146 -> x64, local copies, waits for them, and re-layouts: 66.4 us -> 34.2 us
    pallas_call x1 -> x3, Pallas kernels: 6.21 us -> 27.1 us  [the longest x2 14.1 us: front(): pl.pallas_call(functools.partial(front_kernel, groups, head_dim, first),...]
    reduce_scatter x2, waiting for transfers between devices: 15.3 us -> 34.4 us  [local(): lax.psum_scatter(weight_grad, 'dp', scatter_dimension=0)]
    ppermute x4 -> x0, waiting for transfers between devices: 17.4 us -> none  [the longest x3 17.4 us: hop(): lax.ppermute(chip_sum(step, *others).astype(bf16), 'dp', [(at, (at + 2) %...]
    reduce_scatter x2, waiting for transfers between devices: 59.1 us -> 46 us  [local(): lax.psum_scatter(kv_sums[group], 'dp', scatter_dimension=0, tiled=True)]
    dot_general x3 -> x1, matrix products: 13.9 us -> 5.18 us  [dot(): return lax.dot_general(a, b, dims, preferred_element_type=jnp.float32)]
  transfers between devices with their start and end apart: 13 -> 9, of which waited for: 9 -> 7; matrix products, arithmetic and copies ran while one was open for 8% -> 8% of each run, Pallas kernels for 48% -> 52%
where the time goes in v4:
time: 801 us; the launch traced here: 804 us
  Pallas kernels  447 us (56%)
  waiting for transfers between devices  247 us (31%)
  local copies, waits for them, and re-layouts  45 us (6%)
  other arithmetic  42 us (5%)
  between operations  15.7 us (2%)
    pallas_call x3, Pallas kernels, tensor_sum(): pl.pallas_call(functools.partial(tensor_sum_kernel, bits, whole), out_sha...  178 us
    pallas_call x2, Pallas kernels, mlp_chunk(): pl.pallas_call(mlp_kernel, grid=(width // block,), in_specs=[held(normed)...  61.6 us
    all_gather x1, waiting for transfers between devices, local(): kv_every = lax.all_gather(kv_local, 'dp', axis=0, tiled=True)  59.2 us
    all_gather x2, waiting for transfers between devices, chunk_gather(): return lax.all_gather(shard, 'dp', axis=0)  55.6 us
    all_gather x1, waiting for transfers between devices, local(): lax.all_gather(jnp.concatenate([w_qkv, w_out.T], axis=1).astype(bf16), 'd...  48.8 us
    reduce_scatter x2, waiting for transfers between devices, local(): lax.psum_scatter(kv_sums[group], 'dp', scatter_dimension=0, tiled=True)  46 us
    pallas_call x1, Pallas kernels, last_sum(): pl.pallas_call(functools.partial(last_sum_kernel, bits, data_ways), out_s...  42.3 us
    reduce_scatter x2, waiting for transfers between devices, local(): lax.psum_scatter(weight_grad, 'dp', scatter_dimension=0)  34.4 us
  transfers between devices with their start and end apart: 9, of which 7 were waited for; matrix products, arithmetic and copies ran while one was open for 8% of the time, Pallas kernels for 52%

profile of v4, /device:TPU:0, one launch (start us, length us, event | category | flops | bytes accessed | tf_op | source)
XLA Modules:
  0.0 803.9 jit_solution(12745230774802809367)
XLA Ops:
  11.8 1.9 multiply_sine_fusion
  15.0 4.0 multiply_reduce_fusion
  19.6 9.9 %multiply_convert_fusion = (bf16[1024,2048]{1,0:T(8,128)(2,1)}, f32[1024,2048]{1,0:T(8,128)}) fusion(f32[2048]{0:T(1024)S(1)} %get-tuple-element.202, f32[1024,2048]{1,0:T(8,128)} %hidden_ref.3, f32[1024]{0:T(1024)S(1)} %add_rsqrt_fusion), kind=kLoop, calls=%fused_computation | loop fusion | flops 6291456 | bytes 20983808 | tf_op jit(solution)/shard_map/convert_element_type | solution.py:977
  29.5 48.8 %all-gather.7.cloned.1.call-done.refs_0_.refs_1_.weight_ref = bf16[2048,1536]{1,0:T(8,128)(2,1)} async-done(((bf16[256,1536]{1,0:T(8,128)(2,1)}), bf16[2048,1536]{1,0:T(8,128)(2,1)}) %all-gather.7.cloned.1.call-update) | async-done | bytes 6291472 | tf_op jit(solution)/shard_map/all_gather | solution.py:950
  78.3 6.9 shard_map.362
  85.3 2.7 copy.55
  90.2 6.6 copy.57
  97.7 2.0 pad_maximum_fusion.1
  99.7 7.2 shard_map.363
  106.9 59.2 %all-gather.9.cloned.1.call-done.kv_ref = bf16[8192,512]{1,0:T(8,128)(2,1)} async-done(((bf16[1024,512]{1,0:T(8,128)(2,1)}), bf16[8192,512]{1,0:T(8,128)(2,1)}) %all-gather.9.cloned.1.call-update) | async-done | bytes 8388624 | tf_op jit(solution)/shard_map/all_gather | solution.py:983
  169.6 8.1 %shard_map.364 = (bf16[1024,256]{1,0:T(8,128)(2,1)}, f32[2,1,1024]{2,1,0:T(1,128)}) custom-call(s32[3,2]{1,0:T(4,128)} %pad_add_fusion.bound_ref, bf16[1024,256]{1,0:T(8,128)(2,1)} %get-tuple-element.110.query_ref, s32[2,1,512]{2,1,0:T(1,128)} %bitcast.78, bf16[8192,512]{1,0:T(8,128)(2,1)} %all-gather.9.cloned.1.call-done.kv_ref), custom_call_target="tpu_custom_call" | custom-call | flops 8589934592 | bytes 8388608 | tf_op jit(solution)/shard_map/pallas_call | solution.py:72
  177.7 1.9 constant_dynamic-update-slice_fusion.1
  179.5 8.2 %shard_map.365 = (bf16[1024,256]{1,0:T(8,128)(2,1)}, f32[2,1,1024]{2,1,0:T(1,128)}) custom-call(s32[3,2]{1,0:T(4,128)} %pad_add_fusion.bound_ref, bf16[1024,256]{1,0:T(8,128)(2,1)} %get-tuple-element.113.query_ref, s32[2,1,512]{2,1,0:T(1,128)} %bitcast.79, bf16[8192,512]{1,0:T(8,128)(2,1)} %all-gather.9.cloned.1.call-done.kv_ref), custom_call_target="tpu_custom_call" | custom-call | flops 8589934592 | bytes 8388608 | tf_op jit(solution)/shard_map/pallas_call | solution.py:72
  187.7 1.9 constant_dynamic-update-slice_fusion.left_ref.mixed_ref
  189.6 8.2 %shard_map.366.part_ref = bf16[4,1024,512]{2,1,0:T(8,128)(2,1)} custom-call(bf16[1024,512]{1,0:T(8,128)(2,1)} %constant_dynamic-update-slice_fusion.left_ref.mixed_ref, bf16[2048,1536]{1,0:T(8,128)(2,1)} %all-gather.7.cloned.1.call-done.refs_0_.refs_1_.weight_ref), custom_call_target="tpu_custom_call" | custom-call | flops 2147483648 | bytes 2097152 | tf_op jit(solution)/shard_map/pallas_call | solution.py:843
  197.8 33.9 %all-gather.11.cloned.1.call-done = bf16[24,256,512]{2,1,0:T(8,128)(2,1)} async-done(((bf16[3,256,512]{2,1,0:T(8,128)(2,1)}), bf16[24,256,512]{2,1,0:T(8,128)(2,1)}) %all-gather.11.cloned.1.call-update) | async-done | bytes 6291472 | tf_op jit(solution)/shard_map/all_gather | solution.py:995
  231.9 2.2 copy-done.2
  234.1 71.6 %shard_map.367.sum_ref = bf16[4,1024,512]{2,1,0:T(8,128)(2,1)S(1)} custom-call(bf16[4,1024,512]{2,1,0:T(8,128)(2,1)S(1)} %copy-done.2), custom_call_target="tpu_custom_call" | custom-call | bytes 268435456 | tf_op jit(solution)/shard_map/pallas_call | solution.py:423
  305.7 2.0 copy-done
  307.8 11.2 %shard_map.368 = (f32[1024,2048]{1,0:T(8,128)}, bf16[1024,2048]{1,0:T(8,128)(2,1)}, bf16[2048,1024]{1,0:T(8,128)(2,1)}, f32[1024,1]{1,0:T(8,128)}) custom-call(bf16[4,1024,512]{2,1,0:T(8,128)(2,1)} %copy-done, f32[1024,2048]{1,0:T(8,128)} %hidden_ref.3, f32[1,2048]{1,0:T(1,128)} %bitcast.74), custom_call_target="tpu_custom_call" | custom-call | flops 20971520 | bytes 37748736 | tf_op jit(solution)/shard_map/pallas_call | solution.py:699
  318.9 23.4 %shard_map.369 = (bf16[1024,512]{1,0:T(8,128)(2,1)}, bf16[1024,512]{1,0:T(8,128)(2,1)}, bf16[1024,512]{1,0:T(8,128)(2,1)}, bf16[8,3,256,512]{3,2,1,0:T(8,128)(2,1)}) custom-call(bf16[1024,2048]{1,0:T(8,128)(2,1)} %get-tuple-element.117.normed_ref, bf16[1024,2048]{1,0:T(8,128)(2,1)} %cot_ref.5, bf16[2048,1024]{1,0:T(8,128)(2,1)} %get-tuple-element.118.normed_t_ref, ...), custom_call_target="tpu_custom_call" | custom-call | flops 25769803776 | bytes 12582912 | tf_op jit(solution)/shard_map/pallas_call | solution.py:246
  342.4 21.7 %all-gather.13.cloned.1.call-done = bf16[24,256,1024]{2,1,0:T(8,128)(2,1)} async-done(((bf16[3,256,1024]{2,1,0:T(8,128)(2,1)}), bf16[24,256,1024]{2,1,0:T(8,128)(2,1)}) %all-gather.13.cloned.1.call-update) | async-done | bytes 12582928 | tf_op jit(solution)/shard_map/all_gather | solution.py:995
  364.1 38.2 %shard_map.370 = (bf16[1024,1024]{1,0:T(8,128)(2,1)}, bf16[1024,1024]{1,0:T(8,128)(2,1)}, bf16[1024,1024]{1,0:T(8,128)(2,1)}, bf16[8,3,256,1024]{3,2,1,0:T(8,128)(2,1)}) custom-call(bf16[1024,2048]{1,0:T(8,128)(2,1)} %get-tuple-element.117.normed_ref, bf16[1024,2048]{1,0:T(8,128)(2,1)} %cot_ref.5, bf16[2048,1024]{1,0:T(8,128)(2,1)} %get-tuple-element.118.normed_t_ref, ...), custom_call_target="tpu_custom_call" | custom-call | flops 51539607552 | bytes 25165824 | tf_op jit(solution)/shard_map/pallas_call | solution.py:246
  402.8 19.3 %shard_map.371.part_ref = bf16[4,1024,512]{2,1,0:T(8,128)(2,1)} custom-call(bf16[1024,512]{1,0:T(8,128)(2,1)} %get-tuple-element.122.refs_0_, bf16[1024,512]{1,0:T(8,128)(2,1)} %get-tuple-element.123.refs_1_, bf16[8,3,256,512]{3,2,1,0:T(8,128)(2,1)} %bitcast.67, bf16[1024,1024]{1,0:T(8,128)(2,1)} %get-tuple-element.125.refs_3_, ...), custom_call_target="tpu_custom_call" | custom-call | flops 8589934592 | bytes 8388608 | tf_op jit(solution)/shard_map/pallas_call | solution.py:282
  422.0 2.2 copy-done.7
  424.2 71.3 %shard_map.372.sum_ref = bf16[4,1024,512]{2,1,0:T(8,128)(2,1)S(1)} custom-call(bf16[4,1024,512]{2,1,0:T(8,128)(2,1)S(1)} %copy-done.7), custom_call_target="tpu_custom_call" | custom-call | bytes 268435456 | tf_op jit(solution)/shard_map/pallas_call | solution.py:423
  495.6 2.0 copy-done.3
  497.5 12.9 %shard_map.373 = (f32[1024,2048]{1,0:T(8,128)}, bf16[1024,2048]{1,0:T(8,128)(2,1)}, f32[1,2048]{1,0:T(1,128)}) custom-call(bf16[4,1024,512]{2,1,0:T(8,128)(2,1)} %copy-done.3, bf16[1024,2048]{1,0:T(8,128)(2,1)} %cot_ref.5, f32[1024,2048]{1,0:T(8,128)} %get-tuple-element.116.resid_ref, f32[1024,1]{1,0:T(8,128)} %get-tuple-element.129.scale_ref, ...), custom_call_target="tpu_custom_call" | custom-call | flops 20971520 | bytes 33554432 | tf_op jit(solution)/shard_map/pallas_call | solution.py:750
  510.4 5.2 fusion.5
  516.7 13.0 %shard_map.374 = (f32[1024,256]{1,0:T(8,128)}, bf16[8192,256]{1,0:T(8,128)(2,1)}) custom-call(s32[3,2]{1,0:T(4,128)} %pad_add_fusion.bound_ref, bf16[1024,256]{1,0:T(8,128)(2,1)} %get-tuple-element.110.query_ref, bf16[1024,256]{1,0:T(8,128)(2,1)} %get-tuple-element.199.grad_ref, bf16[1024,256]{1,0:T(8,128)(2,1)} %get-tuple-element.112.out_ref, ...), custom_call_target="tpu_custom_call" | custom-call | flops 21474836480 | bytes 8388608 | tf_op jit(solution)/shard_map/pallas_call | solution.py:173
  529.7 34.4 %reduce-scatter.8.cloned.1.call-done = bf16[1,3,256,1024]{3,2,1,0:T(8,128)(2,1)} async-done(((bf16[8,3,256,1024]{3,2,1,0:T(8,128)(2,1)}), bf16[1,3,256,1024]{3,2,1,0:T(8,128)(2,1)}) %reduce-scatter.8.cloned.1.call-update) | async-done | bytes 1572880 | tf_op jit(solution)/shard_map/reduce_scatter | solution.py:1020
  564.3 12.9 %shard_map.375 = (f32[1024,256]{1,0:T(8,128)}, bf16[8192,256]{1,0:T(8,128)(2,1)}) custom-call(s32[3,2]{1,0:T(4,128)} %pad_add_fusion.bound_ref, bf16[1024,256]{1,0:T(8,128)(2,1)} %get-tuple-element.113.query_ref, bf16[1024,256]{1,0:T(8,128)(2,1)} %get-tuple-element.134.grad_ref, bf16[1024,256]{1,0:T(8,128)(2,1)} %get-tuple-element.114.out_ref, ...), custom_call_target="tpu_custom_call" | custom-call | flops 21474836480 | bytes 8388608 | tf_op jit(solution)/shard_map/pallas_call | solution.py:173
  577.2 46.0 %reduce-scatter.10.cloned.1.call-done.refs_2_ = bf16[1024,256]{1,0:T(8,128)(2,1)} async-done(((bf16[8192,256]{1,0:T(8,128)(2,1)}), bf16[1024,256]{1,0:T(8,128)(2,1)}) %reduce-scatter.10.cloned.1.call-update) | async-done | bytes 524304 | tf_op jit(solution)/shard_map/reduce_scatter | solution.py:1053
  626.0 12.3 %shard_map.376.part_ref = bf16[4,1024,512]{2,1,0:T(8,128)(2,1)} custom-call(bf16[1024,512]{1,0:T(8,128)(2,1)} %get-tuple-element.137.refs_0_, bf16[8,3,256,512]{3,2,1,0:T(8,128)(2,1)} %bitcast.68, bf16[1024,1024]{1,0:T(8,128)(2,1)} %get-tuple-element.138.refs_2_, bf16[8,3,256,1024]{3,2,1,0:T(8,128)(2,1)} %bitcast.65), custom_call_target="tpu_custom_call" | custom-call | flops 4294967296 | bytes 4194304 | tf_op jit(solution)/shard_map/pallas_call | solution.py:282
  638.3 2.5 copy-done.1
  640.9 35.1 %shard_map.377 = bf16[1024,512]{1,0:T(8,128)(2,1)S(1)} custom-call(bf16[4,1024,512]{2,1,0:T(8,128)(2,1)S(1)} %copy-done.1), custom_call_target="tpu_custom_call" | custom-call | bytes 134217728 | tf_op jit(solution)/shard_map/pallas_call | solution.py:423
  680.3 8.9 %shard_map.378 = (f32[2,256,1536]{2,1,0:T(8,128)}, f32[2,256,1536]{2,1,0:T(8,128)}, f32[2,256,1536]{2,1,0:T(8,128)}, bf16[2,256,1536]{2,1,0:T(8,128)(2,1)}, f32[...) custom-call(bf16[3,256,512]{2,1,0:T(8,128)(2,1)S(1)} %bitcast.59, ...), custom_call_target="tpu_custom_call" | custom-call | bytes 30670848 | tf_op jit(solution)/shard_map/pallas_call | solution.py:807
  689.2 5.1 fusion
  694.3 2.0 pad_maximum_fusion.6
  696.3 7.4 shard_map.379
  703.7 13.0 %shard_map.380 = bf16[2048,1536]{1,0:T(8,128)(2,1)} custom-call(bf16[1024,2048]{1,0:T(8,128)(2,1)} %get-tuple-element.106.normed_ref, bf16[1024,1024]{1,0:T(8,128)(2,1)} %get-tuple-element.162.grad_ref, bf16[1024,2048]{1,0:T(8,128)(2,1)} %get-tuple-element.130.left_ref, bf16[1024,512]{1,0:T(8,128)(2,1)} %constant_dynamic-update-slice_fusion.left_ref.mixed_ref), custom_call_target="tpu_custom_call" | custom-call | flops 6442450944 | bytes 6291456 | tf_op jit(solution)/shard_map/pallas_call | solution.py:872
  718.5 13.2 %shard_map.381 = (bf16[4,1024,512]{2,1,0:T(8,128)(2,1)}, f32[1024,1]{1,0:T(8,128)}, f32[1,2048]{1,0:T(1,128)}) custom-call(bf16[1024,1024]{1,0:T(8,128)(2,1)} %get-tuple-element.162.grad_ref, bf16[2048,1536]{1,0:T(8,128)(2,1)} %all-gather.7.cloned.1.call-done.refs_0_.refs_1_.weight_ref, f32[1024,2048]{1,0:T(8,128)} %hidden_ref.3, f32[1024,1]{1,0:T(8,128)} %copy.58.scale_ref, ...), custom_call_target="tpu_custom_call" | custom-call | flops 8589934592 | bytes 4194304 | tf_op jit(solution)/shard_map/pallas_call | solution.py:658
  735.1 2.3 copy-done.6
  737.3 42.3 %shard_map.382 = (bf16[1024,512]{1,0:T(8,128)(2,1)S(1)}, f32[8,128]{1,0:T(8,128)S(1)}, f32[40,128]{1,0:T(8,128)S(1)}) custom-call(bf16[4,1024,512]{2,1,0:T(8,128)(2,1)S(1)} %copy-done.6, f32[8,128]{1,0:T(8,128)S(1)} %bitcast.62, f32[40,128]{1,0:T(8,128)S(1)} %pad_bitcast_fusion.gains_ref), custom_call_target="tpu_custom_call" | custom-call | bytes 134217728 | tf_op jit(solution)/shard_map/pallas_call | solution.py:510
  782.0 4.2 multiply_add_fusion
  786.2 3.0 reduce-scatter.14.cloned.1.call-done
  790.9 2.9 shard_map.383
  793.8 3.4 fusion.15
  (116 shorter events, 30.1 us)
Async XLA Ops:
  7.2 71.1 %all-gather.7.cloned.1.call-start = ((), (), s32[]{:S(2)}) async-start(), calls=%async_computation.5 | async-start | bytes 7077888 | tf_op jit(solution)/shard_map/all_gather | solution.py:950
  8.4 2.3 copy-start.27
  8.4 2.5 copy-start.18
  10.7 155.4 %all-gather.9.cloned.1.call-start = ((), (), s32[]{:S(2)}) async-start(), calls=%async_computation.6 | async-start | bytes 9437184 | tf_op jit(solution)/shard_map/all_gather | solution.py:983
  11.8 155.0 %copy-start.26 = (s32[1024]{0:T(1024)}, s32[1024]{0:T(1024)S(1)}, u32[]{:S(2)}) copy-start(s32[1024]{0:T(1024)S(1)} %select_reduce_fusion) | copy-start | bytes 12292
  19.0 10.5 %copy-start.20 = (f32[1024]{0:T(1024)}, f32[1024]{0:T(1024)S(1)}, u32[]{:S(2)}) copy-start(f32[1024]{0:T(1024)S(1)} %add_rsqrt_fusion) | copy-start | bytes 12292
  19.6 9.9 %copy-start.22 = (f32[2048]{0:T(1024)}, f32[2048]{0:T(1024)S(1)}, u32[]{:S(2)}) copy-start(f32[2048]{0:T(1024)S(1)} %get-tuple-element.202) | copy-start | bytes 24580
  85.2 2.8 copy-start.4
  85.2 146.4 %all-gather.11.cloned.1.call-start = ((), (), s32[]{:S(2)}) async-start(), calls=%async_computation.12 | async-start | bytes 7077888 | tf_op jit(solution)/shard_map/all_gather | solution.py:995
  88.2 1.1 copy-start.13
  166.1 198.0 %all-gather.13.cloned.1.call-start = ((), (), s32[]{:S(2)}) async-start(), calls=%async_computation.13 | async-start | bytes 14155776 | tf_op jit(solution)/shard_map/all_gather | solution.py:995
  166.8 1.1 copy-start.15
  166.8 1.5 slice-start
  231.7 265.9 %reduce-scatter.6.cloned.1.call-start = ((), (), s32[]{:S(2)}) async-start(), calls=%async_computation.7 | async-start | bytes 7077888 | tf_op jit(solution)/shard_map/reduce_scatter | solution.py:1020
  231.9 2.2 copy-start.2
  305.7 2.0 copy-start
  342.3 221.8 %reduce-scatter.8.cloned.1.call-start = ((), (), s32[]{:S(2)}) async-start(), calls=%async_computation.8 | async-start | bytes 14155776 | tf_op jit(solution)/shard_map/reduce_scatter | solution.py:1020
  402.3 220.9 %reduce-scatter.10.cloned.1.call-start = ((), (), s32[]{:S(2)}) async-start(), calls=%async_computation.9 | async-start | bytes 4718592 | tf_op jit(solution)/shard_map/reduce_scatter | solution.py:1053
  422.0 2.2 copy-start.7
  495.6 2.0 copy-start.3
  564.1 132.2 %reduce-scatter.12.cloned.1.call-start = ((), (), s32[]{:S(2)}) async-start(), calls=%async_computation.10 | async-start | bytes 4718592 | tf_op jit(solution)/shard_map/reduce_scatter | solution.py:1053
  623.2 0.7 copy-start.25
  623.2 166.0 %reduce-scatter.14.cloned.1.call-start = ((), (), s32[]{:S(2)}) async-start(), calls=%async_computation.11 | async-start | bytes 7077888 | tf_op jit(solution)/shard_map/reduce_scatter | solution.py:1081
  626.0 50.0 %copy-start.12 = (bf16[1,3,256,512]{3,2,1,0:T(8,128)(2,1)S(1)}, bf16[1,3,256,512]{3,2,1,0:T(8,128)(2,1)}, u32[]{:S(2)}) copy-start(bf16[1,3,256,512]{3,2,1,0:T(8,128)(2,1)} %reduce-scatter.6.cloned.1.call-done) | copy-start | bytes 2359300
  638.3 2.6 copy-start.1
  640.9 35.1 %copy-start.5 = (f32[1536,256]{1,0:T(8,128)S(1)}, f32[1536,256]{1,0:T(8,128)}, u32[]{:S(2)}) copy-start(f32[1536,256]{1,0:T(8,128)} %refs_5_.1) | copy-start | bytes 4718596
  640.9 35.1 %copy-start.8 = (f32[2,256,1536]{2,1,0:T(8,128)S(1)}, f32[2,256,1536]{2,1,0:T(8,128)}, u32[]{:S(2)}) copy-start(f32[2,256,1536]{2,1,0:T(8,128)} %refs_3_.1) | copy-start | bytes 9437188
  676.0 1.4 copy-start.9
  677.5 1.4 copy-start.10
  678.9 1.4 copy-start.11
  716.7 0.8 copy-start.21
  735.1 2.3 copy-start.6
  737.3 44.0 %copy-start.19 = (f32[4352]{0:T(1024)S(1)}, f32[4352]{0:T(1024)}, u32[]{:S(2)}) copy-start(f32[4352]{0:T(1024)} %param.27) | copy-start | bytes 52228
  737.3 44.0 %copy-start.23 = (f32[4352]{0:T(1024)S(1)}, f32[4352]{0:T(1024)}, u32[]{:S(2)}) copy-start(f32[4352]{0:T(1024)} %param.37) | copy-start | bytes 52228
  737.3 44.0 %copy-start.24 = (f32[4352]{0:T(1024)S(1)}, f32[4352]{0:T(1024)}, u32[]{:S(2)}) copy-start(f32[4352]{0:T(1024)} %param.32) | copy-start | bytes 52228
  782.0 11.8 %copy-start.17 = (f32[256,1024]{1,0:T(8,128)S(1)}, f32[256,1024]{1,0:T(8,128)}, u32[]{:S(2)}) copy-start(f32[256,1024]{1,0:T(8,128)} %param.28) | copy-start | bytes 3145732
  786.2 7.6 copy-start.14
  786.2 7.6 copy-start.16
Sparse Core Ops, SparseCore 0:
  10.8 67.4 all-gather.6
  85.4 80.6 all-gather.8
  168.3 63.2 all-gather.10
  233.7 130.3 all-gather.12
  366.3 68.0 reduce-scatter.5
  436.5 127.5 reduce-scatter.7
  566.4 56.7 reduce-scatter.9
  625.5 57.7 reduce-scatter.11
  716.8 72.3 reduce-scatter.13
